TPU v7x, 32 devices: a whole 2x2x4 slice. The times are simulated.
32 devices in a mesh: hid: 8 (over z, y), wid: 4 (over x, core).
Axes of the slice: x: 2, y: 2, z: 4, core: 2. Of those that a mesh axis runs over, the one named last changes fastest.
Arguments:
- inputs: bfloat16 [512, 6144], P('hid', 'wid'), may hold values from -420 to 420
- cotangent: bfloat16 [512, 6144], P('hid', 'wid'), may hold values from -6 to 6
- norm_gain: float32 [6144], P('wid'), may hold values from 0.5 to 1.5
- qkv_weight: bfloat16 [6144, 3, 4096], P('wid', None, 'hid'), may hold values from -0.078125 to 0.078125
- out_weight: bfloat16 [4096, 6144], P('hid', 'wid'), may hold values from -0.375 to 0.375
- up_weight: bfloat16 [6144, 16384], P('wid', 'hid'), may hold values from -0.078125 to 0.078125
- down_weight: bfloat16 [16384, 6144], P('hid', 'wid'), may hold values from -0.046875 to 0.046875
- query_gain: float32 [128], replicated, may hold values from 0.5 to 1.5
- key_gain: float32 [128], replicated, may hold values from 0.5 to 1.5
Outputs:
- input_grad: bfloat16 [512, 6144], P('hid', 'wid')
- qkv_grad: bfloat16 [6144, 3, 4096], P('wid', None, 'hid')
- out_grad: bfloat16 [4096, 6144], P('hid', 'wid')
- up_grad: bfloat16 [6144, 16384], P('wid', 'hid')
- down_grad: bfloat16 [16384, 6144], P('hid', 'wid')
All inputs are finite; a program needn't handle non-finite values.
Results may differ from a plain program's by a relative error of at most 0.011.
Values may be sent and summed in bfloat16 or wider, within the bound.
A program may use at most 128 MiB of HBM per device.

v0:
```python
import math

import jax
import jax.numpy as jnp
from jax import lax
from jax.sharding import PartitionSpec as P

HEAD_DIM = 128
PATCHES = 256


EPSILON = 1e-06


def combined_all(value, axis, join):
    pieces = jax.tree.map(lambda part: lax.all_gather(part, axis), value)
    head = jax.tree.map(lambda part: part[0], pieces)
    tail = jax.tree.map(lambda part: part[1:], pieces)
    subtotal, _ = lax.scan(lambda subtotal, share: (join(subtotal, share), None), head, tail)
    return subtotal


def product(form, left_arr, right_arr):
    return jnp.einsum(form, left_arr, right_arr, preferred_element_type=jnp.float32)


def head_norm(values, gain):
    centre = jnp.mean(values, axis=-1, keepdims=True)
    centred = values - centre
    inverse = lax.rsqrt(jnp.mean(centred * centred, axis=-1, keepdims=True) + EPSILON)
    unit_rows = centred * inverse
    return (unit_rows, inverse, unit_rows * gain)


def head_norm_back(upstream, unit_rows, inverse, gain):
    scaled = upstream * gain
    return inverse * (
        scaled
        - jnp.mean(scaled, axis=-1, keepdims=True)
        - unit_rows * jnp.mean(scaled * unit_rows, axis=-1, keepdims=True)
    )


def gelu_pair(pre_act, upstream):
    hidden, pullback = jax.vjp(jax.nn.gelu, pre_act)
    return (hidden.astype(jnp.bfloat16), pullback(upstream)[0].astype(jnp.bfloat16))


def merge_moments(first_part, second_part):
    first_count, first_mean, first_square = first_part
    second_count, second_mean, second_square = second_part
    joint_count = first_count + second_count
    offset = second_mean - first_mean
    return (
        joint_count,
        first_mean + offset * (second_count / joint_count),
        first_square + second_square + offset * offset * (first_count * second_count / joint_count),
    )


def attention_pair(qkv_rows, att_grad, query_gain, key_gain):
    tok_count = qkv_rows.shape[0]
    head_width = qkv_rows.shape[2]
    head_count = head_width // HEAD_DIM
    image_count = tok_count // PATCHES
    score_scale = 1.0 / math.sqrt(HEAD_DIM)

    def per_image(values):
        return values.reshape(image_count, PATCHES, head_count, HEAD_DIM)

    query_unit, query_inverse, query_normed = head_norm(per_image(qkv_rows[:, 0]), query_gain)
    key_unit, key_inverse, key_normed = head_norm(per_image(qkv_rows[:, 1]), key_gain)
    query_normed = query_normed.astype(jnp.bfloat16)
    key_normed = key_normed.astype(jnp.bfloat16)
    value_rows = per_image(qkv_rows[:, 2]).astype(jnp.bfloat16)
    scores = product("ipha,iqha->ihpq", query_normed, key_normed) * score_scale
    exponent = jnp.exp(scores)
    probs = exponent / jnp.sum(exponent, axis=-1, keepdims=True)
    probs_low = probs.astype(jnp.bfloat16)
    attended = (
        product("ihpq,iqha->ipha", probs_low, value_rows)
        .astype(jnp.bfloat16)
        .reshape(tok_count, head_width)
    )
    grad_rows = per_image(att_grad)
    probs_grad = product("ipha,iqha->ihpq", grad_rows, value_rows)
    value_grad = product("ihpq,ipha->iqha", probs_low, grad_rows)
    score_grad = (
        probs * (probs_grad - jnp.sum(probs * probs_grad, axis=-1, keepdims=True)) * score_scale
    ).astype(jnp.bfloat16)
    qn_grad = product("ihpq,iqha->ipha", score_grad, key_normed)
    kn_grad = product("ihpq,ipha->iqha", score_grad, query_normed)
    query_grad = head_norm_back(qn_grad, query_unit, query_inverse, query_gain)
    key_grad = head_norm_back(kn_grad, key_unit, key_inverse, key_gain)
    qkv_back = jnp.stack(
        [
            query_grad.reshape(tok_count, head_width),
            key_grad.reshape(tok_count, head_width),
            value_grad.reshape(tok_count, head_width),
        ],
        axis=1,
    ).astype(jnp.bfloat16)
    return (attended, qkv_back)


def local(
    inputs,
    cotangent,
    norm_gain,
    qkv_weight,
    out_weight,
    up_weight,
    down_weight,
    query_gain,
    key_gain,
):
    input_rows = inputs.astype(jnp.float32)
    row_centre = jnp.mean(input_rows, axis=-1)
    row_deviation = input_rows - row_centre[:, None]
    row_square = jnp.sum(row_deviation * row_deviation, axis=-1)
    width_count = jnp.full((1,), float(input_rows.shape[1]), jnp.float32)
    total_count, mean_all, square_all = combined_all(
        (width_count, row_centre, row_square), "wid", merge_moments
    )
    inverse = lax.rsqrt(square_all / total_count + EPSILON)[:, None]
    unit_rows = (input_rows - mean_all[:, None]) * inverse
    normed = (unit_rows * norm_gain).astype(jnp.bfloat16)
    normed_all, grad_all = (
        lax.all_gather(normed, "hid", axis=0, tiled=True),
        lax.all_gather(cotangent, "hid", axis=0, tiled=True),
    )
    pre_part = product("td,df->tf", normed_all, up_weight)
    qkv_part = product("td,dch->tch", normed_all, qkv_weight)
    hidden_part = product("td,fd->tf", grad_all, down_weight)
    att_part = product("td,hd->th", grad_all, out_weight)
    pre_act, qkv_rows, hidden_grad, att_sum = lax.psum(
        (pre_part, qkv_part, hidden_part, att_part), "wid"
    )
    hidden, pre_grad = gelu_pair(pre_act, hidden_grad)
    att_grad = att_sum.astype(jnp.bfloat16)
    attended, qkv_back = attention_pair(qkv_rows, att_grad, query_gain, key_gain)
    qkv_grad = product("td,tch->dch", normed_all, qkv_back).astype(jnp.bfloat16)
    out_grad = product("th,td->hd", attended, grad_all).astype(jnp.bfloat16)
    up_grad = product("td,tf->df", normed_all, pre_grad).astype(jnp.bfloat16)
    down_grad = product("tf,td->fd", hidden, grad_all).astype(jnp.bfloat16)
    normed_grad = lax.psum_scatter(
        product("tf,df->td", pre_grad, up_weight), "hid", scatter_dimension=0, tiled=True
    ) + lax.psum_scatter(
        product("tch,dch->td", qkv_back, qkv_weight), "hid", scatter_dimension=0, tiled=True
    )
    unit_grad = normed_grad * norm_gain
    grad_total, grad_project = lax.psum(
        (jnp.sum(unit_grad, axis=-1), jnp.sum(unit_grad * unit_rows, axis=-1)), "wid"
    )
    input_grad = (
        inverse
        * (
            unit_grad
            - (grad_total / total_count)[:, None]
            - unit_rows * (grad_project / total_count)[:, None]
        )
    ).astype(jnp.bfloat16)
    return (input_grad, qkv_grad, out_grad, up_grad, down_grad)


def solution(mesh):
    placed = (
        P("hid", "wid"),
        P("hid", "wid"),
        P("wid"),
        P("wid", None, "hid"),
        P("hid", "wid"),
        P("wid", "hid"),
        P("hid", "wid"),
        P(),
        P(),
    )
    return jax.shard_map(
        local,
        mesh=mesh,
        in_specs=placed,
        out_specs=(
            P("hid", "wid"),
            P("wid", None, "hid"),
            P("hid", "wid"),
            P("wid", "hid"),
            P("hid", "wid"),
        ),
        check_vma=False,
    )
```

profile of v0, /device:TPU:0, one launch (start us, length us, event | category | flops | bytes accessed | tf_op | source)
XLA Modules:
  0.0 506.3 jit_solution(10603074725824817677)
XLA Ops:
  13.2 43.9 %all-gather.5.cloned.1.call-done = bf16[512,1536]{1,0:T(8,128)(2,1)} async-done(((bf16[64,1536]{1,0:T(8,128)(2,1)}), bf16[512,1536]{1,0:T(8,128)(2,1)}) %all-gather.5.cloned.1.call-update) | async-done | bytes 1572880 | tf_op jit(solution)/shard_map/all_gather | solution.py:130
  57.1 2.4 fusion.89
  59.5 25.8 %all-reduce.10 = (f32[4]{0:T(128)}, f32[256]{0:T(256)S(1)}, f32[256]{0:T(256)S(1)}, bf16[512,512]{1,0:T(8,128)(2,1)S(1)}) all-reduce(f32[4]{0:T(128)S(1)} %dynamic-update-slice, f32[256]{0:T(256)S(1)} %get-tuple-element.81, f32[256]{0:T(256)S(1)} %dynamic-update-slice.2, f32[512,512]{1,0:T(8,128)S(1)} %fusion.89), channel_id=1, replica_groups=mesh['hid'=8,'wid'=4] {'wid'}, use_global_device_ids=true, to_apply=%add | all-reduce | flops 262660 | bytes 1576992
  86.4 13.3 %while.14 = (s32[]{:T(128)}, f32[1]{0:T(128)}, f32[64]{0:T(128)S(1)}, f32[64]{0:T(128)S(1)}, f32[3,1]{0,1:T(1,128)S(1)}, /*index=5*/f32[3,64]{1,0:T(4,128)S(1)}, f32[3,64]{1,0:T(4,128)S(1)}, s32[]{:T(128)}) while((s32[]{:T(128)}, f32[1]{0:T(128)}, f32[64]{0:T(128)S(1)}, f32[64]{0:T(128)S(1)}, f32[3,1]{0,1:T(1,128)S(1)}, ...), condition=%wide.region_3.4_spmd, body=%wide.region_2.3_spmd.sunk | while | flops 454 | bytes 1701 | solution.py:19
  101.2 8.7 %fusion.86 = f32[512,2048]{1,0:T(8,128)} fusion(bf16[512,1536]{1,0:T(8,128)(2,1)} %all-gather.5.cloned.1.call-done, bf16[2048,1536]{1,0:T(8,128)(2,1)} %param.17), kind=kOutput, calls=%fused_computation.110 | convolution fusion | flops 3221225472 | bytes 12058624 | tf_op jit(solution)/shard_map/td,fd->tf/dot_general | solution.py:24
  110.0 34.9 %all-gather.7.cloned.1.call-done = bf16[512,1536]{1,0:T(8,128)(2,1)} async-done(((bf16[64,1536]{1,0:T(8,128)(2,1)}), bf16[512,1536]{1,0:T(8,128)(2,1)}) %all-gather.7.cloned.1.call-update) | async-done | bytes 1572880 | tf_op jit(solution)/shard_map/all_gather | solution.py:129
  144.9 7.2 %fusion.30 = f32[512,3,512]{2,0,1:T(8,128)} fusion(bf16[1536,3,512]{2,0,1:T(8,128)(2,1)} %param.14, bf16[512,1536]{1,0:T(8,128)(2,1)} %all-gather.7.cloned.1.call-done), kind=kOutput, calls=%fused_computation.39 | convolution fusion | flops 2415919104 | bytes 9437184 | tf_op jit(solution)/shard_map/td,dch->tch/dot_general | solution.py:24
  152.1 7.9 %fusion.87 = f32[512,2048]{1,0:T(8,128)} fusion(bf16[512,1536]{1,0:T(8,128)(2,1)S(1)} %copy-done.13, bf16[1536,2048]{1,0:T(8,128)(2,1)} %param.16), kind=kOutput, calls=%fused_computation.111 | convolution fusion | flops 3221225472 | bytes 12058624 | tf_op jit(solution)/shard_map/td,df->tf/dot_general | solution.py:24
  161.5 202.0 %all-reduce.9.cloned.1.call-done = (f32[512,2048]{1,0:T(8,128)}, f32[512,2048]{1,0:T(8,128)}, f32[512,3,512]{2,0,1:T(8,128)}) async-done(((f32[512,2048]{1,0:T(8,128)}, f32[512,2048]{1,0:T(8,128)}, f32[512,3,512]{2,0,1:T(8,128)}), (f32[512,2048]{1,0:T(8,128)}, f32[512,2048]{1,0:T(8,128)}, f32[512,3,512]{2,0,1:T(8,128)})) %all-reduce.9.cloned.1.call-update) | async-done | bytes 11534352 | tf_op jit(solution)/shard_map/psum | solution.py:136
  363.4 1.3 slice.48
  364.7 2.7 fusion.81
  370.3 1.6 reshape_squeeze.8
  372.2 1.3 reduce_sum.130
  374.7 3.0 fusion.90
  377.8 2.0 fusion.22
  379.7 3.0 fusion.44
  382.7 5.8 %fusion.79 = (f32[2,256,4]{1,2,0:T(4,128)S(1)}, f32[2,256,4]{1,2,0:T(4,128)S(1)}, f32[2,256,4,128]{1,3,2,0:T(8,128)}) fusion(f32[2,256,4]{1,2,0:T(4,128)S(1)} %add_rsqrt_fusion, f32[2,256,4,128]{1,3,2,0:T(8,128)S(1)} %copy.95, f32[2,256,4]{1,2,0:T(4,128)S(1)} %broadcast_multiply_fusion.4, f32[128]{0:T(128)S(1)} %copy-done.11, ...), kind=kOutput, calls=%fused_computation.107 | convolution fusion | flops 141555968 | bytes 7398400 | tf_op jit(solution)/shard_map/ihpq,ipha->iqha/dot_general | solution.py:24
  388.5 5.8 %fusion.80 = (f32[2,256,4]{1,2,0:T(4,128)S(1)}, f32[2,256,4]{1,2,0:T(4,128)S(1)}, f32[2,256,4,128]{1,3,2,0:T(8,128)}) fusion(f32[2,256,4]{1,2,0:T(4,128)S(1)} %add_rsqrt_fusion.1, f32[2,256,4,128]{1,3,2,0:T(8,128)S(1)} %copy.93, f32[2,256,4]{1,2,0:T(4,128)S(1)} %broadcast_multiply_fusion.5, f32[128]{0:T(128)S(1)} %copy-done.10, ...), kind=kOutput, calls=%fused_computation.108 | convolution fusion | flops 141555968 | bytes 7398400 | tf_op jit(solution)/shard_map/ihpq,iqha->ipha/dot_general | solution.py:24
  394.8 1.5 multiply_convert_fusion.3
  396.8 1.5 multiply_convert_fusion.4
  398.9 5.4 %fusion.12 = bf16[512,2048]{1,0:T(8,128)(2,1)S(1)} fusion(f32[512,2048]{1,0:T(8,128)} %get-tuple-element.73, f32[512,2048]{1,0:T(8,128)} %get-tuple-element.74), kind=kLoop, calls=%fused_computation.21 | loop fusion | flops 20971520 | bytes 10485760 | tf_op jit(solution)/shard_map/convert_element_type | solution.py:46
  404.3 5.6 %fusion.88 = f32[512,1536]{1,0:T(8,128)S(1)} fusion(bf16[512,2048]{1,0:T(8,128)(2,1)S(1)} %fusion.12, bf16[1536,2048]{1,0:T(8,128)(2,1)} %param.16), kind=kOutput, calls=%fused_computation.112 | convolution fusion | flops 3221225472 | bytes 11534336 | tf_op jit(solution)/shard_map/tf,df->td/dot_general | solution.py:24
  411.2 4.3 fusion.13
  416.6 2.1 fusion.45
  419.0 3.7 convolution_convert_fusion.3
  422.7 4.3 convolution_convert_fusion.2
  427.0 5.3 %convolution_convert_fusion.1 = bf16[1536,2048]{1,0:T(8,128)(2,1)} fusion(bf16[512,1536]{1,0:T(8,128)(2,1)S(1)} %copy-done.14, bf16[512,2048]{1,0:T(8,128)(2,1)S(1)} %fusion.12), kind=kOutput, calls=%fused_computation.11 | convolution fusion | flops 3224371200 | bytes 9961472 | tf_op jit(solution)/shard_map/td,tf->df/dot_general | solution.py:24
  432.3 5.7 %convolution_convert_fusion = bf16[2048,1536]{1,0:T(8,128)(2,1)} fusion(bf16[512,1536]{1,0:T(8,128)(2,1)S(1)} %copy-done.12, f32[512,2048]{1,0:T(8,128)S(1)} %copy-done.3), kind=kOutput, calls=%fused_computation.10 | convolution fusion | flops 3233808384 | bytes 12058624 | tf_op jit(solution)/shard_map/tf,td->fd/dot_general | solution.py:24
  438.0 52.1 %reduce-scatter.2.cloned.1.call-done = f32[64,1536]{1,0:T(8,128)} async-done(((f32[512,1536]{1,0:T(8,128)}), f32[64,1536]{1,0:T(8,128)}) %reduce-scatter.2.cloned.1.call-update) | async-done | bytes 393232 | tf_op jit(solution)/shard_map/reduce_scatter | solution.py:146
  490.1 1.3 multiply_reduce_fusion.5
  491.4 5.9 %all-reduce.3 = (f32[64]{0:T(128)S(1)}, f32[64]{0:T(128)S(1)}) all-reduce(f32[64]{0:T(128)S(1)} %get-tuple-element.52, f32[64]{0:T(128)S(1)} %get-tuple-element.51), channel_id=1, replica_groups=mesh['hid'=8,'wid'=4] {'wid'}, use_global_device_ids=true, to_apply=%region_23.24 | all-reduce | flops 128 | bytes 1024 | tf_op jit(solution)/shard_map/psum | solution.py:152
  497.9 1.9 fusion.62
  (98 shorter events, 20.2 us)
Async XLA Ops:
  7.2 50.0 %copy-start = (bf16[512,1536]{1,0:T(8,128)(2,1)S(1)}, bf16[512,1536]{1,0:T(8,128)(2,1)}, u32[]{:S(2)}) copy-start(bf16[512,1536]{1,0:T(8,128)(2,1)} %param.15) | copy-start | bytes 4718596
  7.2 49.9 %all-gather.5.cloned.1.call-start = ((), (), s32[]{:S(2)}) async-start(), calls=%async_computation.1 | async-start | bytes 1769472 | tf_op jit(solution)/shard_map/all_gather | solution.py:130
  7.9 137.0 %all-gather.7.cloned.1.call-start = ((), (), s32[]{:S(2)}) async-start(), calls=%async_computation.2 | async-start | bytes 1769472 | tf_op jit(solution)/shard_map/all_gather | solution.py:129
  13.2 87.1 %copy-start.2 = (bf16[64,1536]{1,0:T(8,128)(2,1)S(1)}, bf16[64,1536]{1,0:T(8,128)(2,1)}, u32[]{:S(2)}) copy-start(bf16[64,1536]{1,0:T(8,128)(2,1)} %param.11) | copy-start | bytes 589828
  13.2 87.1 %copy-start.9 = (f32[1536]{0:T(1024)S(1)}, f32[1536]{0:T(1024)}, u32[]{:S(2)}) copy-start(f32[1536]{0:T(1024)} %param.13) | copy-start | bytes 18436
  101.2 262.3 %all-reduce.9.cloned.1.call-start = ((), (), s32[]{:S(2)}) async-start(), calls=%async_computation.4 | async-start | bytes 23068672 | tf_op jit(solution)/shard_map/psum | solution.py:136
  144.9 7.2 %copy-start.13 = (bf16[512,1536]{1,0:T(8,128)(2,1)S(1)}, bf16[512,1536]{1,0:T(8,128)(2,1)}, u32[]{:S(2)}) copy-start(bf16[512,1536]{1,0:T(8,128)(2,1)} %all-gather.7.cloned.1.call-done) | copy-start | bytes 4718596
  160.0 330.1 %reduce-scatter.2.cloned.1.call-start = ((), (), s32[]{:S(2)}) async-start(), calls=%async_computation.3 | async-start | bytes 3538944 | tf_op jit(solution)/shard_map/reduce_scatter | solution.py:146
  374.6 3.2 copy-start.10
  374.6 3.2 copy-start.11
  377.8 2.0 copy-start.5
  388.5 5.8 %copy-start.6 = (bf16[2,256,4,128]{1,3,2,0:T(8,128)(2,1)S(1)}, bf16[2,256,4,128]{1,3,2,0:T(8,128)(2,1)}, u32[]{:S(2)}) copy-start(bf16[2,256,4,128]{1,3,2,0:T(8,128)(2,1)} %fusion.44) | copy-start | bytes 1572868
  398.9 12.3 %slice-start = ((s8[4718592]{0:T(1024)(128)(4,1)}), s8[4194304]{0:T(1024)(128)(4,1)S(1)}, s32[]{:S(2)}) async-start(s8[4718592]{0:T(1024)(128)(4,1)} %bitcast.82), calls=%async_computation.5 | async-start | bytes 8388608
  404.3 6.9 %slice-start.1 = ((s8[4718592]{0:T(1024)(128)(4,1)}), s8[524288]{0:T(1024)(128)(4,1)S(1)}, s32[]{:S(2)}) async-start(s8[4718592]{0:T(1024)(128)(4,1)} %bitcast.82), calls=%async_computation.6 | async-start | bytes 1048576
  410.1 1.1 copy-start.7
  415.5 1.0 copy-start.4
  419.0 3.7 copy-start.8
  419.0 3.7 copy-start.14
  427.0 5.3 %copy-start.3 = (f32[512,2048]{1,0:T(8,128)S(1)}, f32[512,2048]{1,0:T(8,128)}, u32[]{:S(2)}) copy-start(f32[512,2048]{1,0:T(8,128)} %get-tuple-element.73) | copy-start | bytes 12582916
  427.0 5.3 %copy-start.12 = (bf16[512,1536]{1,0:T(8,128)(2,1)S(1)}, bf16[512,1536]{1,0:T(8,128)(2,1)}, u32[]{:S(2)}) copy-start(bf16[512,1536]{1,0:T(8,128)(2,1)} %all-gather.5.cloned.1.call-done) | copy-start | bytes 4718596
  432.3 67.4 %copy-start.1 = (bf16[512,1536]{1,0:T(8,128)(2,1)S(1)}, bf16[512,1536]{1,0:T(8,128)(2,1)}, u32[]{:S(2)}) copy-start(bf16[512,1536]{1,0:T(8,128)(2,1)} %param.15) | copy-start | bytes 4718596
Sparse Core Ops, SparseCore 0:
  10.2 46.8 all-gather.4
  101.3 43.5 all-gather.6
  160.1 203.2 all-reduce.8
  415.7 74.4 reduce-scatter.1
where the time goes:
time: 507 us; the launch traced here: 506 us
  waiting for transfers between devices  334 us (66%)
  matrix products  76.9 us (15%)
  blocking collectives  31.6 us (6%)
  local copies, waits for them, and re-layouts  19.3 us (4%)
  other arithmetic  18.2 us (4%)
  between operations  14.8 us (3%)
  loops' own time  11.5 us (2%)
    psum x1, waiting for transfers between devices, local(): lax.psum((pre_part, qkv_part, hidden_part, att_part), 'wid')  202 us
    dot_general x16, matrix products, product(): jnp.einsum(form, left_arr, right_arr, preferred_element_type=jnp.float32)  76.9 us
    reduce_scatter x1, waiting for transfers between devices, local(): lax.psum_scatter(product('tf,df->td', pre_grad, up_weight), 'hid', scatte...  52.1 us
    all_gather x1, waiting for transfers between devices, local(): lax.all_gather(cotangent, 'hid', axis=0, tiled=True)  43.9 us
    all_gather x1, waiting for transfers between devices, local(): lax.all_gather(normed, 'hid', axis=0, tiled=True)  34.9 us
    unnamed x1, blocking collectives  25.8 us
    another operation x1, loops' own time, combined_all(): lax.scan(lambda subtotal, share: (join(subtotal, share), None), head, tail)  11.5 us
  transfers between devices with their start and end apart: 4, of which 4 were waited for; matrix products, arithmetic and copies ran while one was open for 7% of the time, Pallas kernels for 0%

commit v1 on v0

--- a/solution.py
+++ b/solution.py
@@ -12,12 +12,14 @@
 EPSILON = 1e-06
 
 
-def combined_all(value, axis, join):
-    pieces = jax.tree.map(lambda part: lax.all_gather(part, axis), value)
-    head = jax.tree.map(lambda part: part[0], pieces)
-    tail = jax.tree.map(lambda part: part[1:], pieces)
-    subtotal, _ = lax.scan(lambda subtotal, share: (join(subtotal, share), None), head, tail)
-    return subtotal
+def swapped(value, axis, bit):
+    size = lax.axis_size(axis)
+    return lax.ppermute(value, axis, [(at, at ^ bit) for at in range(size)])
+
+
+def axis_bits(axis):
+    size = lax.axis_size(axis)
+    return [1 << at for at in range(size.bit_length() - 1)]
 
 
 def product(form, left_arr, right_arr):
@@ -44,18 +46,6 @@
 def gelu_pair(pre_act, upstream):
     hidden, pullback = jax.vjp(jax.nn.gelu, pre_act)
     return (hidden.astype(jnp.bfloat16), pullback(upstream)[0].astype(jnp.bfloat16))
-
-
-def merge_moments(first_part, second_part):
-    first_count, first_mean, first_square = first_part
-    second_count, second_mean, second_square = second_part
-    joint_count = first_count + second_count
-    offset = second_mean - first_mean
-    return (
-        joint_count,
-        first_mean + offset * (second_count / joint_count),
-        first_square + second_square + offset * offset * (first_count * second_count / joint_count),
-    )
 
 
 def attention_pair(qkv_rows, att_grad, query_gain, key_gain):
@@ -103,6 +93,52 @@
     return (attended, qkv_back)
 
 
+def row_moments(input_rows):
+    count = float(input_rows.shape[1])
+    mean = jnp.mean(input_rows, axis=-1)
+    deviation = input_rows - mean[:, None]
+    square = jnp.sum(deviation * deviation, axis=-1)
+    for bit in axis_bits("wid"):
+        other_mean, other_square = swapped(jnp.stack([mean, square]), "wid", bit)
+        offset = other_mean - mean
+        mean = 0.5 * (mean + other_mean)
+        square = square + other_square + offset * offset * (0.5 * count)
+        count = 2.0 * count
+    return (mean, lax.rsqrt(square / count + EPSILON), count)
+
+
+def row_totals(sums):
+    for bit in axis_bits("wid"):
+        sums = sums + swapped(sums, "wid", bit)
+    return sums
+
+
+def halves(values, core):
+    half = values.shape[0] // 2
+    own = lax.dynamic_slice_in_dim(values, core * half, half, axis=0)
+    other = lax.dynamic_slice_in_dim(values, (1 - core) * half, half, axis=0)
+    return (own, other)
+
+
+def summed_product(form, rows, weight):
+    own, other = rows
+    subtotal = product(form, own, weight) + swapped(
+        product(form, other, weight).astype(jnp.bfloat16), "wid", 1
+    ).astype(jnp.float32)
+    for bit in axis_bits("wid")[1:]:
+        subtotal = subtotal + swapped(
+            subtotal.astype(jnp.bfloat16), "wid", bit
+        ).astype(jnp.float32)
+    return subtotal
+
+
+def both_halves(own):
+    return jnp.concatenate([own, swapped(own, "wid", 1)], axis=0)
+
+
+CHUNKS = 4
+
+
 def local(
     inputs,
     cotangent,
@@ -114,43 +150,49 @@
     query_gain,
     key_gain,
 ):
+    core = lax.axis_index("wid") % 2
+    grad_all = lax.all_gather(cotangent, "hid", axis=0, tiled=True)
     input_rows = inputs.astype(jnp.float32)
-    row_centre = jnp.mean(input_rows, axis=-1)
-    row_deviation = input_rows - row_centre[:, None]
-    row_square = jnp.sum(row_deviation * row_deviation, axis=-1)
-    width_count = jnp.full((1,), float(input_rows.shape[1]), jnp.float32)
-    total_count, mean_all, square_all = combined_all(
-        (width_count, row_centre, row_square), "wid", merge_moments
-    )
-    inverse = lax.rsqrt(square_all / total_count + EPSILON)[:, None]
-    unit_rows = (input_rows - mean_all[:, None]) * inverse
+    centre, inverse, total_count = row_moments(input_rows)
+    inverse = inverse[:, None]
+    unit_rows = (input_rows - centre[:, None]) * inverse
     normed = (unit_rows * norm_gain).astype(jnp.bfloat16)
-    normed_all, grad_all = (
-        lax.all_gather(normed, "hid", axis=0, tiled=True),
-        lax.all_gather(cotangent, "hid", axis=0, tiled=True),
-    )
-    pre_part = product("td,df->tf", normed_all, up_weight)
-    qkv_part = product("td,dch->tch", normed_all, qkv_weight)
-    hidden_part = product("td,fd->tf", grad_all, down_weight)
-    att_part = product("td,hd->th", grad_all, out_weight)
-    pre_act, qkv_rows, hidden_grad, att_sum = lax.psum(
-        (pre_part, qkv_part, hidden_part, att_part), "wid"
-    )
-    hidden, pre_grad = gelu_pair(pre_act, hidden_grad)
-    att_grad = att_sum.astype(jnp.bfloat16)
+    normed_all = lax.all_gather(normed, "hid", axis=0, tiled=True)
+    grad_halves = halves(grad_all, core)
+    normed_halves = halves(normed_all, core)
+    grad_order = jnp.concatenate(grad_halves, axis=0)
+    normed_order = jnp.concatenate(normed_halves, axis=0)
+
+    att_grad = summed_product("td,hd->th", grad_halves, out_weight).astype(jnp.bfloat16)
+    width = up_weight.shape[1] // CHUNKS
+    spans = [slice(at * width, (at + 1) * width) for at in range(CHUNKS)]
+    hidden_grads = [
+        summed_product("td,fd->tf", grad_halves, down_weight[span]) for span in spans
+    ]
+    qkv_rows = summed_product("td,dch->tch", normed_halves, qkv_weight)
     attended, qkv_back = attention_pair(qkv_rows, att_grad, query_gain, key_gain)
-    qkv_grad = product("td,tch->dch", normed_all, qkv_back).astype(jnp.bfloat16)
-    out_grad = product("th,td->hd", attended, grad_all).astype(jnp.bfloat16)
-    up_grad = product("td,tf->df", normed_all, pre_grad).astype(jnp.bfloat16)
-    down_grad = product("tf,td->fd", hidden, grad_all).astype(jnp.bfloat16)
-    normed_grad = lax.psum_scatter(
-        product("tf,df->td", pre_grad, up_weight), "hid", scatter_dimension=0, tiled=True
-    ) + lax.psum_scatter(
-        product("tch,dch->td", qkv_back, qkv_weight), "hid", scatter_dimension=0, tiled=True
-    )
-    unit_grad = normed_grad * norm_gain
-    grad_total, grad_project = lax.psum(
-        (jnp.sum(unit_grad, axis=-1), jnp.sum(unit_grad * unit_rows, axis=-1)), "wid"
+    attended = both_halves(attended)
+    qkv_back = both_halves(qkv_back)
+    normed_grad = product("tch,dch->td", qkv_back, qkv_weight)
+    hidden, pre_grad = [], []
+    for span, hidden_grad in zip(spans, hidden_grads):
+        pre_act = summed_product("td,df->tf", normed_halves, up_weight[:, span])
+        hidden_own, pre_own = gelu_pair(pre_act, hidden_grad)
+        pre_both = both_halves(pre_own)
+        pre_grad.append(pre_both)
+        hidden.append(both_halves(hidden_own))
+        normed_grad = normed_grad + product("tf,df->td", pre_both, up_weight[:, span])
+    hidden = jnp.concatenate(hidden, axis=1)
+    pre_grad = jnp.concatenate(pre_grad, axis=1)
+    normed_grad = jnp.concatenate(halves(normed_grad, core), axis=0).astype(jnp.bfloat16)
+    normed_grad = lax.psum_scatter(normed_grad, "hid", scatter_dimension=0, tiled=True)
+    qkv_grad = product("td,tch->dch", normed_order, qkv_back).astype(jnp.bfloat16)
+    out_grad = product("th,td->hd", attended, grad_order).astype(jnp.bfloat16)
+    up_grad = product("td,tf->df", normed_order, pre_grad).astype(jnp.bfloat16)
+    down_grad = product("tf,td->fd", hidden, grad_order).astype(jnp.bfloat16)
+    unit_grad = normed_grad.astype(jnp.float32) * norm_gain
+    grad_total, grad_project = row_totals(
+        jnp.stack([jnp.sum(unit_grad, axis=-1), jnp.sum(unit_grad * unit_rows, axis=-1)])
     )
     input_grad = (
         inverse

time: 507 us -> 325 us (0.64)
  waiting for transfers between devices: 334 us -> 155 us
  blocking collectives: 31.6 us -> 0 us
  starting transfers between devices: 0.34 us -> 20.3 us
  matrix products: 76.9 us -> 94.8 us
  loops' own time: 11.5 us -> 0 us
  other arithmetic: 18.2 us -> 25.7 us
  local copies, waits for them, and re-layouts: 19.3 us -> 14 us
    psum x1 -> x0, waiting for transfers between devices: 202 us -> none  [local(): lax.psum((pre_part, qkv_part, hidden_part, att_part), 'wid')]
    ppermute x0 -> x34, waiting for transfers between devices: none -> 38.3 us  [swapped(): return lax.ppermute(value, axis, [(at, at ^ bit) for at in range(size)])]
    unnamed x1 -> x0, blocking collectives: 25.8 us -> none
    ppermute x0 -> x34, starting transfers between devices: none -> 20.2 us  [swapped(): return lax.ppermute(value, axis, [(at, at ^ bit) for at in range(size)])]
    dot_general x16 -> x35, matrix products: 76.9 us -> 92.4 us  [product(): jnp.einsum(form, left_arr, right_arr, preferred_element_type=jnp.float32)]
    another operation x1 -> x0, loops' own time: 11.5 us -> none  [combined_all(): lax.scan(lambda subtotal, share: (join(subtotal, share), None), head, tail)]
    reduce_scatter x1, waiting for transfers between devices: 52.1 us -> 43.4 us  [local(): lax.psum_scatter(normed_grad, 'hid', scatter_dimension=0, tiled=True)]
    convert_element_type x1 -> x7, other arithmetic: 5.41 us -> 13.6 us  [the longest x4 8.85 us: gelu_pair(): hidden.astype(jnp.bfloat16)]
  transfers between devices with their start and end apart: 4 -> 37, of which waited for: 4 -> 9; matrix products, arithmetic and copies ran while one was open for 7% -> 39% of each run, Pallas kernels for 0% -> 0%
where the time goes in v1:
time: 325 us; the launch traced here: 324 us
  waiting for transfers between devices  155 us (48%)
  matrix products  94.8 us (29%)
  other arithmetic  25.7 us (8%)
  starting transfers between devices  20.3 us (6%)
  between operations  14.7 us (5%)
  local copies, waits for them, and re-layouts  14 us (4%)
    dot_general x35, matrix products, product(): jnp.einsum(form, left_arr, right_arr, preferred_element_type=jnp.float32)  92.4 us
    reduce_scatter x1, waiting for transfers between devices, local(): lax.psum_scatter(normed_grad, 'hid', scatter_dimension=0, tiled=True)  43.4 us
    all_gather x1, waiting for transfers between devices, local(): grad_all = lax.all_gather(cotangent, 'hid', axis=0, tiled=True)  38.7 us
    ppermute x34, waiting for transfers between devices, swapped(): return lax.ppermute(value, axis, [(at, at ^ bit) for at in range(size)])  38.3 us
    all_gather x1, waiting for transfers between devices, local(): normed_all = lax.all_gather(normed, 'hid', axis=0, tiled=True)  33.8 us
    ppermute x34, starting transfers between devices, swapped(): return lax.ppermute(value, axis, [(at, at ^ bit) for at in range(size)])  20.2 us
    convert_element_type x4, other arithmetic, gelu_pair(): hidden.astype(jnp.bfloat16)  8.85 us
  transfers between devices with their start and end apart: 37, of which 9 were waited for; matrix products, arithmetic and copies ran while one was open for 39% of the time, Pallas kernels for 0%

profile of v1, /device:TPU:0, one launch (start us, length us, event | category | flops | bytes accessed | tf_op | source)
XLA Modules:
  0.0 324.4 jit_solution(7699672710453503108)
XLA Ops:
  11.6 2.9 collective-permute-start.1
  18.4 38.7 %all-gather.5.cloned.1.call-done = bf16[512,1536]{1,0:T(8,128)(2,1)} async-done(((bf16[64,1536]{1,0:T(8,128)(2,1)}), bf16[512,1536]{1,0:T(8,128)(2,1)}) %all-gather.5.cloned.1.call-update) | async-done | bytes 1572880 | tf_op jit(solution)/shard_map/all_gather | solution.py:154
  58.8 3.6 %fusion.70 = bf16[256,512]{1,0:T(8,128)(2,1)} fusion(bf16[256,1536]{1,0:T(8,128)(2,1)S(1)} %get-tuple-element.17, bf16[2048,1536]{1,0:T(8,128)(2,1)} %param.15), kind=kOutput, calls=%fused_computation.81 | convolution fusion | flops 402784256 | bytes 2621440 | tf_op jit(solution)/shard_map/td,fd->tf/dot_general | solution.py:26
  68.7 33.8 %all-gather.3.cloned.1.call-done = bf16[512,1536]{1,0:T(8,128)(2,1)} async-done(((bf16[64,1536]{1,0:T(8,128)(2,1)}), bf16[512,1536]{1,0:T(8,128)(2,1)}) %all-gather.3.cloned.1.call-update) | async-done | bytes 1572880 | tf_op jit(solution)/shard_map/all_gather | solution.py:160
  103.9 2.5 convolution_convert_fusion.6
  110.8 4.8 %convolution_convert_fusion.4 = bf16[256,3,512]{2,0,1:T(8,128)(2,1)} fusion(bf16[1536,3,512]{2,0,1:T(8,128)(2,1)} %param.12, bf16[256,1536]{1,0:T(8,128)(2,1)S(1)} %get-tuple-element.15), kind=kOutput, calls=%fused_computation.49 | convolution fusion | flops 1208352768 | bytes 6291456 | tf_op jit(solution)/shard_map/td,dch->tch/dot_general | solution.py:26
  116.3 2.4 fusion.167
  135.1 10.4 %collective-permute-done.5 = bf16[256,512]{1,0:T(8,128)(2,1)S(1)} collective-permute-done((bf16[256,512]{1,0:T(8,128)(2,1)S(1)}, bf16[256,512]{1,0:T(8,128)(2,1)S(1)}, u32[]{:S(2)}, u32[]{:S(2)}) %collective-permute-start.5) | collective-permute-done | bytes 262176 | tf_op jit(solution)/shard_map/ppermute | solution.py:17
  148.5 2.7 collective-permute-done.25
  152.7 2.5 multiply_convert_fusion
  155.8 12.2 %collective-permute-done.20 = bf16[256,512]{1,0:T(8,128)(2,1)S(1)} collective-permute-done((bf16[256,512]{1,0:T(8,128)(2,1)}, bf16[256,512]{1,0:T(8,128)(2,1)S(1)}, u32[]{:S(2)}, u32[]{:S(2)}) %collective-permute-start.20) | collective-permute-done | bytes 262176 | tf_op jit(solution)/shard_map/ppermute | solution.py:17
  169.5 2.5 multiply_convert_fusion.1
  172.1 4.1 %fusion.93 = (bf16[256,3,512]{2,0,1:T(8,128)(2,1)S(1)}, f32[256,3,512]{2,0,1:T(8,128)S(1)}) fusion(bf16[256,3,512]{2,0,1:T(8,128)(2,1)} %collective-permute-done.2, bf16[1536,3,512]{2,0,1:T(8,128)(2,1)} %param.12, bf16[256,1536]{1,0:T(8,128)(2,1)S(1)} %copy-done.16), kind=kOutput, calls=%fused_computation.109 | convolution fusion | flops 1209139200 | bytes 8650752 | tf_op jit(solution)/shard_map/td,dch->tch/dot_general | solution.py:26
  177.2 2.4 multiply_convert_fusion.2
  181.6 4.2 %fusion.73 = f32[512,1536]{1,0:T(8,128)} fusion(bf16[1536,2048]{1,0:T(8,128)(2,1)} %param.14, bf16[256,512]{1,0:T(8,128)(2,1)S(1)} %collective-permute-done.26, bf16[256,512]{1,0:T(8,128)(2,1)S(1)} %get-tuple-element.26), kind=kOutput, calls=%fused_computation.89 | convolution fusion | flops 806354944 | bytes 5242880 | tf_op jit(solution)/shard_map/tf,df->td/dot_general | solution.py:26
  185.7 10.5 %collective-permute-done.3 = bf16[256,3,512]{2,0,1:T(8,128)(2,1)S(1)} collective-permute-done((bf16[256,3,512]{2,0,1:T(8,128)(2,1)S(1)}, bf16[256,3,512]{2,0,1:T(8,128)(2,1)S(1)}, u32[]{:S(2)}, u32[]{:S(2)}) %collective-permute-start.3) | collective-permute-done | bytes 786464 | tf_op jit(solution)/shard_map/ppermute | solution.py:17
  203.0 2.4 multiply_convert_fusion.6
  208.7 2.2 multiply_convert_fusion.7
  212.1 2.4 fusion.55
  214.4 2.4 fusion.145
  217.4 3.1 fusion.198
  220.5 3.0 fusion.197
  227.5 2.6 fusion.78
  230.1 2.6 fusion.83
  232.7 2.7 fusion.88
  236.3 5.3 %fusion.4 = bf16[512,1536]{1,0:T(8,128)(2,1)S(1)} fusion(f32[512,1536]{1,0:T(8,128)S(1)} %copy-done.4, f32[512,1536]{1,0:T(8,128)S(1)} %fusion.78, f32[512,1536]{1,0:T(8,128)S(1)} %fusion.83, f32[512,1536]{1,0:T(8,128)S(1)} %fusion.88, bf16[1536,3,512]{2,0,1:T(8,128)(2,1)} %param.12, bf16[256,3,512]{2,0,1:T(8,128)(2,1)S(1)} %collective-permute-done.6, ...), kind=kOutput, calls=%fused_computation.8 | convolution fusion | flops 2426142720 | bytes 20447232 | tf_op jit(solution)/shard_map/tch,dch->td/dot_general | solution.py:26
  244.2 8.1 %convolution_convert_fusion.1 = bf16[1536,2048]{1,0:T(8,128)(2,1)} fusion(bf16[256,512]{1,0:T(8,128)(2,1)} %copy-done.28, bf16[256,512]{1,0:T(8,128)(2,1)S(1)} %get-tuple-element.26, bf16[256,512]{1,0:T(8,128)(2,1)} %collective-permute-done.21, bf16[256,512]{1,0:T(8,128)(2,1)} %get-tuple-element.24, bf16[256,512]{1,0:T(8,128)(2,1)} %collective-permute-done.16, ...), kind=kOutput, calls=%fused_computation.2 | convolution fusion | flops 3244294144 | bytes 9961472 | tf_op jit(solution)/shard_map/td,tf->df/dot_general | solution.py:26
  252.3 2.7 convolution_convert_fusion.5
  255.6 7.5 %convolution_convert_fusion = bf16[2048,1536]{1,0:T(8,128)(2,1)} fusion(bf16[256,512]{1,0:T(8,128)(2,1)} %collective-permute-done.33, bf16[256,512]{1,0:T(8,128)(2,1)S(1)} %copy-done.24, bf16[256,512]{1,0:T(8,128)(2,1)} %collective-permute-done.32, bf16[256,512]{1,0:T(8,128)(2,1)S(1)} %copy-done.25, bf16[256,512]{1,0:T(8,128)(2,1)} %collective-permute-done.31, ...), kind=kOutput, calls=%fused_computation.1 | convolution fusion | flops 3244294144 | bytes 9961472 | tf_op jit(solution)/shard_map/tf,td->fd/dot_general | solution.py:26
  263.1 43.4 %reduce-scatter.2.cloned.1.call-done = bf16[64,1536]{1,0:T(8,128)(2,1)} async-done(((bf16[512,1536]{1,0:T(8,128)(2,1)}), bf16[64,1536]{1,0:T(8,128)(2,1)}) %reduce-scatter.2.cloned.1.call-update) | async-done | bytes 196624 | tf_op jit(solution)/shard_map/reduce_scatter | solution.py:188
  307.8 3.2 convolution_convert_fusion.3
  312.6 4.3 %convolution_convert_fusion.2 = bf16[1536,3,512]{2,0,1:T(8,128)(2,1)} fusion(bf16[256,1536]{1,0:T(8,128)(2,1)S(1)} %copy-done.14, bf16[256,1536]{1,0:T(8,128)(2,1)S(1)} %copy-done.17, bf16[256,3,512]{2,0,1:T(8,128)(2,1)S(1)} %copy-done.50, bf16[256,1,512]{2,0,1:T(8,128)(2,1)S(1)} %copy.108, bf16[256,1,512]{2,0,1:T(8,128)(2,1)S(1)} %copy.107, ...), kind=kOutput, calls=%fused_computation.3 | convolution fusion | flops 2427715584 | bytes 7864320 | tf_op jit(solution)/shard_map/td,tch->dch/dot_general | solution.py:26
  (253 shorter events, 71.5 us)
Async XLA Ops:
  7.2 49.9 %all-gather.5.cloned.1.call-start = ((), (), s32[]{:S(2)}) async-start(), calls=%async_computation.2 | async-start | bytes 1769472 | tf_op jit(solution)/shard_map/all_gather | solution.py:154
  7.9 94.5 %all-gather.3.cloned.1.call-start = ((), (), s32[]{:S(2)}) async-start(), calls=%async_computation.1 | async-start | bytes 1769472 | tf_op jit(solution)/shard_map/all_gather | solution.py:160
  18.3 288.2 %reduce-scatter.2.cloned.1.call-start = ((), (), s32[]{:S(2)}) async-start(), calls=%async_computation.3 | async-start | bytes 1769472 | tf_op jit(solution)/shard_map/reduce_scatter | solution.py:188
  62.3 53.8 %collective-permute-start.22 = (bf16[256,512]{1,0:T(8,128)(2,1)}, bf16[256,512]{1,0:T(8,128)(2,1)}, u32[]{:S(2)}, u32[]{:S(2)}) collective-permute-start(bf16[256,512]{1,0:T(8,128)(2,1)} %fusion.70), channel_id=1, source_target_pairs={{0,1},{1,0},{2,3},{3,2},{4,5},{5,4},{6,7},{7,6},{8,9},{9,8},{10,11... | collective-permute-start | bytes 786440 | tf_op jit(solution)/shard_map/ppermute | solution.py:17
  63.7 55.1 %collective-permute-start.17 = (bf16[256,512]{1,0:T(8,128)(2,1)}, bf16[256,512]{1,0:T(8,128)(2,1)S(1)}, u32[]{:S(2)}, u32[]{:S(2)}) collective-permute-start(bf16[256,512]{1,0:T(8,128)(2,1)} %fusion.67), channel_id=1, source_target_pairs={{0,1},{1,0},{2,3},{3,2},{4,5},{5,4},{6,7},{7,6},{8,9},{9,8},{10,11... | collective-permute-start | bytes 786440 | tf_op jit(solution)/shard_map/ppermute | solution.py:17
  65.5 55.3 %collective-permute-start.12 = (bf16[256,512]{1,0:T(8,128)(2,1)}, bf16[256,512]{1,0:T(8,128)(2,1)S(1)}, u32[]{:S(2)}, u32[]{:S(2)}) collective-permute-start(bf16[256,512]{1,0:T(8,128)(2,1)} %fusion.64), channel_id=1, source_target_pairs={{0,1},{1,0},{2,3},{3,2},{4,5},{5,4},{6,7},{7,6},{8,9},{9,8},{10,11... | collective-permute-start | bytes 786440 | tf_op jit(solution)/shard_map/ppermute | solution.py:17
  66.8 55.5 %collective-permute-start.7 = (bf16[256,512]{1,0:T(8,128)(2,1)}, bf16[256,512]{1,0:T(8,128)(2,1)S(1)}, u32[]{:S(2)}, u32[]{:S(2)}) collective-permute-start(bf16[256,512]{1,0:T(8,128)(2,1)} %fusion.61), channel_id=1, source_target_pairs={{0,1},{1,0},{2,3},{3,2},{4,5},{5,4},{6,7},{7,6},{8,9},{9,8},{10,11... | collective-permute-start | bytes 786440 | tf_op jit(solution)/shard_map/ppermute | solution.py:17
  68.7 55.6 %collective-permute-start.4 = (bf16[256,512]{1,0:T(8,128)(2,1)}, bf16[256,512]{1,0:T(8,128)(2,1)S(1)}, u32[]{:S(2)}, u32[]{:S(2)}) collective-permute-start(bf16[256,512]{1,0:T(8,128)(2,1)} %convolution_convert_fusion.11), channel_id=1, source_target_pairs={{0,1},{1,0},{2,3},{3,2},{4,5},{5,4},{6,7},{7,6},{8,9},{9,8},{10,11... | collective-permute-start | bytes 786440 | tf_op jit(solution)/shard_map/ppermute | solution.py:17
  116.2 8.7 %collective-permute-start.24 = (bf16[256,512]{1,0:T(8,128)(2,1)S(1)}, bf16[256,512]{1,0:T(8,128)(2,1)S(1)}, u32[]{:S(2)}, u32[]{:S(2)}) collective-permute-start(bf16[256,512]{1,0:T(8,128)(2,1)S(1)} %convolution_convert_fusion.6), channel_id=1, source_target_pairs={{0,1},{1,0},{2,3},{3,2},{4,5},{5,4},{6,7},{7,6},{8,9},{9,8},{10,11... | collective-permute-start | bytes 786440 | tf_op jit(solution)/shard_map/ppermute | solution.py:17
  118.7 9.2 %collective-permute-start.19 = (bf16[256,512]{1,0:T(8,128)(2,1)S(1)}, bf16[256,512]{1,0:T(8,128)(2,1)S(1)}, u32[]{:S(2)}, u32[]{:S(2)}) collective-permute-start(bf16[256,512]{1,0:T(8,128)(2,1)S(1)} %convolution_convert_fusion.7), channel_id=1, source_target_pairs={{0,1},{1,0},{2,3},{3,2},{4,5},{5,4},{6,7},{7,6},{8,9},{9,8},{10,11... | collective-permute-start | bytes 786440 | tf_op jit(solution)/shard_map/ppermute | solution.py:17
  120.7 9.2 %collective-permute-start.14 = (bf16[256,512]{1,0:T(8,128)(2,1)S(1)}, bf16[256,512]{1,0:T(8,128)(2,1)S(1)}, u32[]{:S(2)}, u32[]{:S(2)}) collective-permute-start(bf16[256,512]{1,0:T(8,128)(2,1)S(1)} %convolution_convert_fusion.8), channel_id=1, source_target_pairs={{0,1},{1,0},{2,3},{3,2},{4,5},{5,4},{6,7},{7,6},{8,9},{9,8},{10,11... | collective-permute-start | bytes 786440 | tf_op jit(solution)/shard_map/ppermute | solution.py:17
  122.3 10.6 %collective-permute-start.9 = (bf16[256,512]{1,0:T(8,128)(2,1)S(1)}, bf16[256,512]{1,0:T(8,128)(2,1)S(1)}, u32[]{:S(2)}, u32[]{:S(2)}) collective-permute-start(bf16[256,512]{1,0:T(8,128)(2,1)S(1)} %convolution_convert_fusion.9), channel_id=1, source_target_pairs={{0,1},{1,0},{2,3},{3,2},{4,5},{5,4},{6,7},{7,6},{8,9},{9,8},{10,11... | collective-permute-start | bytes 786440 | tf_op jit(solution)/shard_map/ppermute | solution.py:17
  124.2 47.8 %collective-permute-start.2 = (bf16[256,3,512]{2,0,1:T(8,128)(2,1)}, bf16[256,3,512]{2,0,1:T(8,128)(2,1)}, u32[]{:S(2)}, u32[]{:S(2)}) collective-permute-start(bf16[256,3,512]{2,0,1:T(8,128)(2,1)} %convolution_convert_fusion.4), channel_id=1, source_target_pairs={{0,1},{1,0},{2,3},{3,2},{4,5},{5,4},{6,7},{7,6},{8,9},{9,8},{10,11... | collective-permute-start | bytes 2359304 | tf_op jit(solution)/shard_map/ppermute | solution.py:17
  124.9 23.1 %collective-permute-start.23 = (bf16[256,512]{1,0:T(8,128)(2,1)}, bf16[256,512]{1,0:T(8,128)(2,1)S(1)}, u32[]{:S(2)}, u32[]{:S(2)}) collective-permute-start(bf16[256,512]{1,0:T(8,128)(2,1)} %get-tuple-element.37), channel_id=1, source_target_pairs={{0,2},{1,3},{2,0},{3,1},{4,6},{5,7},{6,4},{7,5},{8,10},{9,11},{10,... | collective-permute-start | bytes 786440 | tf_op jit(solution)/shard_map/ppermute | solution.py:17
  127.9 27.4 %collective-permute-start.18 = (bf16[256,512]{1,0:T(8,128)(2,1)}, bf16[256,512]{1,0:T(8,128)(2,1)}, u32[]{:S(2)}, u32[]{:S(2)}) collective-permute-start(bf16[256,512]{1,0:T(8,128)(2,1)} %get-tuple-element.41), channel_id=1, source_target_pairs={{0,2},{1,3},{2,0},{3,1},{4,6},{5,7},{6,4},{7,5},{8,10},{9,11},{10,... | collective-permute-start | bytes 786440 | tf_op jit(solution)/shard_map/ppermute | solution.py:17
  129.9 15.6 %collective-permute-start.5 = (bf16[256,512]{1,0:T(8,128)(2,1)S(1)}, bf16[256,512]{1,0:T(8,128)(2,1)S(1)}, u32[]{:S(2)}, u32[]{:S(2)}) collective-permute-start(bf16[256,512]{1,0:T(8,128)(2,1)S(1)} %get-tuple-element.51), channel_id=1, source_target_pairs={{0,2},{1,3},{2,0},{3,1},{4,6},{5,7},{6,4},{7,5},{8,10},{9,11},{10,... | collective-permute-start | bytes 786440 | tf_op jit(solution)/shard_map/ppermute | solution.py:17
  133.0 18.3 %collective-permute-start.25 = (bf16[256,512]{1,0:T(8,128)(2,1)}, bf16[256,512]{1,0:T(8,128)(2,1)}, u32[]{:S(2)}, u32[]{:S(2)}) collective-permute-start(bf16[256,512]{1,0:T(8,128)(2,1)} %get-tuple-element.35), channel_id=1, source_target_pairs={{0,2},{1,3},{2,0},{3,1},{4,6},{5,7},{6,4},{7,5},{8,10},{9,11},{10,... | collective-permute-start | bytes 786440 | tf_op jit(solution)/shard_map/ppermute | solution.py:17
  145.5 30.7 %collective-permute-start.13 = (bf16[256,512]{1,0:T(8,128)(2,1)}, bf16[256,512]{1,0:T(8,128)(2,1)}, u32[]{:S(2)}, u32[]{:S(2)}) collective-permute-start(bf16[256,512]{1,0:T(8,128)(2,1)} %get-tuple-element.45), channel_id=1, source_target_pairs={{0,2},{1,3},{2,0},{3,1},{4,6},{5,7},{6,4},{7,5},{8,10},{9,11},{10,... | collective-permute-start | bytes 786440 | tf_op jit(solution)/shard_map/ppermute | solution.py:17
  148.0 31.7 %collective-permute-start.8 = (bf16[256,512]{1,0:T(8,128)(2,1)}, bf16[256,512]{1,0:T(8,128)(2,1)S(1)}, u32[]{:S(2)}, u32[]{:S(2)}) collective-permute-start(bf16[256,512]{1,0:T(8,128)(2,1)} %get-tuple-element.49), channel_id=1, source_target_pairs={{0,2},{1,3},{2,0},{3,1},{4,6},{5,7},{6,4},{7,5},{8,10},{9,11},{10,... | collective-permute-start | bytes 786440 | tf_op jit(solution)/shard_map/ppermute | solution.py:17
  151.2 16.7 %collective-permute-start.20 = (bf16[256,512]{1,0:T(8,128)(2,1)}, bf16[256,512]{1,0:T(8,128)(2,1)S(1)}, u32[]{:S(2)}, u32[]{:S(2)}) collective-permute-start(bf16[256,512]{1,0:T(8,128)(2,1)} %get-tuple-element.39), channel_id=1, source_target_pairs={{0,2},{1,3},{2,0},{3,1},{4,6},{5,7},{6,4},{7,5},{8,10},{9,11},{10,... | collective-permute-start | bytes 786440 | tf_op jit(solution)/shard_map/ppermute | solution.py:17
  155.3 21.4 %collective-permute-start.15 = (bf16[256,512]{1,0:T(8,128)(2,1)}, bf16[256,512]{1,0:T(8,128)(2,1)S(1)}, u32[]{:S(2)}, u32[]{:S(2)}) collective-permute-start(bf16[256,512]{1,0:T(8,128)(2,1)} %get-tuple-element.43), channel_id=1, source_target_pairs={{0,2},{1,3},{2,0},{3,1},{4,6},{5,7},{6,4},{7,5},{8,10},{9,11},{10,... | collective-permute-start | bytes 786440 | tf_op jit(solution)/shard_map/ppermute | solution.py:17
  168.0 11.7 %collective-permute-start.10 = (bf16[256,512]{1,0:T(8,128)(2,1)}, bf16[256,512]{1,0:T(8,128)(2,1)S(1)}, u32[]{:S(2)}, u32[]{:S(2)}) collective-permute-start(bf16[256,512]{1,0:T(8,128)(2,1)} %get-tuple-element.47), channel_id=1, source_target_pairs={{0,2},{1,3},{2,0},{3,1},{4,6},{5,7},{6,4},{7,5},{8,10},{9,11},{10,... | collective-permute-start | bytes 786440 | tf_op jit(solution)/shard_map/ppermute | solution.py:17
  172.0 9.5 %collective-permute-start.26 = (bf16[256,512]{1,0:T(8,128)(2,1)S(1)}, bf16[256,512]{1,0:T(8,128)(2,1)S(1)}, u32[]{:S(2)}, u32[]{:S(2)}) collective-permute-start(bf16[256,512]{1,0:T(8,128)(2,1)S(1)} %get-tuple-element.26), channel_id=1, source_target_pairs={{0,1},{1,0},{2,3},{3,2},{4,5},{5,4},{6,7},{7,6},{8,9},{9,8},{10,11... | collective-permute-start | bytes 786440 | tf_op jit(solution)/shard_map/ppermute | solution.py:17
  176.2 51.2 %collective-permute-start.21 = (bf16[256,512]{1,0:T(8,128)(2,1)}, bf16[256,512]{1,0:T(8,128)(2,1)}, u32[]{:S(2)}, u32[]{:S(2)}) collective-permute-start(bf16[256,512]{1,0:T(8,128)(2,1)} %get-tuple-element.24), channel_id=1, source_target_pairs={{0,1},{1,0},{2,3},{3,2},{4,5},{5,4},{6,7},{7,6},{8,9},{9,8},{10,11... | collective-permute-start | bytes 786440 | tf_op jit(solution)/shard_map/ppermute | solution.py:17
  176.6 19.6 %collective-permute-start.3 = (bf16[256,3,512]{2,0,1:T(8,128)(2,1)S(1)}, bf16[256,3,512]{2,0,1:T(8,128)(2,1)S(1)}, u32[]{:S(2)}, u32[]{:S(2)}) collective-permute-start(bf16[256,3,512]{2,0,1:T(8,128)(2,1)S(1)} %get-tuple-element.53), channel_id=1, source_target_pairs={{0,2},{1,3},{2,0},{3,1},{4,6},{5,7},{6,4},{7,5},{8,10},{9,11},{10,... | collective-permute-start | bytes 2359304 | tf_op jit(solution)/shard_map/ppermute | solution.py:17
  179.7 50.4 %collective-permute-start.16 = (bf16[256,512]{1,0:T(8,128)(2,1)}, bf16[256,512]{1,0:T(8,128)(2,1)}, u32[]{:S(2)}, u32[]{:S(2)}) collective-permute-start(bf16[256,512]{1,0:T(8,128)(2,1)} %get-tuple-element.22), channel_id=1, source_target_pairs={{0,1},{1,0},{2,3},{3,2},{4,5},{5,4},{6,7},{7,6},{8,9},{9,8},{10,11... | collective-permute-start | bytes 786440 | tf_op jit(solution)/shard_map/ppermute | solution.py:17
  181.1 51.6 %collective-permute-start.11 = (bf16[256,512]{1,0:T(8,128)(2,1)}, bf16[256,512]{1,0:T(8,128)(2,1)}, u32[]{:S(2)}, u32[]{:S(2)}) collective-permute-start(bf16[256,512]{1,0:T(8,128)(2,1)} %get-tuple-element.20), channel_id=1, source_target_pairs={{0,1},{1,0},{2,3},{3,2},{4,5},{5,4},{6,7},{7,6},{8,9},{9,8},{10,11... | collective-permute-start | bytes 786440 | tf_op jit(solution)/shard_map/ppermute | solution.py:17
  243.0 12.5 %collective-permute-start.33 = (bf16[256,512]{1,0:T(8,128)(2,1)S(1)}, bf16[256,512]{1,0:T(8,128)(2,1)}, u32[]{:S(2)}, u32[]{:S(2)}) collective-permute-start(bf16[256,512]{1,0:T(8,128)(2,1)S(1)} %copy-done.24), channel_id=1, source_target_pairs={{0,1},{1,0},{2,3},{3,2},{4,5},{5,4},{6,7},{7,6},{8,9},{9,8},{10,11... | collective-permute-start | bytes 786440 | tf_op jit(solution)/shard_map/ppermute | solution.py:17
  243.6 11.9 %collective-permute-start.32 = (bf16[256,512]{1,0:T(8,128)(2,1)}, bf16[256,512]{1,0:T(8,128)(2,1)}, u32[]{:S(2)}, u32[]{:S(2)}) collective-permute-start(bf16[256,512]{1,0:T(8,128)(2,1)} %get-tuple-element.23), channel_id=1, source_target_pairs={{0,1},{1,0},{2,3},{3,2},{4,5},{5,4},{6,7},{7,6},{8,9},{9,8},{10,11... | collective-permute-start | bytes 786440 | tf_op jit(solution)/shard_map/ppermute | solution.py:17
  243.7 11.8 %collective-permute-start.31 = (bf16[256,512]{1,0:T(8,128)(2,1)}, bf16[256,512]{1,0:T(8,128)(2,1)}, u32[]{:S(2)}, u32[]{:S(2)}) collective-permute-start(bf16[256,512]{1,0:T(8,128)(2,1)} %get-tuple-element.21), channel_id=1, source_target_pairs={{0,1},{1,0},{2,3},{3,2},{4,5},{5,4},{6,7},{7,6},{8,9},{9,8},{10,11... | collective-permute-start | bytes 786440 | tf_op jit(solution)/shard_map/ppermute | solution.py:17
  244.1 11.4 %collective-permute-start.30 = (bf16[256,512]{1,0:T(8,128)(2,1)}, bf16[256,512]{1,0:T(8,128)(2,1)}, u32[]{:S(2)}, u32[]{:S(2)}) collective-permute-start(bf16[256,512]{1,0:T(8,128)(2,1)} %get-tuple-element.19), channel_id=1, source_target_pairs={{0,1},{1,0},{2,3},{3,2},{4,5},{5,4},{6,7},{7,6},{8,9},{9,8},{10,11... | collective-permute-start | bytes 786440 | tf_op jit(solution)/shard_map/ppermute | solution.py:17
  255.0 52.8 %collective-permute-start.29 = (bf16[256,512]{0,1:T(8,128)(2,1)}, bf16[256,512]{0,1:T(8,128)(2,1)}, u32[]{:S(2)}, u32[]{:S(2)}) collective-permute-start(bf16[256,512]{0,1:T(8,128)(2,1)} %bitcast.172), channel_id=1, source_target_pairs={{0,1},{1,0},{2,3},{3,2},{4,5},{5,4},{6,7},{7,6},{8,9},{9,8},{10,11... | collective-permute-start | bytes 786440 | tf_op jit(solution)/shard_map/ppermute | solution.py:17
  (61 other events, 771.2 us)
Sparse Core Ops, SparseCore 0:
  10.2 46.8 all-gather.4
  59.9 42.5 all-gather.2
  243.2 63.2 reduce-scatter.1

commit v2 on v1

--- a/solution.py
+++ b/solution.py
@@ -1,8 +1,11 @@
+import functools
 import math
 
 import jax
 import jax.numpy as jnp
 from jax import lax
+from jax.experimental import pallas as pl
+from jax.experimental.pallas import tpu as pltpu
 from jax.sharding import PartitionSpec as P
 
 HEAD_DIM = 128
@@ -120,23 +123,345 @@
     return (own, other)
 
 
-def summed_product(form, rows, weight):
-    own, other = rows
-    subtotal = product(form, own, weight) + swapped(
-        product(form, other, weight).astype(jnp.bfloat16), "wid", 1
-    ).astype(jnp.float32)
-    for bit in axis_bits("wid")[1:]:
-        subtotal = subtotal + swapped(
-            subtotal.astype(jnp.bfloat16), "wid", bit
-        ).astype(jnp.float32)
-    return subtotal
+MESH = pl.DeviceIdType.MESH
+CHUNK = 512
+
+
+def forward_kernel(
+    sizes,
+    cot_ref,
+    normed_ref,
+    out_ref,
+    down_ref,
+    qkv_ref,
+    up_ref,
+    cot_all,
+    normed_all,
+    total,
+    out_w,
+    down_w,
+    qkv_w,
+    up_w,
+    core_send,
+    core_recv,
+    x_send,
+    x_recv,
+    load_sem,
+    slot_sem,
+    rise_sem,
+    fall_sem,
+    pair_sem,
+    core_out_sem,
+    core_in_sem,
+    x_out_sem,
+    x_in_sem,
+):
+    depth, out_n, down_n, up_n, width = sizes
+    hid, wid = lax.axis_index("hid"), lax.axis_index("wid")
+    z, y = hid // 2, hid % 2
+    core = wid % 2
+    above, below, pair = hid + 2, hid - 2, z * 2 + 1 - y
+    core_peer = wid + 1 - 2 * core
+    x_peer = wid + 2 - 4 * ((wid // 2) % 2)
+
+    loads = [
+        pltpu.make_async_copy(src, dst, load_sem.at[at])
+        for at, (src, dst) in enumerate(
+            [(out_ref, out_w), (down_ref, down_w), (qkv_ref, qkv_w), (up_ref, up_w)]
+        )
+    ]
+    for load in loads:
+        load.start()
+
+    gathered = (cot_all, normed_all)
+    cot_all[hid] = cot_ref[...]
+    normed_all[hid] = normed_ref[...]
+
+    barrier = pltpu.get_barrier_semaphore()
+    pl.semaphore_signal(barrier, inc=1, device_id={"hid": pair}, device_id_type=MESH)
+    pl.semaphore_signal(barrier, inc=1, device_id={"wid": core_peer}, device_id_type=MESH)
+    pl.semaphore_signal(barrier, inc=1, device_id={"wid": x_peer}, device_id_type=MESH)
+
+    @pl.when(z < depth - 1)
+    def _():
+        pl.semaphore_signal(barrier, inc=1, device_id={"hid": above}, device_id_type=MESH)
+
+    @pl.when(z > 0)
+    def _():
+        pl.semaphore_signal(barrier, inc=1, device_id={"hid": below}, device_id_type=MESH)
+
+    neighbours = 3 + jnp.where(z > 0, 1, 0) + jnp.where(z < depth - 1, 1, 0)
+    pl.semaphore_wait(barrier, neighbours)
+
+    def block_copy(kind, level, side, sems, target):
+        slot = level * 2 + side
+        return pltpu.make_async_remote_copy(
+            src_ref=gathered[kind].at[slot],
+            dst_ref=gathered[kind].at[slot],
+            send_sem=sems.at[kind, level],
+            recv_sem=slot_sem.at[kind, slot],
+            device_id={"hid": target},
+            device_id_type=MESH,
+        )
+
+    def to_pair(kind, level):
+        return block_copy(kind, level, y, pair_sem, pair)
+
+    def upward(kind, level):
+        return block_copy(kind, level, y, rise_sem, above)
+
+    def downward(kind, level):
+        return block_copy(kind, level, y, fall_sem, below)
+
+    def begin(kind):
+        @pl.when(z < depth - 1)
+        def _():
+            upward(kind, z).start()
+
+        @pl.when(z > 0)
+        def _():
+            downward(kind, z).start()
+
+        to_pair(kind, z).start()
+
+    def relay(kind, step):
+        @pl.when(z - step >= 0)
+        def _():
+            level = z - step
+            upward(kind, level).wait_recv()
+
+            @pl.when(z < depth - 1)
+            def _():
+                upward(kind, level).start()
+
+            to_pair(kind, level).start()
+
+        @pl.when(z + step <= depth - 1)
+        def _():
+            level = z + step
+            downward(kind, level).wait_recv()
+
+            @pl.when(z > 0)
+            def _():
+                downward(kind, level).start()
+
+            to_pair(kind, level).start()
+
+    def pair_arrived(kind, image):
+        for at in range(depth // 2):
+            block_copy(kind, image * (depth // 2) + at, 1 - y, pair_sem, pair).wait_recv()
+
+    def core_copy(at):
+        return pltpu.make_async_remote_copy(
+            src_ref=core_send.at[at],
+            dst_ref=core_recv.at[at],
+            send_sem=core_out_sem.at[at],
+            recv_sem=core_in_sem.at[at],
+            device_id={"wid": core_peer},
+            device_id_type=MESH,
+        )
+
+    def x_copy(at):
+        return pltpu.make_async_remote_copy(
+            src_ref=x_send.at[at],
+            dst_ref=x_recv.at[at],
+            send_sem=x_out_sem.at[at],
+            recv_sem=x_in_sem.at[at],
+            device_id={"wid": x_peer},
+            device_id_type=MESH,
+        )
+
+    def combine(at):
+        core_copy(at).wait_recv()
+        subtotal = total[at] + core_recv[at].astype(jnp.float32)
+        total[at] = subtotal
+        x_send[at] = subtotal.astype(jnp.bfloat16)
+        x_copy(at).start()
+
+    def place(image, at, part):
+        @pl.when(image == core)
+        def _():
+            total[at] = part
+
+            @pl.when(at > 0)
+            def _():
+                combine(at - 1)
+
+        @pl.when(image != core)
+        def _():
+            core_send[at] = part.astype(jnp.bfloat16)
+            core_copy(at).start()
+
+    def rows_of(kind, image):
+        rows = gathered[kind][pl.ds(image * depth, depth)]
+        return rows.reshape(rows.shape[0] * rows.shape[1], rows.shape[2])
+
+    def turned(rows, weight):
+        return lax.dot_general(
+            rows, weight, (((1,), (1,)), ((), ())), preferred_element_type=jnp.float32
+        )
+
+    def straight(rows, weight):
+        return jnp.dot(rows, weight, preferred_element_type=jnp.float32)
+
+    def span(at):
+        return pl.ds(pl.multiple_of(at * width, width), width)
+
+    first_qkv = out_n + down_n
+    first_up = first_qkv + 3
+
+    def cot_products(image):
+        @pl.loop(0, out_n)
+        def _(at):
+            place(image, at, turned(rows_of(0, image), out_w[span(at), :]))
+
+        @pl.loop(0, down_n)
+        def _(at):
+            place(image, out_n + at, turned(rows_of(0, image), down_w[span(at), :]))
+
+    def normed_products(image):
+        @pl.loop(0, 3)
+        def _(at):
+            place(image, first_qkv + at, straight(rows_of(1, image), qkv_w[at]))
+
+        @pl.loop(0, up_n)
+        def _(at):
+            place(image, first_up + at, straight(rows_of(1, image), up_w[:, span(at)]))
+
+        @pl.when(image == core)
+        def _():
+            combine(first_up + up_n - 1)
+
+    begin(0)
+    begin(1)
+    near = z // (depth // 2)
+    far = 1 - near
+    for step in range(1, depth // 2):
+        relay(0, step)
+        relay(1, step)
+    late = list(range(depth // 2, depth))
+    pair_arrived(0, near)
+    for load in loads[:2]:
+        load.wait()
+    cot_products(near)
+    for step in late[: len(late) // 2]:
+        relay(0, step)
+        relay(1, step)
+    pair_arrived(1, near)
+    for load in loads[2:]:
+        load.wait()
+    normed_products(near)
+    for step in late[len(late) // 2 :]:
+        relay(0, step)
+        relay(1, step)
+    pair_arrived(0, far)
+    cot_products(far)
+    pair_arrived(1, far)
+    normed_products(far)
+
+    @pl.loop(0, first_up + up_n)
+    def _(at):
+        x_copy(at).wait_recv()
+        total[at] = total[at] + x_recv[at].astype(jnp.float32)
+
+    @pl.loop(0, first_up + up_n)
+    def _(at):
+        core_copy(at).wait_send()
+        x_copy(at).wait_send()
+
+    for kind in range(2):
+        for level in range(depth):
+            to_pair(kind, level).wait_send()
+
+            @pl.when((z < depth - 1) & (level <= z))
+            def _():
+                upward(kind, level).wait_send()
+
+            @pl.when((z > 0) & (level >= z))
+            def _():
+                downward(kind, level).wait_send()
+
+
+def forward_products(cotangent, normed, out_weight, down_weight, qkv_weight, up_weight):
+    blocks = lax.axis_size("hid")
+    depth = blocks // 2
+    rows, columns = cotangent.shape
+    width = min(CHUNK, out_weight.shape[0])
+    out_n, down_n, up_n = (
+        out_weight.shape[0] // width,
+        down_weight.shape[0] // width,
+        up_weight.shape[1] // width,
+    )
+    assert qkv_weight.shape[2] == width
+    count = out_n + down_n + 3 + up_n
+    half = rows * depth
+    vmem = pl.BlockSpec(memory_space=pltpu.VMEM)
+    hbm = pl.BlockSpec(memory_space=pl.ANY)
+    all_shape = jax.ShapeDtypeStruct((blocks, rows, columns), jnp.bfloat16)
+    weights = (out_weight, down_weight, qkv_weight, up_weight)
+    slots = pltpu.VMEM((count, half, width), jnp.bfloat16)
+    macs = 2 * half * columns * width * count
+    return pl.pallas_call(
+        functools.partial(forward_kernel, (depth, out_n, down_n, up_n, width)),
+        out_shape=(
+            all_shape,
+            all_shape,
+            jax.ShapeDtypeStruct((count, half, width), jnp.float32),
+        ),
+        in_specs=[vmem, vmem, hbm, hbm, hbm, hbm],
+        out_specs=(vmem, vmem, vmem),
+        scratch_shapes=[pltpu.VMEM(weight.shape, weight.dtype) for weight in weights]
+        + [slots] * 4
+        + [
+            pltpu.SemaphoreType.DMA((4,)),
+            pltpu.SemaphoreType.DMA((2, blocks)),
+            pltpu.SemaphoreType.DMA((2, depth)),
+            pltpu.SemaphoreType.DMA((2, depth)),
+            pltpu.SemaphoreType.DMA((2, depth)),
+            pltpu.SemaphoreType.DMA((count,)),
+            pltpu.SemaphoreType.DMA((count,)),
+            pltpu.SemaphoreType.DMA((count,)),
+            pltpu.SemaphoreType.DMA((count,)),
+        ],
+        compiler_params=pltpu.CompilerParams(
+            collective_id=0, has_side_effects=True, vmem_limit_bytes=56 * 1024 * 1024
+        ),
+        cost_estimate=pl.CostEstimate(
+            flops=2 * macs, bytes_accessed=32 * 1024 * 1024, transcendentals=0
+        ),
+        name="forward_products",
+    )(cotangent, normed, *weights)
+
+
+def scatter_sum(partial):
+    size = lax.axis_size("hid")
+    depth = size // 2
+    index = lax.axis_index("hid")
+    z, y = index // 2, index % 2
+    blocks = partial.reshape(depth, 2, partial.shape[0] // size, partial.shape[1])
+    mine = lax.dynamic_index_in_dim(blocks, y, axis=1, keepdims=False)
+    given = lax.dynamic_index_in_dim(blocks, 1 - y, axis=1, keepdims=False)
+    mine = mine + swapped(given.astype(jnp.bfloat16), "hid", 1).astype(jnp.float32)
+
+    def share(level):
+        return lax.dynamic_index_in_dim(mine, level, axis=0, keepdims=False)
+
+    result = share(z)
+    for way in (1, -1):
+        pairs = [
+            (at, at + 2 * way) for at in range(size) if 0 <= at + 2 * way < size
+        ]
+        flow = None
+        for far in range(depth - 1, 0, -1):
+            part = share(jnp.clip(z + way * far, 0, depth - 1))
+            flow = part if flow is None else flow + part
+            flow = lax.ppermute(flow.astype(jnp.bfloat16), "hid", pairs).astype(jnp.float32)
+        result = result + flow
+    return result
 
 
 def both_halves(own):
     return jnp.concatenate([own, swapped(own, "wid", 1)], axis=0)
-
-
-CHUNKS = 4
 
 
 def local(
@@ -151,46 +476,52 @@
     key_gain,
 ):
     core = lax.axis_index("wid") % 2
-    grad_all = lax.all_gather(cotangent, "hid", axis=0, tiled=True)
     input_rows = inputs.astype(jnp.float32)
     centre, inverse, total_count = row_moments(input_rows)
     inverse = inverse[:, None]
     unit_rows = (input_rows - centre[:, None]) * inverse
     normed = (unit_rows * norm_gain).astype(jnp.bfloat16)
-    normed_all = lax.all_gather(normed, "hid", axis=0, tiled=True)
-    grad_halves = halves(grad_all, core)
-    normed_halves = halves(normed_all, core)
-    grad_order = jnp.concatenate(grad_halves, axis=0)
-    normed_order = jnp.concatenate(normed_halves, axis=0)
-
-    att_grad = summed_product("td,hd->th", grad_halves, out_weight).astype(jnp.bfloat16)
-    width = up_weight.shape[1] // CHUNKS
-    spans = [slice(at * width, (at + 1) * width) for at in range(CHUNKS)]
-    hidden_grads = [
-        summed_product("td,fd->tf", grad_halves, down_weight[span]) for span in spans
-    ]
-    qkv_rows = summed_product("td,dch->tch", normed_halves, qkv_weight)
+    grad_all, normed_all, total = forward_products(
+        cotangent,
+        normed,
+        out_weight,
+        down_weight,
+        jnp.transpose(qkv_weight, (1, 0, 2)),
+        up_weight,
+    )
+    for bit in axis_bits("wid")[2:]:
+        total = total + swapped(total.astype(jnp.bfloat16), "wid", bit).astype(jnp.float32)
+    grad_all = grad_all.reshape(-1, grad_all.shape[2])
+    normed_all = normed_all.reshape(-1, normed_all.shape[2])
+    grad_order = jnp.concatenate(halves(grad_all, core), axis=0)
+    normed_order = jnp.concatenate(halves(normed_all, core), axis=0)
+    out_n = out_weight.shape[0] // total.shape[2]
+    down_n = down_weight.shape[0] // total.shape[2]
+
+    def side_by_side(pieces):
+        return jnp.concatenate(list(pieces), axis=1)
+
+    att_grad = side_by_side(total[:out_n]).astype(jnp.bfloat16)
+    qkv_rows = jnp.transpose(total[out_n + down_n : out_n + down_n + 3], (1, 0, 2))
+    hidden, pre_grad = [], []
+    for at in range(down_n):
+        hidden_own, pre_own = gelu_pair(total[out_n + down_n + 3 + at], total[out_n + at])
+        hidden.append(hidden_own)
+        pre_grad.append(pre_own)
+    pre_grad = both_halves(side_by_side(pre_grad))
     attended, qkv_back = attention_pair(qkv_rows, att_grad, query_gain, key_gain)
+    qkv_back = both_halves(qkv_back)
+    hidden = both_halves(side_by_side(hidden))
     attended = both_halves(attended)
-    qkv_back = both_halves(qkv_back)
-    normed_grad = product("tch,dch->td", qkv_back, qkv_weight)
-    hidden, pre_grad = [], []
-    for span, hidden_grad in zip(spans, hidden_grads):
-        pre_act = summed_product("td,df->tf", normed_halves, up_weight[:, span])
-        hidden_own, pre_own = gelu_pair(pre_act, hidden_grad)
-        pre_both = both_halves(pre_own)
-        pre_grad.append(pre_both)
-        hidden.append(both_halves(hidden_own))
-        normed_grad = normed_grad + product("tf,df->td", pre_both, up_weight[:, span])
-    hidden = jnp.concatenate(hidden, axis=1)
-    pre_grad = jnp.concatenate(pre_grad, axis=1)
-    normed_grad = jnp.concatenate(halves(normed_grad, core), axis=0).astype(jnp.bfloat16)
-    normed_grad = lax.psum_scatter(normed_grad, "hid", scatter_dimension=0, tiled=True)
+    normed_grad = product("tf,df->td", pre_grad, up_weight) + product(
+        "tch,dch->td", qkv_back, qkv_weight
+    )
+    normed_grad = scatter_sum(jnp.concatenate(halves(normed_grad, core), axis=0))
     qkv_grad = product("td,tch->dch", normed_order, qkv_back).astype(jnp.bfloat16)
     out_grad = product("th,td->hd", attended, grad_order).astype(jnp.bfloat16)
     up_grad = product("td,tf->df", normed_order, pre_grad).astype(jnp.bfloat16)
     down_grad = product("tf,td->fd", hidden, grad_order).astype(jnp.bfloat16)
-    unit_grad = normed_grad.astype(jnp.float32) * norm_gain
+    unit_grad = normed_grad * norm_gain
     grad_total, grad_project = row_totals(
         jnp.stack([jnp.sum(unit_grad, axis=-1), jnp.sum(unit_grad * unit_rows, axis=-1)])
     )

time: 325 us -> 234 us (0.72)
  waiting for transfers between devices: 155 us -> 32.6 us
  Pallas kernels: 0 us -> 77.9 us
  matrix products: 94.8 us -> 51.2 us
  starting transfers between devices: 20.3 us -> 38.3 us
  between operations: 14.7 us -> 1.51 us
  other arithmetic: 25.7 us -> 18.7 us
    pallas_call x0 -> x1, Pallas kernels: none -> 77.9 us  [forward_products(): pl.pallas_call(functools.partial(forward_kernel, (depth, out_n, down_n, u...]
    all_gather x2 -> x0, waiting for transfers between devices: 72.5 us -> none  [the longest x1 38.7 us: local(): grad_all = lax.all_gather(cotangent, 'hid', axis=0, tiled=True)]
    reduce_scatter x1 -> x0, waiting for transfers between devices: 43.4 us -> none  [local(): lax.psum_scatter(normed_grad, 'hid', scatter_dimension=0, tiled=True)]
    dot_general x35 -> x12, matrix products: 92.4 us -> 49.7 us  [product(): jnp.einsum(form, left_arr, right_arr, preferred_element_type=jnp.float32)]
    ppermute x34 -> x9, waiting for transfers between devices: 38.3 us -> 19.3 us  [swapped(): return lax.ppermute(value, axis, [(at, at ^ bit) for at in range(size)])]
    ppermute x0 -> x6, starting transfers between devices: none -> 16.5 us  [scatter_sum(): lax.ppermute(flow.astype(jnp.bfloat16), 'hid', pairs).astype(jnp.float32)]
    ppermute x0 -> x6, waiting for transfers between devices: none -> 13.4 us  [scatter_sum(): lax.ppermute(flow.astype(jnp.bfloat16), 'hid', pairs).astype(jnp.float32)]
    convert_element_type x4 -> x1, other arithmetic: 8.85 us -> 4.56 us  [gelu_pair(): hidden.astype(jnp.bfloat16)]
  transfers between devices with their start and end apart: 37 -> 15, of which waited for: 9 -> 6; matrix products, arithmetic and copies ran while one was open for 39% -> 20% of each run, Pallas kernels for 0% -> 0%
where the time goes in v2:
time: 234 us; the launch traced here: 233 us
  Pallas kernels  77.9 us (33%)
  matrix products  51.2 us (22%)
  starting transfers between devices  38.3 us (16%)
  waiting for transfers between devices  32.6 us (14%)
  other arithmetic  18.7 us (8%)
  local copies, waits for them, and re-layouts  13.3 us (6%)
    pallas_call x1, Pallas kernels, forward_products(): pl.pallas_call(functools.partial(forward_kernel, (depth, out_n, down_n, u...  77.9 us
    dot_general x12, matrix products, product(): jnp.einsum(form, left_arr, right_arr, preferred_element_type=jnp.float32)  49.7 us
    ppermute x9, starting transfers between devices, swapped(): return lax.ppermute(value, axis, [(at, at ^ bit) for at in range(size)])  21.8 us
    ppermute x9, waiting for transfers between devices, swapped(): return lax.ppermute(value, axis, [(at, at ^ bit) for at in range(size)])  19.3 us
    ppermute x6, starting transfers between devices, scatter_sum(): lax.ppermute(flow.astype(jnp.bfloat16), 'hid', pairs).astype(jnp.float32)  16.5 us
    ppermute x6, waiting for transfers between devices, scatter_sum(): lax.ppermute(flow.astype(jnp.bfloat16), 'hid', pairs).astype(jnp.float32)  13.4 us
    unnamed x80, local copies, waits for them, and re-layouts  4.68 us
  transfers between devices with their start and end apart: 15, of which 6 were waited for; matrix products, arithmetic and copies ran while one was open for 20% of the time, Pallas kernels for 0%

profile of v2, /device:TPU:0, one launch (start us, length us, event | category | flops | bytes accessed | tf_op | source)
XLA Modules:
  0.0 233.5 jit_solution(6755801733030920092)
XLA Ops:
  4.2 2.9 %collective-permute-start.1 = (f32[2,64]{1,0:T(2,128)S(1)}, f32[2,64]{1,0:T(2,128)S(1)}, u32[]{:S(2)}, u32[]{:S(2)}) collective-permute-start(f32[2,64]{1,0:T(2,128)S(1)} %pad_maximum_fusion.15), channel_id=1, source_target_pairs={{0,2},{1,3},{2,0},{3,1},{4,6},{5,7},{6,4},{7,5},{8,10},{9,11},{10,... | collective-permute-start | bytes 1544 | tf_op jit(solution)/shard_map/ppermute | solution.py:20
  7.1 1.5 collective-permute-done.1
  8.7 1.7 fusion.82.normed_ref
  10.4 77.9 %forward_products.1 = (bf16[8,64,1536]{2,1,0:T(8,128)(2,1)}, bf16[8,64,1536]{2,1,0:T(8,128)(2,1)}, f32[12,256,512]{2,1,0:T(8,128)}) custom-call(bf16[64,1536]{1,0:T(8,128)(2,1)} %cot_ref.1, bf16[64,1536]{1,0:T(8,128)(2,1)} %fusion.82.normed_ref, bf16[512,1536]{1,0:T(8,128)(2,1)} %out_ref.1, bf16[2048,1536]{1,0:T(8,128)(2,1)} %down_ref.1, ...), custom_call_target="tpu_custom_call" | custom-call | flops 9663676416 | bytes 33554432 | tf_op jit(solution)/shard_map/forward_products/pallas_call | solution.py:404
  89.4 1.5 slice_bitcast_fusion
  95.1 1.4 fusion.73
  97.9 1.4 fusion.128
  99.3 2.8 %fusion.119 = (f32[256,4]{0,1:T(4,128)S(1)}, f32[256,4]{0,1:T(4,128)S(1)}, f32[1,256,4,128]{1,3,2,0:T(8,128)}) fusion(f32[256,4]{0,1:T(4,128)S(1)} %add_rsqrt_fusion.1, f32[1,256,4,128]{1,3,2,0:T(8,128)S(1)} %bitcast.263, f32[256,4]{0,1:T(4,128)S(1)} %broadcast_multiply_fusion.5, f32[128]{0:T(128)S(1)} %copy-done.37, bf16[256,4,128]{0,2,1:T(8,128)(2,1)} %copy-done.11, ...), kind=kOutput, calls=%fused_computation.209 | convolution fusion | flops 69205248 | bytes 3424768 | tf_op jit(solution)/shard_map/ihpq,iqha->ipha/dot_general | solution.py:29
  102.1 2.8 %fusion.120 = (f32[256,4]{0,1:T(4,128)S(1)}, f32[256,4]{0,1:T(4,128)S(1)}, f32[1,256,4,128]{1,3,2,0:T(8,128)}) fusion(f32[256,4]{0,1:T(4,128)S(1)} %add_rsqrt_fusion, f32[1,256,4,128]{1,3,2,0:T(8,128)S(1)} %bitcast.261, f32[256,4]{0,1:T(4,128)S(1)} %broadcast_multiply_fusion.4, f32[128]{0:T(128)S(1)} %copy-done.38, bf16[256,4,128]{0,2,1:T(8,128)(2,1)} %copy-done.12, ...), kind=kOutput, calls=%fused_computation.210 | convolution fusion | flops 69205248 | bytes 3424768 | tf_op jit(solution)/shard_map/ihpq,ipha->iqha/dot_general | solution.py:29
  104.9 1.4 convolution_convert_fusion.5
  106.5 1.2 multiply_convert_fusion.1
  109.1 17.2 %collective-permute-start.3 = (bf16[256,3,512]{2,0,1:T(8,128)(2,1)}, bf16[256,3,512]{2,0,1:T(8,128)(2,1)}, u32[]{:S(2)}, u32[]{:S(2)}) collective-permute-start(bf16[256,3,512]{2,0,1:T(8,128)(2,1)} %pad_maximum_fusion.11), channel_id=1, source_target_pairs={{0,1},{1,0},{2,3},{3,2},{4,5},{5,4},{6,7},{7,6},{8,9},{9,8},{10,11... | collective-permute-start | bytes 2359304 | tf_op jit(solution)/shard_map/ppermute | solution.py:20
  126.3 4.6 %fusion.68 = (bf16[256,512]{1,0:T(8,128)(2,1)}, bf16[256,512]{1,0:T(8,128)(2,1)}, bf16[256,512]{1,0:T(8,128)(2,1)S(1)}, bf16[256,512]{1,0:T(8,128)(2,1)}, bf16[2...) fusion(f32[12,256,512]{2,1,0:T(8,128)} %get-tuple-element.8), kind=kLoop, calls=%fused_computation.113 | loop fusion | flops 11534336 | bytes 6291456 | tf_op jit(solution)/shard_map/convert_element_type | solution.py:51
  131.7 5.0 %convolution_bitcast_fusion = f32[512,1536]{1,0:T(8,128)S(1)} fusion(bf16[1536,3,512]{2,0,1:T(8,128)(2,1)} %param.12, bf16[256,3,512]{2,0,1:T(8,128)(2,1)} %collective-permute-done.3, bf16[256,1,512]{2,0,1:T(8,128)(2,1)S(1)} %copy.133, bf16[256,1,512]{2,0,1:T(8,128)(2,1)S(1)} %copy.132, bf16[256,1,512]{2,0,1:T(8,128)(2,1)S(1)} %copy.131), kind=kOutput, calls=%fused_computation.4 | convolution fusion | flops 2422210560 | bytes 9437184 | tf_op jit(solution)/shard_map/tch,dch->td/dot_general | solution.py:29
  136.8 6.6 %convolution_add_fusion = f32[512,1536]{1,0:T(8,128)S(1)} fusion(f32[512,1536]{1,0:T(8,128)S(1)} %convolution_bitcast_fusion, bf16[1536,2048]{1,0:T(8,128)(2,1)} %up_ref.1, bf16[256,2048]{1,0:T(8,128)(2,1)} %collective-permute-done.2, bf16[256,512]{1,0:T(8,128)(2,1)S(1)} %get-tuple-element.20, bf16[256,512]{1,0:T(8,128)(2,1)S(1)} %get-tuple-element.22, ...), kind=kOutput, calls=%fused_computation.5 | convolution fusion | flops 3232497664 | bytes 14680064 | tf_op jit(solution)/shard_map/tf,df->td/dot_general | solution.py:29
  143.9 1.6 copy-done
  148.0 1.4 constant_dynamic-slice_fusion.1
  149.4 16.9 %collective-permute-done.4 = bf16[4,64,1536]{2,1,0:T(8,128)(2,1)} collective-permute-done((bf16[4,64,1536]{2,1,0:T(8,128)(2,1)}, bf16[4,64,1536]{2,1,0:T(8,128)(2,1)}, u32[]{:S(2)}, u32[]{:S(2)}) %collective-permute-start.4) | collective-permute-done | bytes 786464 | tf_op jit(solution)/shard_map/ppermute | solution.py:20
  166.3 1.4 bitcast_add_fusion
  167.7 3.6 %collective-permute-start.5 = (bf16[64,1536]{1,0:T(8,128)(2,1)S(1)}, bf16[64,1536]{1,0:T(8,128)(2,1)S(1)}, u32[]{:S(2)}, u32[]{:S(2)}) collective-permute-start(bf16[64,1536]{1,0:T(8,128)(2,1)S(1)} %get-tuple-element.36), channel_id=1, source_target_pairs={{0,8},{4,12},{8,16},{12,20},{16,24},{20,28},{1,9},{5,13},{9,17},{1... | collective-permute-start | bytes 589832 | tf_op jit(solution)/shard_map/ppermute | solution.py:458
  171.4 1.3 collective-permute-start.8
  172.8 2.0 collective-permute-done.5
  174.8 9.7 %collective-permute-done.8 = bf16[64,1536]{1,0:T(8,128)(2,1)S(1)} collective-permute-done((bf16[64,1536]{1,0:T(8,128)(2,1)S(1)}, bf16[64,1536]{1,0:T(8,128)(2,1)S(1)}, u32[]{:S(2)}, u32[]{:S(2)}) %collective-permute-start.8) | collective-permute-done | bytes 196640 | tf_op jit(solution)/shard_map/ppermute | solution.py:458
  185.3 4.3 %collective-permute-start.6 = (bf16[64,1536]{1,0:T(8,128)(2,1)}, bf16[64,1536]{1,0:T(8,128)(2,1)}, u32[]{:S(2)}, u32[]{:S(2)}) collective-permute-start(bf16[64,1536]{1,0:T(8,128)(2,1)} %get-tuple-element.34), channel_id=1, source_target_pairs={{0,8},{4,12},{8,16},{12,20},{16,24},{20,28},{1,9},{5,13},{9,17},{1... | collective-permute-start | bytes 589832 | tf_op jit(solution)/shard_map/ppermute | solution.py:458
  189.6 1.3 collective-permute-start.9
  194.4 3.8 %convolution_convert_fusion.3 = bf16[512,1536]{1,0:T(8,128)(2,1)} fusion(bf16[256,1536]{1,0:T(8,128)(2,1)} %get-tuple-element.29, bf16[256,1536]{1,0:T(8,128)(2,1)} %get-tuple-element.28, bf16[256,512]{0,1:T(8,128)(2,1)} %collective-permute-done.13, bf16[256,512]{0,1:T(8,128)(2,1)} %bitcast.46), kind=kOutput, calls=%fused_computation.7 | convolution fusion | flops 810287104 | bytes 3670016 | tf_op jit(solution)/shard_map/th,td->hd/dot_general | solution.py:29
  199.3 4.6 %collective-permute-start.7 = (bf16[64,1536]{1,0:T(8,128)(2,1)S(1)}, bf16[64,1536]{1,0:T(8,128)(2,1)S(1)}, u32[]{:S(2)}, u32[]{:S(2)}) collective-permute-start(bf16[64,1536]{1,0:T(8,128)(2,1)S(1)} %get-tuple-element.32), channel_id=1, source_target_pairs={{0,8},{4,12},{8,16},{12,20},{16,24},{20,28},{1,9},{5,13},{9,17},{1... | collective-permute-start | bytes 589832 | tf_op jit(solution)/shard_map/ppermute | solution.py:458
  203.9 1.4 collective-permute-start.10
  205.4 5.9 %convolution_convert_fusion.2 = bf16[1536,3,512]{2,0,1:T(8,128)(2,1)} fusion(bf16[256,1536]{0,1:T(8,128)(2,1)S(1)} %copy-done.32, bf16[256,1536]{0,1:T(8,128)(2,1)S(1)} %copy-done.31, bf16[256,3,512]{2,0,1:T(8,128)(2,1)} %collective-permute-done.3, bf16[256,1,512]{2,0,1:T(8,128)(2,1)S(1)} %copy.133, bf16[256,1,512]{2,0,1:T(8,128)(2,1)S(1)} %copy-done.8, ...), kind=kOutput, calls=%fused_computation.3 | convolution fusion | flops 2427715584 | bytes 7864320 | tf_op jit(solution)/shard_map/td,tch->dch/dot_general | solution.py:29
  211.4 1.6 collective-permute-done.10
  213.4 7.5 %convolution_convert_fusion.1 = bf16[1536,2048]{1,0:T(8,128)(2,1)} fusion(bf16[256,1536]{0,1:T(8,128)(2,1)S(1)} %copy-done.32, bf16[256,1536]{0,1:T(8,128)(2,1)S(1)} %copy-done.31, bf16[256,2048]{1,0:T(8,128)(2,1)} %collective-permute-done.2, bf16[256,512]{1,0:T(8,128)(2,1)S(1)} %copy-done.22, bf16[256,512]{1,0:T(8,128)(2,1)S(1)} %copy-done.24, ...), kind=kOutput, calls=%fused_computation.2 | convolution fusion | flops 3238002688 | bytes 9961472 | tf_op jit(solution)/shard_map/td,tf->df/dot_general | solution.py:29
  221.5 11.0 %convolution_convert_fusion = bf16[2048,1536]{1,0:T(8,128)(2,1)} fusion(bf16[256,2048]{1,0:T(8,128)(2,1)S(1)} %collective-permute-done.14, bf16[256,512]{1,0:T(8,128)(2,1)S(1)} %copy-done.16, bf16[256,512]{1,0:T(8,128)(2,1)S(1)} %copy-done.18, bf16[256,512]{1,0:T(8,128)(2,1)S(1)} %copy-done.20, bf16[256,512]{1,0:T(8,128)(2,1)S(1)} %copy-done.14, ...), kind=kOutput, calls=%fused_computation.1 | convolution fusion | flops 3238002688 | bytes 9961472 | tf_op jit(solution)/shard_map/tf,td->fd/dot_general | solution.py:29
  (154 shorter events, 22.6 us)
Async XLA Ops:
  2.9 1.3 collective-permute-start
  4.2 4.4 %collective-permute-start.1 = (f32[2,64]{1,0:T(2,128)S(1)}, f32[2,64]{1,0:T(2,128)S(1)}, u32[]{:S(2)}, u32[]{:S(2)}) collective-permute-start(f32[2,64]{1,0:T(2,128)S(1)} %pad_maximum_fusion.15), channel_id=1, source_target_pairs={{0,2},{1,3},{2,0},{3,1},{4,6},{5,7},{6,4},{7,5},{8,10},{9,11},{10,... | collective-permute-start | bytes 1544 | tf_op jit(solution)/shard_map/ppermute | solution.py:20
  107.8 23.9 %copy-start.5 = (bf16[256,1,512]{2,0,1:T(8,128)(2,1)}, bf16[256,1,512]{2,0,1:T(8,128)(2,1)S(1)}, u32[]{:S(2)}) copy-start(bf16[256,1,512]{2,0,1:T(8,128)(2,1)S(1)} %copy.131) | copy-start | bytes 786436
  108.1 23.6 %copy-start.7 = (bf16[256,1,512]{2,0,1:T(8,128)(2,1)}, bf16[256,1,512]{2,0,1:T(8,128)(2,1)S(1)}, u32[]{:S(2)}) copy-start(bf16[256,1,512]{2,0,1:T(8,128)(2,1)S(1)} %copy.132) | copy-start | bytes 786436
  109.1 22.6 %collective-permute-start.3 = (bf16[256,3,512]{2,0,1:T(8,128)(2,1)}, bf16[256,3,512]{2,0,1:T(8,128)(2,1)}, u32[]{:S(2)}, u32[]{:S(2)}) collective-permute-start(bf16[256,3,512]{2,0,1:T(8,128)(2,1)} %pad_maximum_fusion.11), channel_id=1, source_target_pairs={{0,1},{1,0},{2,3},{3,2},{4,5},{5,4},{6,7},{7,6},{8,9},{9,8},{10,11... | collective-permute-start | bytes 2359304 | tf_op jit(solution)/shard_map/ppermute | solution.py:20
  131.0 5.7 %collective-permute-start.2 = (bf16[256,2048]{1,0:T(8,128)(2,1)S(1)}, bf16[256,2048]{1,0:T(8,128)(2,1)}, u32[]{:S(2)}, u32[]{:S(2)}) collective-permute-start(bf16[256,2048]{1,0:T(8,128)(2,1)S(1)} %pad_maximum_fusion.5), channel_id=1, source_target_pairs={{0,1},{1,0},{2,3},{3,2},{4,5},{5,4},{6,7},{7,6},{8,9},{9,8},{10,11... | collective-permute-start | bytes 3145736 | tf_op jit(solution)/shard_map/ppermute | solution.py:20
  146.5 19.8 %collective-permute-start.4 = (bf16[4,64,1536]{2,1,0:T(8,128)(2,1)}, bf16[4,64,1536]{2,1,0:T(8,128)(2,1)}, u32[]{:S(2)}, u32[]{:S(2)}) collective-permute-start(bf16[4,64,1536]{2,1,0:T(8,128)(2,1)} %fusion.24), channel_id=1, source_target_pairs={{0,4},{4,0},{8,12},{12,8},{16,20},{20,16},{24,28},{28,24},{1,5},{5... | collective-permute-start | bytes 2359304 | tf_op jit(solution)/shard_map/ppermute | solution.py:20
  148.0 18.2 %copy-start.1 = (f32[512,1536]{1,0:T(8,128)S(1)}, f32[512,1536]{1,0:T(8,128)}, u32[]{:S(2)}) copy-start(f32[512,1536]{1,0:T(8,128)} %copy-done) | copy-start | bytes 9437188
  148.0 46.4 %collective-permute-start.13 = (bf16[256,512]{0,1:T(8,128)(2,1)}, bf16[256,512]{0,1:T(8,128)(2,1)}, u32[]{:S(2)}, u32[]{:S(2)}) collective-permute-start(bf16[256,512]{0,1:T(8,128)(2,1)} %bitcast.46), channel_id=1, source_target_pairs={{0,1},{1,0},{2,3},{3,2},{4,5},{5,4},{6,7},{7,6},{8,9},{9,8},{10,11... | collective-permute-start | bytes 786440 | tf_op jit(solution)/shard_map/ppermute | solution.py:20
  149.4 23.3 %copy-start.3 = (bf16[8,64,1536]{2,1,0:T(8,128)(2,1)S(1)}, bf16[8,64,1536]{2,1,0:T(8,128)(2,1)}, u32[]{:S(2)}) copy-start(bf16[8,64,1536]{2,1,0:T(8,128)(2,1)} %get-tuple-element.9) | copy-start | bytes 4718596
  167.6 23.3 %copy-start.13 = (bf16[256,512]{1,0:T(8,128)(2,1)S(1)}, bf16[256,512]{1,0:T(8,128)(2,1)}, u32[]{:S(2)}) copy-start(bf16[256,512]{1,0:T(8,128)(2,1)} %get-tuple-element.18) | copy-start | bytes 786436
  167.6 23.3 %copy-start.15 = (bf16[256,512]{1,0:T(8,128)(2,1)S(1)}, bf16[256,512]{1,0:T(8,128)(2,1)}, u32[]{:S(2)}) copy-start(bf16[256,512]{1,0:T(8,128)(2,1)} %get-tuple-element.19) | copy-start | bytes 786436
  167.6 23.3 %copy-start.17 = (bf16[256,512]{1,0:T(8,128)(2,1)S(1)}, bf16[256,512]{1,0:T(8,128)(2,1)}, u32[]{:S(2)}) copy-start(bf16[256,512]{1,0:T(8,128)(2,1)} %get-tuple-element.21) | copy-start | bytes 786436
  167.7 23.3 %copy-start.19 = (bf16[256,512]{1,0:T(8,128)(2,1)S(1)}, bf16[256,512]{1,0:T(8,128)(2,1)}, u32[]{:S(2)}) copy-start(bf16[256,512]{1,0:T(8,128)(2,1)} %get-tuple-element.23) | copy-start | bytes 786436
  167.7 7.1 %collective-permute-start.5 = (bf16[64,1536]{1,0:T(8,128)(2,1)S(1)}, bf16[64,1536]{1,0:T(8,128)(2,1)S(1)}, u32[]{:S(2)}, u32[]{:S(2)}) collective-permute-start(bf16[64,1536]{1,0:T(8,128)(2,1)S(1)} %get-tuple-element.36), channel_id=1, source_target_pairs={{0,8},{4,12},{8,16},{12,20},{16,24},{20,28},{1,9},{5,13},{9,17},{1... | collective-permute-start | bytes 589832 | tf_op jit(solution)/shard_map/ppermute | solution.py:458
  171.4 13.2 %collective-permute-start.8 = (bf16[64,1536]{1,0:T(8,128)(2,1)S(1)}, bf16[64,1536]{1,0:T(8,128)(2,1)S(1)}, u32[]{:S(2)}, u32[]{:S(2)}) collective-permute-start(bf16[64,1536]{1,0:T(8,128)(2,1)S(1)} %get-tuple-element.37), channel_id=1, source_target_pairs={{8,0},{12,4},{16,8},{20,12},{24,16},{28,20},{9,1},{13,5},{17,9},{2... | collective-permute-start | bytes 589832 | tf_op jit(solution)/shard_map/ppermute | solution.py:458
  185.3 12.9 %collective-permute-start.6 = (bf16[64,1536]{1,0:T(8,128)(2,1)}, bf16[64,1536]{1,0:T(8,128)(2,1)}, u32[]{:S(2)}, u32[]{:S(2)}) collective-permute-start(bf16[64,1536]{1,0:T(8,128)(2,1)} %get-tuple-element.34), channel_id=1, source_target_pairs={{0,8},{4,12},{8,16},{12,20},{16,24},{20,28},{1,9},{5,13},{9,17},{1... | collective-permute-start | bytes 589832 | tf_op jit(solution)/shard_map/ppermute | solution.py:458
  189.6 8.6 %collective-permute-start.9 = (bf16[64,1536]{1,0:T(8,128)(2,1)}, bf16[64,1536]{1,0:T(8,128)(2,1)}, u32[]{:S(2)}, u32[]{:S(2)}) collective-permute-start(bf16[64,1536]{1,0:T(8,128)(2,1)} %get-tuple-element.35), channel_id=1, source_target_pairs={{8,0},{12,4},{16,8},{20,12},{24,16},{28,20},{9,1},{13,5},{17,9},{2... | collective-permute-start | bytes 589832 | tf_op jit(solution)/shard_map/ppermute | solution.py:458
  194.4 27.1 %collective-permute-start.14 = (bf16[256,2048]{1,0:T(8,128)(2,1)}, bf16[256,2048]{1,0:T(8,128)(2,1)S(1)}, u32[]{:S(2)}, u32[]{:S(2)}) collective-permute-start(bf16[256,2048]{1,0:T(8,128)(2,1)} %pad_maximum_fusion.6), channel_id=1, source_target_pairs={{0,1},{1,0},{2,3},{3,2},{4,5},{5,4},{6,7},{7,6},{8,9},{9,8},{10,11... | collective-permute-start | bytes 3145736 | tf_op jit(solution)/shard_map/ppermute | solution.py:20
  194.4 11.0 %copy-start.6 = (bf16[256,1,512]{2,0,1:T(8,128)(2,1)S(1)}, bf16[256,1,512]{2,0,1:T(8,128)(2,1)}, u32[]{:S(2)}) copy-start(bf16[256,1,512]{2,0,1:T(8,128)(2,1)} %copy-done.5) | copy-start | bytes 786436
  194.4 11.0 %copy-start.8 = (bf16[256,1,512]{2,0,1:T(8,128)(2,1)S(1)}, bf16[256,1,512]{2,0,1:T(8,128)(2,1)}, u32[]{:S(2)}) copy-start(bf16[256,1,512]{2,0,1:T(8,128)(2,1)} %copy-done.7) | copy-start | bytes 786436
  194.4 11.0 %copy-start.31 = (bf16[256,1536]{0,1:T(8,128)(2,1)S(1)}, bf16[256,1536]{0,1:T(8,128)(2,1)}, u32[]{:S(2)}) copy-start(bf16[256,1536]{0,1:T(8,128)(2,1)} %copy.146) | copy-start | bytes 2359300
  194.4 11.0 %copy-start.32 = (bf16[256,1536]{0,1:T(8,128)(2,1)S(1)}, bf16[256,1536]{0,1:T(8,128)(2,1)}, u32[]{:S(2)}) copy-start(bf16[256,1536]{0,1:T(8,128)(2,1)} %copy.147) | copy-start | bytes 2359300
  199.3 12.0 %collective-permute-start.7 = (bf16[64,1536]{1,0:T(8,128)(2,1)S(1)}, bf16[64,1536]{1,0:T(8,128)(2,1)S(1)}, u32[]{:S(2)}, u32[]{:S(2)}) collective-permute-start(bf16[64,1536]{1,0:T(8,128)(2,1)S(1)} %get-tuple-element.32), channel_id=1, source_target_pairs={{0,8},{4,12},{8,16},{12,20},{16,24},{20,28},{1,9},{5,13},{9,17},{1... | collective-permute-start | bytes 589832 | tf_op jit(solution)/shard_map/ppermute | solution.py:458
  203.9 9.1 %copy-start.2 = (bf16[64,1536]{1,0:T(8,128)(2,1)S(1)}, bf16[64,1536]{1,0:T(8,128)(2,1)}, u32[]{:S(2)}) copy-start(bf16[64,1536]{1,0:T(8,128)(2,1)} %param.9) | copy-start | bytes 589828
  203.9 9.5 %copy-start.22 = (bf16[256,512]{1,0:T(8,128)(2,1)S(1)}, bf16[256,512]{1,0:T(8,128)(2,1)}, u32[]{:S(2)}) copy-start(bf16[256,512]{1,0:T(8,128)(2,1)} %copy-done.21) | copy-start | bytes 786436
  203.9 9.5 %copy-start.24 = (bf16[256,512]{1,0:T(8,128)(2,1)S(1)}, bf16[256,512]{1,0:T(8,128)(2,1)}, u32[]{:S(2)}) copy-start(bf16[256,512]{1,0:T(8,128)(2,1)} %copy-done.23) | copy-start | bytes 786436
  203.9 9.5 %copy-start.27 = (bf16[256,512]{1,0:T(8,128)(2,1)S(1)}, bf16[256,512]{1,0:T(8,128)(2,1)}, u32[]{:S(2)}) copy-start(bf16[256,512]{1,0:T(8,128)(2,1)} %copy-done.25) | copy-start | bytes 786436
  203.9 9.5 %copy-start.30 = (bf16[256,512]{1,0:T(8,128)(2,1)S(1)}, bf16[256,512]{1,0:T(8,128)(2,1)}, u32[]{:S(2)}) copy-start(bf16[256,512]{1,0:T(8,128)(2,1)} %copy-done.28) | copy-start | bytes 786436
  203.9 9.0 %collective-permute-start.10 = (bf16[64,1536]{1,0:T(8,128)(2,1)S(1)}, bf16[64,1536]{1,0:T(8,128)(2,1)S(1)}, u32[]{:S(2)}, u32[]{:S(2)}) collective-permute-start(bf16[64,1536]{1,0:T(8,128)(2,1)S(1)} %get-tuple-element.33), channel_id=1, source_target_pairs={{8,0},{12,4},{16,8},{20,12},{24,16},{28,20},{9,1},{13,5},{17,9},{2... | collective-permute-start | bytes 589832 | tf_op jit(solution)/shard_map/ppermute | solution.py:458
  213.3 7.6 %collective-permute-start.11 = (f32[2,64]{1,0:T(2,128)S(1)}, f32[2,64]{1,0:T(2,128)S(1)}, u32[]{:S(2)}, u32[]{:S(2)}) collective-permute-start(f32[2,64]{1,0:T(2,128)S(1)} %pad_maximum_fusion.16), channel_id=1, source_target_pairs={{0,1},{1,0},{2,3},{3,2},{4,5},{5,4},{6,7},{7,6},{8,9},{9,8},{10,11... | collective-permute-start | bytes 1544 | tf_op jit(solution)/shard_map/ppermute | solution.py:20
  221.0 11.6 %collective-permute-start.12 = (f32[2,64]{1,0:T(2,128)S(1)}, f32[2,64]{1,0:T(2,128)S(1)}, u32[]{:S(2)}, u32[]{:S(2)}) collective-permute-start(f32[2,64]{1,0:T(2,128)S(1)} %fusion.117), channel_id=1, source_target_pairs={{0,2},{1,3},{2,0},{3,1},{4,6},{5,7},{6,4},{7,5},{8,10},{9,11},{10,... | collective-permute-start | bytes 1544 | tf_op jit(solution)/shard_map/ppermute | solution.py:20
  (22 other events, 113.7 us)

commit v3 on v2

--- a/solution.py
+++ b/solution.py
@@ -44,11 +44,6 @@
         - jnp.mean(scaled, axis=-1, keepdims=True)
         - unit_rows * jnp.mean(scaled * unit_rows, axis=-1, keepdims=True)
     )
-
-
-def gelu_pair(pre_act, upstream):
-    hidden, pullback = jax.vjp(jax.nn.gelu, pre_act)
-    return (hidden.astype(jnp.bfloat16), pullback(upstream)[0].astype(jnp.bfloat16))
 
 
 def attention_pair(qkv_rows, att_grad, query_gain, key_gain):
@@ -116,14 +111,20 @@
     return sums
 
 
-def halves(values, core):
-    half = values.shape[0] // 2
-    own = lax.dynamic_slice_in_dim(values, core * half, half, axis=0)
-    other = lax.dynamic_slice_in_dim(values, (1 - core) * half, half, axis=0)
-    return (own, other)
-
-
 MESH = pl.DeviceIdType.MESH
+GELU_SLOPE = math.sqrt(2.0 / math.pi)
+GELU_CUBE = 0.044715
+
+
+def gelu_both(pre_act, upstream):
+    square = pre_act * pre_act
+    bend = jnp.tanh(GELU_SLOPE * pre_act * (1.0 + GELU_CUBE * square))
+    lift = 0.5 * (1.0 + bend)
+    slope = GELU_SLOPE * (1.0 + 3.0 * GELU_CUBE * square)
+    derivative = lift + 0.5 * pre_act * (1.0 - bend * bend) * slope
+    return (pre_act * lift, derivative * upstream)
+
+
 CHUNK = 512
 
 
@@ -137,6 +138,10 @@
     up_ref,
     cot_all,
     normed_all,
+    att_out,
+    qkv_out,
+    hidden_all,
+    pre_all,
     total,
     out_w,
     down_w,
@@ -155,14 +160,18 @@
     core_in_sem,
     x_out_sem,
     x_in_sem,
+    hand_out_sem,
+    hand_in_sem,
 ):
-    depth, out_n, down_n, up_n, width = sizes
+    depth, out_n, down_n, up_n, width, stages = sizes
     hid, wid = lax.axis_index("hid"), lax.axis_index("wid")
     z, y = hid // 2, hid % 2
     core = wid % 2
     above, below, pair = hid + 2, hid - 2, z * 2 + 1 - y
     core_peer = wid + 1 - 2 * core
-    x_peer = wid + 2 - 4 * ((wid // 2) % 2)
+    x_peers = [
+        wid + bit - 2 * bit * ((wid // bit) % 2) for bit in (2 << at for at in range(stages))
+    ]
 
     loads = [
         pltpu.make_async_copy(src, dst, load_sem.at[at])
@@ -180,7 +189,8 @@
     barrier = pltpu.get_barrier_semaphore()
     pl.semaphore_signal(barrier, inc=1, device_id={"hid": pair}, device_id_type=MESH)
     pl.semaphore_signal(barrier, inc=1, device_id={"wid": core_peer}, device_id_type=MESH)
-    pl.semaphore_signal(barrier, inc=1, device_id={"wid": x_peer}, device_id_type=MESH)
+    for peer in x_peers:
+        pl.semaphore_signal(barrier, inc=1, device_id={"wid": peer}, device_id_type=MESH)
 
     @pl.when(z < depth - 1)
     def _():
@@ -190,7 +200,7 @@
     def _():
         pl.semaphore_signal(barrier, inc=1, device_id={"hid": below}, device_id_type=MESH)
 
-    neighbours = 3 + jnp.where(z > 0, 1, 0) + jnp.where(z < depth - 1, 1, 0)
+    neighbours = 2 + stages + jnp.where(z > 0, 1, 0) + jnp.where(z < depth - 1, 1, 0)
     pl.semaphore_wait(barrier, neighbours)
 
     def block_copy(kind, level, side, sems, target):
@@ -261,13 +271,13 @@
             device_id_type=MESH,
         )
 
-    def x_copy(at):
+    def x_copy(at, stage=0):
         return pltpu.make_async_remote_copy(
-            src_ref=x_send.at[at],
-            dst_ref=x_recv.at[at],
-            send_sem=x_out_sem.at[at],
-            recv_sem=x_in_sem.at[at],
-            device_id={"wid": x_peer},
+            src_ref=x_send.at[stage, at],
+            dst_ref=x_recv.at[stage, at],
+            send_sem=x_out_sem.at[stage, at],
+            recv_sem=x_in_sem.at[stage, at],
+            device_id={"wid": x_peers[stage]},
             device_id_type=MESH,
         )
 
@@ -275,7 +285,7 @@
         core_copy(at).wait_recv()
         subtotal = total[at] + core_recv[at].astype(jnp.float32)
         total[at] = subtotal
-        x_send[at] = subtotal.astype(jnp.bfloat16)
+        x_send[0, at] = subtotal.astype(jnp.bfloat16)
         x_copy(at).start()
 
     def place(image, at, part):
@@ -319,11 +329,12 @@
         def _(at):
             place(image, out_n + at, turned(rows_of(0, image), down_w[span(at), :]))
 
-    def normed_products(image):
+    def qkv_products(image):
         @pl.loop(0, 3)
         def _(at):
             place(image, first_qkv + at, straight(rows_of(1, image), qkv_w[at]))
 
+    def up_products(image):
         @pl.loop(0, up_n)
         def _(at):
             place(image, first_up + at, straight(rows_of(1, image), up_w[:, span(at)]))
@@ -331,6 +342,21 @@
         @pl.when(image == core)
         def _():
             combine(first_up + up_n - 1)
+
+    def hand_copy(kind, at, image):
+        block = ((hidden_all, pre_all)[kind]).at[image_rows(image), span(at)]
+        return pltpu.make_async_remote_copy(
+            src_ref=block,
+            dst_ref=block,
+            send_sem=hand_out_sem.at[kind, at],
+            recv_sem=hand_in_sem.at[kind, at],
+            device_id={"wid": core_peer},
+            device_id_type=MESH,
+        )
+
+    def image_rows(image):
+        half = total.shape[1]
+        return pl.ds(pl.multiple_of(image * half, half), half)
 
     begin(0)
     begin(1)
@@ -350,24 +376,62 @@
     pair_arrived(1, near)
     for load in loads[2:]:
         load.wait()
-    normed_products(near)
+    qkv_products(near)
     for step in late[len(late) // 2 :]:
         relay(0, step)
         relay(1, step)
+    up_products(near)
     pair_arrived(0, far)
     cot_products(far)
     pair_arrived(1, far)
-    normed_products(far)
-
-    @pl.loop(0, first_up + up_n)
+    qkv_products(far)
+    up_products(far)
+
+    def arrived(at, stage):
+        x_copy(at, stage).wait_recv()
+        return total[at] + x_recv[stage, at].astype(jnp.float32)
+
+    for stage in range(stages - 1):
+
+        @pl.loop(0, first_up + up_n)
+        def _(at):
+            subtotal = arrived(at, stage)
+            total[at] = subtotal
+            x_send[stage + 1, at] = subtotal.astype(jnp.bfloat16)
+            x_copy(at, stage + 1).start()
+
+    last = stages - 1
+    for at in range(out_n):
+        att_out[:, at * width : (at + 1) * width] = arrived(at, last).astype(jnp.bfloat16)
+
+    @pl.loop(0, down_n)
     def _(at):
-        x_copy(at).wait_recv()
-        total[at] = total[at] + x_recv[at].astype(jnp.float32)
+        total[out_n + at] = arrived(out_n + at, last)
+
+    @pl.loop(0, 3)
+    def _(at):
+        qkv_out[at] = arrived(first_qkv + at, last)
+
+    @pl.loop(0, up_n)
+    def _(at):
+        hidden, pre_grad = gelu_both(arrived(first_up + at, last), total[out_n + at])
+        hidden_all[image_rows(core), span(at)] = hidden.astype(jnp.bfloat16)
+        pre_all[image_rows(core), span(at)] = pre_grad.astype(jnp.bfloat16)
+        hand_copy(1, at, core).start()
+        hand_copy(0, at, core).start()
+
+    @pl.loop(0, up_n)
+    def _(at):
+        hand_copy(1, at, 1 - core).wait_recv()
+        hand_copy(0, at, 1 - core).wait_recv()
+        hand_copy(1, at, core).wait_send()
+        hand_copy(0, at, core).wait_send()
 
     @pl.loop(0, first_up + up_n)
     def _(at):
         core_copy(at).wait_send()
-        x_copy(at).wait_send()
+        for stage in range(stages):
+            x_copy(at, stage).wait_send()
 
     for kind in range(2):
         for level in range(depth):
@@ -395,6 +459,7 @@
     assert qkv_weight.shape[2] == width
     count = out_n + down_n + 3 + up_n
     half = rows * depth
+    stages = lax.axis_size("wid").bit_length() - 2
     vmem = pl.BlockSpec(memory_space=pltpu.VMEM)
     hbm = pl.BlockSpec(memory_space=pl.ANY)
     all_shape = jax.ShapeDtypeStruct((blocks, rows, columns), jnp.bfloat16)
@@ -402,16 +467,21 @@
     slots = pltpu.VMEM((count, half, width), jnp.bfloat16)
     macs = 2 * half * columns * width * count
     return pl.pallas_call(
-        functools.partial(forward_kernel, (depth, out_n, down_n, up_n, width)),
+        functools.partial(forward_kernel, (depth, out_n, down_n, up_n, width, stages)),
         out_shape=(
             all_shape,
             all_shape,
-            jax.ShapeDtypeStruct((count, half, width), jnp.float32),
+            jax.ShapeDtypeStruct((half, out_weight.shape[0]), jnp.bfloat16),
+            jax.ShapeDtypeStruct((3, half, width), jnp.float32),
+            jax.ShapeDtypeStruct((2 * half, up_weight.shape[1]), jnp.bfloat16),
+            jax.ShapeDtypeStruct((2 * half, up_weight.shape[1]), jnp.bfloat16),
         ),
         in_specs=[vmem, vmem, hbm, hbm, hbm, hbm],
-        out_specs=(vmem, vmem, vmem),
-        scratch_shapes=[pltpu.VMEM(weight.shape, weight.dtype) for weight in weights]
-        + [slots] * 4
+        out_specs=(vmem,) * 6,
+        scratch_shapes=[pltpu.VMEM((count, half, width), jnp.float32)]
+        + [pltpu.VMEM(weight.shape, weight.dtype) for weight in weights]
+        + [slots] * 2
+        + [pltpu.VMEM((stages, count, half, width), jnp.bfloat16)] * 2
         + [
             pltpu.SemaphoreType.DMA((4,)),
             pltpu.SemaphoreType.DMA((2, blocks)),
@@ -420,8 +490,10 @@
             pltpu.SemaphoreType.DMA((2, depth)),
             pltpu.SemaphoreType.DMA((count,)),
             pltpu.SemaphoreType.DMA((count,)),
-            pltpu.SemaphoreType.DMA((count,)),
-            pltpu.SemaphoreType.DMA((count,)),
+            pltpu.SemaphoreType.DMA((stages, count)),
+            pltpu.SemaphoreType.DMA((stages, count)),
+            pltpu.SemaphoreType.DMA((2, up_n)),
+            pltpu.SemaphoreType.DMA((2, up_n)),
         ],
         compiler_params=pltpu.CompilerParams(
             collective_id=0, has_side_effects=True, vmem_limit_bytes=56 * 1024 * 1024
@@ -433,35 +505,71 @@
     )(cotangent, normed, *weights)
 
 
-def scatter_sum(partial):
+def scatter_sums(first, second, works):
     size = lax.axis_size("hid")
     depth = size // 2
     index = lax.axis_index("hid")
     z, y = index // 2, index % 2
-    blocks = partial.reshape(depth, 2, partial.shape[0] // size, partial.shape[1])
-    mine = lax.dynamic_index_in_dim(blocks, y, axis=1, keepdims=False)
-    given = lax.dynamic_index_in_dim(blocks, 1 - y, axis=1, keepdims=False)
-    mine = mine + swapped(given.astype(jnp.bfloat16), "hid", 1).astype(jnp.float32)
-
-    def share(level):
-        return lax.dynamic_index_in_dim(mine, level, axis=0, keepdims=False)
-
-    result = share(z)
-    for way in (1, -1):
-        pairs = [
-            (at, at + 2 * way) for at in range(size) if 0 <= at + 2 * way < size
-        ]
-        flow = None
-        for far in range(depth - 1, 0, -1):
-            part = share(jnp.clip(z + way * far, 0, depth - 1))
-            flow = part if flow is None else flow + part
-            flow = lax.ppermute(flow.astype(jnp.bfloat16), "hid", pairs).astype(jnp.float32)
-        result = result + flow
-    return result
-
-
-def both_halves(own):
-    return jnp.concatenate([own, swapped(own, "wid", 1)], axis=0)
+    ways = (1, -1)
+
+    def split(partial):
+        return partial.reshape(depth, 2, partial.shape[0] // size, partial.shape[1])
+
+    def along(value, at, axis):
+        return lax.dynamic_index_in_dim(value, at, axis=axis, keepdims=False)
+
+    def shifted(flow, way):
+        pairs = [(at, at + 2 * way) for at in range(size) if 0 <= at + 2 * way < size]
+        return lax.ppermute(flow.astype(jnp.bfloat16), "hid", pairs)
+
+    def swap_of(blocks, axis):
+        return swapped(along(blocks, 1 - y, axis).astype(jnp.bfloat16), "hid", 1)
+
+    def chain_step(blocks, flows, far):
+        parts = [along(blocks, jnp.clip(z + way * far, 0, depth - 1), 0) for way in ways]
+        if flows is not None:
+            parts = [part + flow.astype(jnp.float32) for part, flow in zip(parts, flows)]
+        return [shifted(part, way) for part, way in zip(parts, ways)]
+
+    def chain_end(blocks, flows):
+        up, down = (flow.astype(jnp.float32) for flow in flows)
+        return along(blocks, z, 0) + up + down
+
+    first, second = split(first), split(second)
+    done = []
+    first_flows, second_flows = None, None
+    for turn in range(depth):
+        if turn == 0:
+            first_got = [swap_of(first, 1)]
+        else:
+            first_flows = first_got = chain_step(first, first_flows, depth - turn)
+        if turn < depth - 1:
+            second_flows = second_got = chain_step(second, second_flows, depth - 1 - turn)
+        else:
+            second = chain_end(second, second_flows)
+            second_got = [swap_of(second, 0)]
+        if turn < len(works):
+            first_got, second_got, work = lax.optimization_barrier(
+                (first_got, second_got, works[turn]())
+            )
+            done.append(work)
+        if turn == 0:
+            first = along(first, y, 1) + first_got[0].astype(jnp.float32)
+        else:
+            first_flows = first_got
+        if turn < depth - 1:
+            second_flows = second_got
+        else:
+            second = along(second, y, 0) + second_got[0].astype(jnp.float32)
+    first = chain_end(first, first_flows)
+    return (jnp.concatenate([first, second], axis=1), done)
+
+
+def both_halves(own, core):
+    other = swapped(own, "wid", 1)
+    return jnp.concatenate(
+        [jnp.where(core == 0, own, other), jnp.where(core == 0, other, own)], axis=0
+    )
 
 
 def local(
@@ -481,7 +589,7 @@
     inverse = inverse[:, None]
     unit_rows = (input_rows - centre[:, None]) * inverse
     normed = (unit_rows * norm_gain).astype(jnp.bfloat16)
-    grad_all, normed_all, total = forward_products(
+    grad_all, normed_all, att_grad, qkv_rows, hidden, pre_grad = forward_products(
         cotangent,
         normed,
         out_weight,
@@ -489,38 +597,30 @@
         jnp.transpose(qkv_weight, (1, 0, 2)),
         up_weight,
     )
-    for bit in axis_bits("wid")[2:]:
-        total = total + swapped(total.astype(jnp.bfloat16), "wid", bit).astype(jnp.float32)
     grad_all = grad_all.reshape(-1, grad_all.shape[2])
     normed_all = normed_all.reshape(-1, normed_all.shape[2])
-    grad_order = jnp.concatenate(halves(grad_all, core), axis=0)
-    normed_order = jnp.concatenate(halves(normed_all, core), axis=0)
-    out_n = out_weight.shape[0] // total.shape[2]
-    down_n = down_weight.shape[0] // total.shape[2]
-
-    def side_by_side(pieces):
-        return jnp.concatenate(list(pieces), axis=1)
-
-    att_grad = side_by_side(total[:out_n]).astype(jnp.bfloat16)
-    qkv_rows = jnp.transpose(total[out_n + down_n : out_n + down_n + 3], (1, 0, 2))
-    hidden, pre_grad = [], []
-    for at in range(down_n):
-        hidden_own, pre_own = gelu_pair(total[out_n + down_n + 3 + at], total[out_n + at])
-        hidden.append(hidden_own)
-        pre_grad.append(pre_own)
-    pre_grad = both_halves(side_by_side(pre_grad))
-    attended, qkv_back = attention_pair(qkv_rows, att_grad, query_gain, key_gain)
-    qkv_back = both_halves(qkv_back)
-    hidden = both_halves(side_by_side(hidden))
-    attended = both_halves(attended)
-    normed_grad = product("tf,df->td", pre_grad, up_weight) + product(
-        "tch,dch->td", qkv_back, qkv_weight
-    )
-    normed_grad = scatter_sum(jnp.concatenate(halves(normed_grad, core), axis=0))
-    qkv_grad = product("td,tch->dch", normed_order, qkv_back).astype(jnp.bfloat16)
-    out_grad = product("th,td->hd", attended, grad_order).astype(jnp.bfloat16)
-    up_grad = product("td,tf->df", normed_order, pre_grad).astype(jnp.bfloat16)
-    down_grad = product("tf,td->fd", hidden, grad_order).astype(jnp.bfloat16)
+    attended, qkv_back = attention_pair(
+        jnp.transpose(qkv_rows, (1, 0, 2)), att_grad, query_gain, key_gain
+    )
+    qkv_back = both_halves(qkv_back, core)
+    attended = both_halves(attended, core)
+
+    def normed_part(span):
+        return product("tf,df->td", pre_grad, up_weight[span]) + product(
+            "tch,dch->td", qkv_back, qkv_weight[span]
+        )
+
+    middle = up_weight.shape[0] // 2
+    normed_grad, (up_grad, down_grad, qkv_grad, out_grad) = scatter_sums(
+        normed_part(slice(None, middle)),
+        normed_part(slice(middle, None)),
+        (
+            lambda: product("td,tf->df", normed_all, pre_grad).astype(jnp.bfloat16),
+            lambda: product("tf,td->fd", hidden, grad_all).astype(jnp.bfloat16),
+            lambda: product("td,tch->dch", normed_all, qkv_back).astype(jnp.bfloat16),
+            lambda: product("th,td->hd", attended, grad_all).astype(jnp.bfloat16),
+        ),
+    )
     unit_grad = normed_grad * norm_gain
     grad_total, grad_project = row_totals(
         jnp.stack([jnp.sum(unit_grad, axis=-1), jnp.sum(unit_grad * unit_rows, axis=-1)])

time: 234 us -> 224 us (0.957)
  Pallas kernels: 77.9 us -> 97.1 us
  waiting for transfers between devices: 32.6 us -> 20.7 us
  other arithmetic: 18.7 us -> 9.46 us
  local copies, waits for them, and re-layouts: 13.3 us -> 6.74 us
  matrix products: 51.2 us -> 45.2 us
  starting transfers between devices: 38.3 us -> 43 us
    ppermute x6 -> x12, starting transfers between devices: 16.5 us -> 37.1 us  [shifted(): return lax.ppermute(flow.astype(jnp.bfloat16), 'hid', pairs)]
    pallas_call x1, Pallas kernels: 77.9 us -> 97.1 us  [forward_products(): pl.pallas_call(functools.partial(forward_kernel, (depth, out_n, down_n, u...]
    ppermute x9 -> x8, starting transfers between devices: 21.8 us -> 5.85 us  [swapped(): return lax.ppermute(value, axis, [(at, at ^ bit) for at in range(size)])]
    ppermute x9 -> x8, waiting for transfers between devices: 19.3 us -> 6.98 us  [swapped(): return lax.ppermute(value, axis, [(at, at ^ bit) for at in range(size)])]
    convert_element_type x3 -> x4, other arithmetic: 6.48 us -> 0.26 us  [shifted(): return lax.ppermute(flow.astype(jnp.bfloat16), 'hid', pairs)]
    dot_general x12 -> x14, matrix products: 49.7 us -> 43.8 us  [product(): jnp.einsum(form, left_arr, right_arr, preferred_element_type=jnp.float32)]
    unnamed x80 -> x36, local copies, waits for them, and re-layouts: 4.68 us -> 1.02 us
    ppermute x6 -> x12, waiting for transfers between devices: 13.4 us -> 13.7 us  [shifted(): return lax.ppermute(flow.astype(jnp.bfloat16), 'hid', pairs)]
  transfers between devices with their start and end apart: 15 -> 20, of which waited for: 6 -> 10; matrix products, arithmetic and copies ran while one was open for 20% -> 12% of each run, Pallas kernels for 0% -> 0%
where the time goes in v3:
time: 224 us; the launch traced here: 223 us
  Pallas kernels  97.1 us (43%)
  matrix products  45.2 us (20%)
  starting transfers between devices  43 us (19%)
  waiting for transfers between devices  20.7 us (9%)
  other arithmetic  9.46 us (4%)
  local copies, waits for them, and re-layouts  6.74 us (3%)
    pallas_call x1, Pallas kernels, forward_products(): pl.pallas_call(functools.partial(forward_kernel, (depth, out_n, down_n, u...  97.1 us
    dot_general x14, matrix products, product(): jnp.einsum(form, left_arr, right_arr, preferred_element_type=jnp.float32)  43.8 us
    ppermute x12, starting transfers between devices, shifted(): return lax.ppermute(flow.astype(jnp.bfloat16), 'hid', pairs)  37.1 us
    ppermute x12, waiting for transfers between devices, shifted(): return lax.ppermute(flow.astype(jnp.bfloat16), 'hid', pairs)  13.7 us
    ppermute x8, waiting for transfers between devices, swapped(): return lax.ppermute(value, axis, [(at, at ^ bit) for at in range(size)])  6.98 us
    ppermute x8, starting transfers between devices, swapped(): return lax.ppermute(value, axis, [(at, at ^ bit) for at in range(size)])  5.85 us
  transfers between devices with their start and end apart: 20, of which 10 were waited for; matrix products, arithmetic and copies ran while one was open for 12% of the time, Pallas kernels for 0%

profile of v3, /device:TPU:0, one launch (start us, length us, event | category | flops | bytes accessed | tf_op | source)
XLA Modules:
  0.0 223.5 jit_solution(3609844727222388647)
XLA Ops:
  4.2 2.9 %collective-permute-start.1 = (f32[2,64]{1,0:T(2,128)S(1)}, f32[2,64]{1,0:T(2,128)S(1)}, u32[]{:S(2)}, u32[]{:S(2)}) collective-permute-start(f32[2,64]{1,0:T(2,128)S(1)} %pad_maximum_fusion.6), channel_id=1, source_target_pairs={{0,2},{1,3},{2,0},{3,1},{4,6},{5,7},{6,4},{7,5},{8,10},{9,11},{10,... | collective-permute-start | bytes 1544 | tf_op jit(solution)/shard_map/ppermute | solution.py:20
  7.1 1.5 collective-permute-done.1
  8.7 1.7 fusion.39.normed_ref
  10.4 97.1 %forward_products.1 = (bf16[8,64,1536]{2,1,0:T(8,128)(2,1)}, bf16[8,64,1536]{2,1,0:T(8,128)(2,1)}, bf16[256,512]{1,0:T(8,128)(2,1)}, f32[3,256,512]{2,1,0:T(8,12...) custom-call(bf16[64,1536]{1,0:T(8,128)(2,1)} %cot_ref.1, bf16[64,1536]{1,0:T(8,128)(2,1)} %fusion.39.normed_ref, ...), custom_call_target="tpu_custom_call" | custom-call | flops 9663676416 | bytes 33554432 | tf_op jit(solution)/shard_map/forward_products/pallas_call | solution.py:469
  114.3 1.4 fusion.30
  118.0 2.9 %fusion.84 = (f32[256,4]{0,1:T(4,128)S(1)}, f32[256,4]{0,1:T(4,128)S(1)}, f32[1,256,4,128]{1,3,2,0:T(8,128)}) fusion(f32[256,4]{0,1:T(4,128)S(1)} %add_rsqrt_fusion.1, f32[1,256,4,128]{1,3,2,0:T(8,128)S(1)} %bitcast.191, f32[256,4]{0,1:T(4,128)S(1)} %broadcast_multiply_fusion.5, f32[128]{0:T(128)S(1)} %copy-done.8, bf16[256,4,128]{0,2,1:T(8,128)(2,1)} %copy-done.2, ...), kind=kOutput, calls=%fused_computation.150 | convolution fusion | flops 69205248 | bytes 3424768 | tf_op jit(solution)/shard_map/ihpq,iqha->ipha/dot_general | solution.py:29
  120.9 2.8 %fusion.85 = (f32[256,4]{0,1:T(4,128)S(1)}, f32[256,4]{0,1:T(4,128)S(1)}, f32[1,256,4,128]{1,3,2,0:T(8,128)}) fusion(f32[256,4]{0,1:T(4,128)S(1)} %add_rsqrt_fusion, f32[1,256,4,128]{1,3,2,0:T(8,128)S(1)} %bitcast.189, f32[256,4]{0,1:T(4,128)S(1)} %broadcast_multiply_fusion.4, f32[128]{0:T(128)S(1)} %copy-done.9, bf16[256,4,128]{0,2,1:T(8,128)(2,1)} %copy-done.3, ...), kind=kOutput, calls=%fused_computation.151 | convolution fusion | flops 69205248 | bytes 3424768 | tf_op jit(solution)/shard_map/ihpq,ipha->iqha/dot_general | solution.py:29
  123.8 5.6 %fusion.1 = f32[512,768]{1,0:T(8,128)} fusion(bf16[512,2048]{1,0:T(8,128)(2,1)} %get-tuple-element.29, bf16[1536,2048]{1,0:T(8,128)(2,1)} %up_ref.1), kind=kOutput, calls=%fused_computation.4 | convolution fusion | flops 1610612736 | bytes 6815744 | tf_op jit(solution)/shard_map/tf,df->td/dot_general | solution.py:29
  129.4 5.0 %fusion.3 = f32[512,768]{1,0:T(8,128)} fusion(bf16[512,2048]{1,0:T(8,128)(2,1)S(1)} %copy-done.12, bf16[1536,2048]{1,0:T(8,128)(2,1)} %up_ref.1), kind=kOutput, calls=%fused_computation.6 | convolution fusion | flops 1610612736 | bytes 6815744 | tf_op jit(solution)/shard_map/tf,df->td/dot_general | solution.py:29
  137.3 8.5 %convolution_convert_fusion.1 = bf16[1536,2048]{1,0:T(8,128)(2,1)} fusion(bf16[512,1536]{1,0:T(8,128)(2,1)} %bitcast.220, bf16[512,2048]{1,0:T(8,128)(2,1)} %get-tuple-element.29), kind=kOutput, calls=%fused_computation.2 | convolution fusion | flops 3224371200 | bytes 9961472 | tf_op jit(solution)/shard_map/td,tf->df/dot_general | solution.py:29
  145.8 1.4 broadcast_select_fusion.1
  147.5 3.4 %bitcast_add_fusion = f32[512,768]{1,0:T(8,128)S(1)} fusion(f32[512,768]{1,0:T(8,128)S(1)} %copy-done.14, bf16[1536,3,512]{2,0,1:T(8,128)(2,1)} %param.12, bf16[256,3,512]{2,0,1:T(8,128)(2,1)S(1)} %get-tuple-element.66, bf16[256,3,512]{2,0,1:T(8,128)(2,1)S(1)} %get-tuple-element.65), kind=kOutput, calls=%fused_computation.14 | convolution fusion | flops 1211498496 | bytes 7077888 | tf_op jit(solution)/shard_map/tch,dch->td/dot_general | solution.py:29
  150.9 3.5 %collective-permute-start.4 = (bf16[2,64,768]{2,1,0:T(8,128)(2,1)S(1)}, bf16[2,64,768]{2,1,0:T(8,128)(2,1)S(1)}, u32[]{:S(2)}, u32[]{:S(2)}) collective-permute-start(bf16[2,64,768]{2,1,0:T(8,128)(2,1)S(1)} %get-tuple-element.64), channel_id=1, source_target_pairs={{0,8},{4,12},{8,16},{12,20},{16,24},{20,28},{1,9},{5,13},{9,17},{1... | collective-permute-start | bytes 589832 | tf_op jit(solution)/shard_map/ppermute | solution.py:523
  154.4 1.6 collective-permute-start.5
  156.0 1.4 bitcast_add_fusion.1
  158.1 5.3 %convolution_convert_fusion = bf16[2048,1536]{1,0:T(8,128)(2,1)} fusion(bf16[512,2048]{1,0:T(8,128)(2,1)S(1)} %copy-done.15, bf16[512,1536]{1,0:T(8,128)(2,1)S(1)} %bitcast.218), kind=kOutput, calls=%fused_computation.1 | convolution fusion | flops 3224371200 | bytes 9961472 | tf_op jit(solution)/shard_map/tf,td->fd/dot_general | solution.py:29
  163.5 4.6 %collective-permute-done.5 = bf16[2,64,768]{2,1,0:T(8,128)(2,1)S(1)} collective-permute-done((bf16[2,64,768]{2,1,0:T(8,128)(2,1)S(1)}, bf16[2,64,768]{2,1,0:T(8,128)(2,1)S(1)}, u32[]{:S(2)}, u32[]{:S(2)}) %collective-permute-start.5) | collective-permute-done | bytes 196640 | tf_op jit(solution)/shard_map/ppermute | solution.py:523
  168.5 9.1 %collective-permute-start.8 = (bf16[2,64,768]{2,1,0:T(8,128)(2,1)S(1)}, bf16[2,64,768]{2,1,0:T(8,128)(2,1)S(1)}, u32[]{:S(2)}, u32[]{:S(2)}) collective-permute-start(bf16[2,64,768]{2,1,0:T(8,128)(2,1)S(1)} %get-tuple-element.62), channel_id=1, source_target_pairs={{0,8},{4,12},{8,16},{12,20},{16,24},{20,28},{1,9},{5,13},{9,17},{1... | collective-permute-start | bytes 589832 | tf_op jit(solution)/shard_map/ppermute | solution.py:523
  177.7 1.3 collective-permute-start.9
  179.1 4.7 %collective-permute-start.6 = (bf16[64,768]{1,0:T(8,128)(2,1)S(1)}, bf16[64,768]{1,0:T(8,128)(2,1)S(1)}, u32[]{:S(2)}, u32[]{:S(2)}) collective-permute-start(bf16[64,768]{1,0:T(8,128)(2,1)S(1)} %get-tuple-element.74), channel_id=1, source_target_pairs={{0,8},{4,12},{8,16},{12,20},{16,24},{20,28},{1,9},{5,13},{9,17},{1... | collective-permute-start | bytes 294920 | tf_op jit(solution)/shard_map/ppermute | solution.py:523
  183.8 1.3 collective-permute-start.7
  186.0 4.3 %collective-permute-done.7 = bf16[64,768]{1,0:T(8,128)(2,1)S(1)} collective-permute-done((bf16[64,768]{1,0:T(8,128)(2,1)S(1)}, bf16[64,768]{1,0:T(8,128)(2,1)S(1)}, u32[]{:S(2)}, u32[]{:S(2)}) %collective-permute-start.7) | collective-permute-done | bytes 98336 | tf_op jit(solution)/shard_map/ppermute | solution.py:523
  190.4 3.6 %collective-permute-start.12 = (bf16[2,64,768]{2,1,0:T(8,128)(2,1)S(1)}, bf16[2,64,768]{2,1,0:T(8,128)(2,1)S(1)}, u32[]{:S(2)}, u32[]{:S(2)}) collective-permute-start(bf16[2,64,768]{2,1,0:T(8,128)(2,1)S(1)} %get-tuple-element.60), channel_id=1, source_target_pairs={{0,8},{4,12},{8,16},{12,20},{16,24},{20,28},{1,9},{5,13},{9,17},{1... | collective-permute-start | bytes 589832 | tf_op jit(solution)/shard_map/ppermute | solution.py:523
  194.0 1.3 collective-permute-start.13
  195.4 4.6 %collective-permute-start.10 = (bf16[64,768]{1,0:T(8,128)(2,1)S(1)}, bf16[64,768]{1,0:T(8,128)(2,1)S(1)}, u32[]{:S(2)}, u32[]{:S(2)}) collective-permute-start(bf16[64,768]{1,0:T(8,128)(2,1)S(1)} %get-tuple-element.72), channel_id=1, source_target_pairs={{0,8},{4,12},{8,16},{12,20},{16,24},{20,28},{1,9},{5,13},{9,17},{1... | collective-permute-start | bytes 294920 | tf_op jit(solution)/shard_map/ppermute | solution.py:523
  199.9 1.3 collective-permute-start.11
  201.2 4.3 %convolution_convert_fusion.2 = bf16[1536,3,512]{2,0,1:T(8,128)(2,1)} fusion(bf16[512,1536,1]{1,0,2:T(8,128)(2,1)S(1)} %bitcast.221, bf16[256,3,512]{2,0,1:T(8,128)(2,1)S(1)} %get-tuple-element.66, bf16[256,3,512]{2,0,1:T(8,128)(2,1)S(1)} %get-tuple-element.65), kind=kOutput, calls=%fused_computation.3 | convolution fusion | flops 2421424128 | bytes 7864320 | tf_op jit(solution)/shard_map/td,tch->dch/dot_general | solution.py:29
  207.2 3.7 %collective-permute-start.14 = (bf16[64,768]{1,0:T(8,128)(2,1)S(1)}, bf16[64,768]{1,0:T(8,128)(2,1)S(1)}, u32[]{:S(2)}, u32[]{:S(2)}) collective-permute-start(bf16[64,768]{1,0:T(8,128)(2,1)S(1)} %get-tuple-element.70), channel_id=1, source_target_pairs={{0,8},{4,12},{8,16},{12,20},{16,24},{20,28},{1,9},{5,13},{9,17},{1... | collective-permute-start | bytes 294920 | tf_op jit(solution)/shard_map/ppermute | solution.py:523
  210.9 1.3 collective-permute-start.15
  212.2 2.1 convolution_convert_fusion.3
  214.3 3.1 %collective-permute-done.15 = bf16[64,768]{1,0:T(8,128)(2,1)S(1)} collective-permute-done((bf16[64,768]{1,0:T(8,128)(2,1)S(1)}, bf16[64,768]{1,0:T(8,128)(2,1)S(1)}, u32[]{:S(2)}, u32[]{:S(2)}) %collective-permute-start.15) | collective-permute-done | bytes 98336 | tf_op jit(solution)/shard_map/ppermute | solution.py:523
  219.5 3.1 %collective-permute-done.19 = f32[2,64]{1,0:T(2,128)S(1)} collective-permute-done((f32[2,64]{1,0:T(2,128)S(1)}, f32[2,64]{1,0:T(2,128)S(1)}, u32[]{:S(2)}, u32[]{:S(2)}) %collective-permute-start.19) | collective-permute-done | bytes 544 | tf_op jit(solution)/shard_map/ppermute | solution.py:20
  (123 shorter events, 22.5 us)
Async XLA Ops:
  2.9 1.3 collective-permute-start
  4.2 4.4 %collective-permute-start.1 = (f32[2,64]{1,0:T(2,128)S(1)}, f32[2,64]{1,0:T(2,128)S(1)}, u32[]{:S(2)}, u32[]{:S(2)}) collective-permute-start(f32[2,64]{1,0:T(2,128)S(1)} %pad_maximum_fusion.6), channel_id=1, source_target_pairs={{0,2},{1,3},{2,0},{3,1},{4,6},{5,7},{6,4},{7,5},{8,10},{9,11},{10,... | collective-permute-start | bytes 1544 | tf_op jit(solution)/shard_map/ppermute | solution.py:20
  109.2 2.3 %copy-start.9 = (f32[128]{0:T(128)S(1)}, f32[128]{0:T(128)}, u32[]{:S(2)}) copy-start(f32[128]{0:T(128)} %param.17) | copy-start | bytes 1540
  111.0 2.1 copy-start.8
  123.8 5.6 %copy-start.12 = (bf16[512,2048]{1,0:T(8,128)(2,1)S(1)}, bf16[512,2048]{1,0:T(8,128)(2,1)}, u32[]{:S(2)}) copy-start(bf16[512,2048]{1,0:T(8,128)(2,1)} %get-tuple-element.29) | copy-start | bytes 6291460
  129.4 5.0 %copy-start.5 = (f32[1,256,4,128]{1,3,2,0:T(8,128)S(1)}, f32[1,256,4,128]{1,3,2,0:T(8,128)}, u32[]{:S(2)}) copy-start(f32[1,256,4,128]{1,3,2,0:T(8,128)} %get-tuple-element.86) | copy-start | bytes 1572868
  136.4 9.5 %collective-permute-start.2 = (bf16[256,3,512]{2,0,1:T(8,128)(2,1)S(1)}, bf16[256,3,512]{2,0,1:T(8,128)(2,1)}, u32[]{:S(2)}, u32[]{:S(2)}) collective-permute-start(bf16[256,3,512]{2,0,1:T(8,128)(2,1)S(1)} %pad_maximum_fusion.1), channel_id=1, source_target_pairs={{0,1},{1,0},{2,3},{3,2},{4,5},{5,4},{6,7},{7,6},{8,9},{9,8},{10,11... | collective-permute-start | bytes 2359304 | tf_op jit(solution)/shard_map/ppermute | solution.py:20
  136.9 48.2 %collective-permute-start.17 = (bf16[256,512]{0,1:T(8,128)(2,1)S(1)}, bf16[256,512]{0,1:T(8,128)(2,1)S(1)}, u32[]{:S(2)}, u32[]{:S(2)}) collective-permute-start(bf16[256,512]{0,1:T(8,128)(2,1)S(1)} %bitcast.207), channel_id=1, source_target_pairs={{0,1},{1,0},{2,3},{3,2},{4,5},{5,4},{6,7},{7,6},{8,9},{9,8},{10,11... | collective-permute-start | bytes 786440 | tf_op jit(solution)/shard_map/ppermute | solution.py:20
  145.8 10.2 %slice-start = ((s8[4718592]{0:T(1024)(128)(4,1)}), s8[4194304]{0:T(1024)(128)(4,1)S(1)}, s32[]{:S(2)}) async-start(s8[4718592]{0:T(1024)(128)(4,1)} %bitcast.216), calls=%async_computation | async-start | bytes 8388608
  147.5 8.5 %slice-start.1 = ((s8[4718592]{0:T(1024)(128)(4,1)}), s8[524288]{0:T(1024)(128)(4,1)S(1)}, s32[]{:S(2)}) async-start(s8[4718592]{0:T(1024)(128)(4,1)} %bitcast.216), calls=%async_computation.1 | async-start | bytes 1048576
  147.5 8.5 %copy-start.13 = (f32[512,768]{1,0:T(8,128)S(1)}, f32[512,768]{1,0:T(8,128)}, u32[]{:S(2)}) copy-start(f32[512,768]{1,0:T(8,128)} %fusion.3) | copy-start | bytes 4718596
  150.9 12.6 %collective-permute-start.4 = (bf16[2,64,768]{2,1,0:T(8,128)(2,1)S(1)}, bf16[2,64,768]{2,1,0:T(8,128)(2,1)S(1)}, u32[]{:S(2)}, u32[]{:S(2)}) collective-permute-start(bf16[2,64,768]{2,1,0:T(8,128)(2,1)S(1)} %get-tuple-element.64), channel_id=1, source_target_pairs={{0,8},{4,12},{8,16},{12,20},{16,24},{20,28},{1,9},{5,13},{9,17},{1... | collective-permute-start | bytes 589832 | tf_op jit(solution)/shard_map/ppermute | solution.py:523
  154.4 3.7 %copy-start.10 = (bf16[8,64,1536]{2,1,0:T(8,128)(2,1)S(1)}, bf16[8,64,1536]{2,1,0:T(8,128)(2,1)}, u32[]{:S(2)}) copy-start(bf16[8,64,1536]{2,1,0:T(8,128)(2,1)} %get-tuple-element.37) | copy-start | bytes 4718596
  154.4 3.7 %copy-start.15 = (bf16[512,2048]{1,0:T(8,128)(2,1)S(1)}, bf16[512,2048]{1,0:T(8,128)(2,1)}, u32[]{:S(2)}) copy-start(bf16[512,2048]{1,0:T(8,128)(2,1)} %get-tuple-element.36) | copy-start | bytes 6291460
  154.4 13.6 %collective-permute-start.5 = (bf16[2,64,768]{2,1,0:T(8,128)(2,1)S(1)}, bf16[2,64,768]{2,1,0:T(8,128)(2,1)S(1)}, u32[]{:S(2)}, u32[]{:S(2)}) collective-permute-start(bf16[2,64,768]{2,1,0:T(8,128)(2,1)S(1)} %get-tuple-element.63), channel_id=1, source_target_pairs={{8,0},{12,4},{16,8},{20,12},{24,16},{28,20},{9,1},{13,5},{17,9},{2... | collective-permute-start | bytes 589832 | tf_op jit(solution)/shard_map/ppermute | solution.py:523
  157.5 10.9 %collective-permute-start.3 = (bf16[4,64,768]{2,1,0:T(8,128)(2,1)S(1)}, bf16[4,64,768]{2,1,0:T(8,128)(2,1)S(1)}, u32[]{:S(2)}, u32[]{:S(2)}) collective-permute-start(bf16[4,64,768]{2,1,0:T(8,128)(2,1)S(1)} %fusion.44), channel_id=1, source_target_pairs={{0,4},{4,0},{8,12},{12,8},{16,20},{20,16},{24,28},{28,24},{1,5},{5... | collective-permute-start | bytes 1179656 | tf_op jit(solution)/shard_map/ppermute | solution.py:20
  168.5 21.7 %collective-permute-start.8 = (bf16[2,64,768]{2,1,0:T(8,128)(2,1)S(1)}, bf16[2,64,768]{2,1,0:T(8,128)(2,1)S(1)}, u32[]{:S(2)}, u32[]{:S(2)}) collective-permute-start(bf16[2,64,768]{2,1,0:T(8,128)(2,1)S(1)} %get-tuple-element.62), channel_id=1, source_target_pairs={{0,8},{4,12},{8,16},{12,20},{16,24},{20,28},{1,9},{5,13},{9,17},{1... | collective-permute-start | bytes 589832 | tf_op jit(solution)/shard_map/ppermute | solution.py:523
  177.7 12.6 %collective-permute-start.9 = (bf16[2,64,768]{2,1,0:T(8,128)(2,1)S(1)}, bf16[2,64,768]{2,1,0:T(8,128)(2,1)S(1)}, u32[]{:S(2)}, u32[]{:S(2)}) collective-permute-start(bf16[2,64,768]{2,1,0:T(8,128)(2,1)S(1)} %get-tuple-element.61), channel_id=1, source_target_pairs={{8,0},{12,4},{16,8},{20,12},{24,16},{28,20},{9,1},{13,5},{17,9},{2... | collective-permute-start | bytes 589832 | tf_op jit(solution)/shard_map/ppermute | solution.py:523
  179.0 22.2 %copy-start.11 = (bf16[8,64,1536]{2,1,0:T(8,128)(2,1)S(1)}, bf16[8,64,1536]{2,1,0:T(8,128)(2,1)}, u32[]{:S(2)}) copy-start(bf16[8,64,1536]{2,1,0:T(8,128)(2,1)} %get-tuple-element.32) | copy-start | bytes 4718596
  179.1 6.9 %collective-permute-start.6 = (bf16[64,768]{1,0:T(8,128)(2,1)S(1)}, bf16[64,768]{1,0:T(8,128)(2,1)S(1)}, u32[]{:S(2)}, u32[]{:S(2)}) collective-permute-start(bf16[64,768]{1,0:T(8,128)(2,1)S(1)} %get-tuple-element.74), channel_id=1, source_target_pairs={{0,8},{4,12},{8,16},{12,20},{16,24},{20,28},{1,9},{5,13},{9,17},{1... | collective-permute-start | bytes 294920 | tf_op jit(solution)/shard_map/ppermute | solution.py:523
  183.8 6.5 %collective-permute-start.7 = (bf16[64,768]{1,0:T(8,128)(2,1)S(1)}, bf16[64,768]{1,0:T(8,128)(2,1)S(1)}, u32[]{:S(2)}, u32[]{:S(2)}) collective-permute-start(bf16[64,768]{1,0:T(8,128)(2,1)S(1)} %get-tuple-element.73), channel_id=1, source_target_pairs={{8,0},{12,4},{16,8},{20,12},{24,16},{28,20},{9,1},{13,5},{17,9},{2... | collective-permute-start | bytes 294920 | tf_op jit(solution)/shard_map/ppermute | solution.py:523
  190.4 16.1 %collective-permute-start.12 = (bf16[2,64,768]{2,1,0:T(8,128)(2,1)S(1)}, bf16[2,64,768]{2,1,0:T(8,128)(2,1)S(1)}, u32[]{:S(2)}, u32[]{:S(2)}) collective-permute-start(bf16[2,64,768]{2,1,0:T(8,128)(2,1)S(1)} %get-tuple-element.60), channel_id=1, source_target_pairs={{0,8},{4,12},{8,16},{12,20},{16,24},{20,28},{1,9},{5,13},{9,17},{1... | collective-permute-start | bytes 589832 | tf_op jit(solution)/shard_map/ppermute | solution.py:523
  194.0 12.4 %collective-permute-start.13 = (bf16[2,64,768]{2,1,0:T(8,128)(2,1)S(1)}, bf16[2,64,768]{2,1,0:T(8,128)(2,1)S(1)}, u32[]{:S(2)}, u32[]{:S(2)}) collective-permute-start(bf16[2,64,768]{2,1,0:T(8,128)(2,1)S(1)} %get-tuple-element.59), channel_id=1, source_target_pairs={{8,0},{12,4},{16,8},{20,12},{24,16},{28,20},{9,1},{13,5},{17,9},{2... | collective-permute-start | bytes 589832 | tf_op jit(solution)/shard_map/ppermute | solution.py:523
  195.4 10.2 %collective-permute-start.10 = (bf16[64,768]{1,0:T(8,128)(2,1)S(1)}, bf16[64,768]{1,0:T(8,128)(2,1)S(1)}, u32[]{:S(2)}, u32[]{:S(2)}) collective-permute-start(bf16[64,768]{1,0:T(8,128)(2,1)S(1)} %get-tuple-element.72), channel_id=1, source_target_pairs={{0,8},{4,12},{8,16},{12,20},{16,24},{20,28},{1,9},{5,13},{9,17},{1... | collective-permute-start | bytes 294920 | tf_op jit(solution)/shard_map/ppermute | solution.py:523
  199.9 6.5 %collective-permute-start.11 = (bf16[64,768]{1,0:T(8,128)(2,1)S(1)}, bf16[64,768]{1,0:T(8,128)(2,1)S(1)}, u32[]{:S(2)}, u32[]{:S(2)}) collective-permute-start(bf16[64,768]{1,0:T(8,128)(2,1)S(1)} %get-tuple-element.71), channel_id=1, source_target_pairs={{8,0},{12,4},{16,8},{20,12},{24,16},{28,20},{9,1},{13,5},{17,9},{2... | collective-permute-start | bytes 294920 | tf_op jit(solution)/shard_map/ppermute | solution.py:523
  206.5 7.8 %collective-permute-start.16 = (bf16[64,768]{1,0:T(8,128)(2,1)S(1)}, bf16[64,768]{1,0:T(8,128)(2,1)S(1)}, u32[]{:S(2)}, u32[]{:S(2)}) collective-permute-start(bf16[64,768]{1,0:T(8,128)(2,1)S(1)} %fusion.62), channel_id=1, source_target_pairs={{0,4},{4,0},{8,12},{12,8},{16,20},{20,16},{24,28},{28,24},{1,5},{5... | collective-permute-start | bytes 294920 | tf_op jit(solution)/shard_map/ppermute | solution.py:20
  207.2 7.2 %collective-permute-start.14 = (bf16[64,768]{1,0:T(8,128)(2,1)S(1)}, bf16[64,768]{1,0:T(8,128)(2,1)S(1)}, u32[]{:S(2)}, u32[]{:S(2)}) collective-permute-start(bf16[64,768]{1,0:T(8,128)(2,1)S(1)} %get-tuple-element.70), channel_id=1, source_target_pairs={{0,8},{4,12},{8,16},{12,20},{16,24},{20,28},{1,9},{5,13},{9,17},{1... | collective-permute-start | bytes 294920 | tf_op jit(solution)/shard_map/ppermute | solution.py:523
  210.9 6.5 %collective-permute-start.15 = (bf16[64,768]{1,0:T(8,128)(2,1)S(1)}, bf16[64,768]{1,0:T(8,128)(2,1)S(1)}, u32[]{:S(2)}, u32[]{:S(2)}) collective-permute-start(bf16[64,768]{1,0:T(8,128)(2,1)S(1)} %get-tuple-element.69), channel_id=1, source_target_pairs={{8,0},{12,4},{16,8},{20,12},{24,16},{28,20},{9,1},{13,5},{17,9},{2... | collective-permute-start | bytes 294920 | tf_op jit(solution)/shard_map/ppermute | solution.py:523
  212.2 5.3 %copy-start = (bf16[64,1536]{1,0:T(8,128)(2,1)S(1)}, bf16[64,1536]{1,0:T(8,128)(2,1)}, u32[]{:S(2)}) copy-start(bf16[64,1536]{1,0:T(8,128)(2,1)} %param.9) | copy-start | bytes 589828
  212.2 5.3 %copy-start.7 = (f32[1536]{0:T(1024)S(1)}, f32[1536]{0:T(1024)}, u32[]{:S(2)}) copy-start(f32[1536]{0:T(1024)} %param.11) | copy-start | bytes 18436
  217.7 1.2 collective-permute-start.18
  218.9 3.6 %collective-permute-start.19 = (f32[2,64]{1,0:T(2,128)S(1)}, f32[2,64]{1,0:T(2,128)S(1)}, u32[]{:S(2)}, u32[]{:S(2)}) collective-permute-start(f32[2,64]{1,0:T(2,128)S(1)} %fusion.82), channel_id=1, source_target_pairs={{0,2},{1,3},{2,0},{3,1},{4,6},{5,7},{6,4},{7,5},{8,10},{9,11},{10,... | collective-permute-start | bytes 1544 | tf_op jit(solution)/shard_map/ppermute | solution.py:20
  (6 other events, 9.4 us)

commit v4 on v3

--- a/solution.py
+++ b/solution.py
@@ -102,13 +102,7 @@
         mean = 0.5 * (mean + other_mean)
         square = square + other_square + offset * offset * (0.5 * count)
         count = 2.0 * count
-    return (mean, lax.rsqrt(square / count + EPSILON), count)
-
-
-def row_totals(sums):
-    for bit in axis_bits("wid"):
-        sums = sums + swapped(sums, "wid", bit)
-    return sums
+    return (mean, lax.rsqrt(square / count + EPSILON))
 
 
 MESH = pl.DeviceIdType.MESH
@@ -505,64 +499,216 @@
     )(cotangent, normed, *weights)
 
 
-def scatter_sums(first, second, works):
-    size = lax.axis_size("hid")
+def scatter_kernel(
+    depth,
+    peers,
+    partial,
+    gain_ref,
+    unit_ref,
+    inverse_ref,
+    grad_out,
+    pair_send,
+    pair_recv,
+    up_send,
+    up_recv,
+    down_send,
+    down_recv,
+    sums,
+    pair_sems,
+    up_sems,
+    down_sems,
+    sum_sems,
+):
+    hid, wid = lax.axis_index("hid"), lax.axis_index("wid")
+    z, y = hid // 2, hid % 2
+    above, below, pair = hid + 2, hid - 2, z * 2 + 1 - y
+    barrier = pltpu.get_barrier_semaphore()
+    pl.semaphore_signal(barrier, inc=1, device_id={"hid": pair}, device_id_type=MESH)
+    for turn in range(1, peers):
+        pl.semaphore_signal(
+            barrier, inc=1, device_id={"wid": (wid + turn) % peers}, device_id_type=MESH
+        )
+
+    @pl.when(z < depth - 1)
+    def _():
+        pl.semaphore_signal(barrier, inc=1, device_id={"hid": above}, device_id_type=MESH)
+
+    @pl.when(z > 0)
+    def _():
+        pl.semaphore_signal(barrier, inc=1, device_id={"hid": below}, device_id_type=MESH)
+
+    pl.semaphore_wait(barrier, peers + jnp.where(z > 0, 1, 0) + jnp.where(z < depth - 1, 1, 0))
+
+    def block_copy(source, target, sems, level, device):
+        return pltpu.make_async_remote_copy(
+            src_ref=source.at[level],
+            dst_ref=target.at[level],
+            send_sem=sems.at[0, level],
+            recv_sem=sems.at[1, level],
+            device_id={"hid": device},
+            device_id_type=MESH,
+        )
+
+    def pair_copy(level):
+        return block_copy(pair_send, pair_recv, pair_sems, level, pair)
+
+    def up_copy(level):
+        return block_copy(up_send, up_recv, up_sems, level, above)
+
+    def down_copy(level):
+        return block_copy(down_send, down_recv, down_sems, level, below)
+
+    def give(level):
+        pair_send[level] = partial[level * 2 + 1 - y].astype(jnp.bfloat16)
+        pair_copy(level).start()
+
+    def joined(level):
+        pair_copy(level).wait_recv()
+        return partial[level * 2 + y] + pair_recv[level].astype(jnp.float32)
+
+    for far in range(depth - 1, 0, -1):
+
+        @pl.when(z + far <= depth - 1)
+        def _():
+            give(z + far)
+
+        @pl.when(z - far >= 0)
+        def _():
+            give(z - far)
+
+    give(z)
+
+    for far in range(depth - 1, 0, -1):
+
+        @pl.when(z + far <= depth - 1)
+        def _():
+            level = z + far
+            held = joined(level)
+
+            @pl.when(z > 0)
+            def _():
+                up_copy(level).wait_recv()
+                up_send[level] = (held + up_recv[level].astype(jnp.float32)).astype(jnp.bfloat16)
+
+            @pl.when(z == 0)
+            def _():
+                up_send[level] = held.astype(jnp.bfloat16)
+
+            up_copy(level).start()
+
+        @pl.when(z - far >= 0)
+        def _():
+            level = z - far
+            held = joined(level)
+
+            @pl.when(z < depth - 1)
+            def _():
+                down_copy(level).wait_recv()
+                down_send[level] = (held + down_recv[level].astype(jnp.float32)).astype(
+                    jnp.bfloat16
+                )
+
+            @pl.when(z == depth - 1)
+            def _():
+                down_send[level] = held.astype(jnp.bfloat16)
+
+            down_copy(level).start()
+
+    partial[hid] = joined(z)
+
+    @pl.when(z > 0)
+    def _():
+        up_copy(z).wait_recv()
+        partial[hid] = partial[hid] + up_recv[z].astype(jnp.float32)
+
+    @pl.when(z < depth - 1)
+    def _():
+        down_copy(z).wait_recv()
+        partial[hid] = partial[hid] + down_recv[z].astype(jnp.float32)
+
+    unit_grad = partial[hid] * gain_ref[...]
+    unit_rows = unit_ref[...]
+    rows, columns = unit_rows.shape
+    plain = jnp.sum(unit_grad, axis=-1, keepdims=True)
+    project = jnp.sum(unit_grad * unit_rows, axis=-1, keepdims=True)
+    lane = lax.broadcasted_iota(jnp.int32, (rows, 128), 1)
+    sums[wid] = jnp.where(lane < 64, plain, project)
+
+    def sum_copy(slot, turn):
+        return pltpu.make_async_remote_copy(
+            src_ref=sums.at[slot],
+            dst_ref=sums.at[slot],
+            send_sem=sum_sems.at[0, turn],
+            recv_sem=sum_sems.at[1, slot],
+            device_id={"wid": (wid + turn) % peers},
+            device_id_type=MESH,
+        )
+
+    for turn in range(1, peers):
+        sum_copy(wid, turn).start()
+    for turn in range(1, peers):
+        sum_copy((wid + turn) % peers, turn).wait_recv()
+    joint = sums[0]
+    for at in range(1, peers):
+        joint = joint + sums[at]
+    joint = joint * (1.0 / (columns * peers))
+    grad_out[...] = (
+        inverse_ref[...] * (unit_grad - joint[:, 0:1] - unit_rows * joint[:, 64:65])
+    ).astype(jnp.bfloat16)
+
+    for turn in range(1, peers):
+        sum_copy(wid, turn).wait_send()
+    for level in range(depth):
+        pair_copy(level).wait_send()
+
+        @pl.when(level > z)
+        def _():
+            up_copy(level).wait_send()
+
+        @pl.when(level < z)
+        def _():
+            down_copy(level).wait_send()
+
+
+def scatter_back(partial, norm_gain, unit_rows, inverse):
+    size, peers = lax.axis_size("hid"), lax.axis_size("wid")
     depth = size // 2
-    index = lax.axis_index("hid")
-    z, y = index // 2, index % 2
-    ways = (1, -1)
-
-    def split(partial):
-        return partial.reshape(depth, 2, partial.shape[0] // size, partial.shape[1])
-
-    def along(value, at, axis):
-        return lax.dynamic_index_in_dim(value, at, axis=axis, keepdims=False)
-
-    def shifted(flow, way):
-        pairs = [(at, at + 2 * way) for at in range(size) if 0 <= at + 2 * way < size]
-        return lax.ppermute(flow.astype(jnp.bfloat16), "hid", pairs)
-
-    def swap_of(blocks, axis):
-        return swapped(along(blocks, 1 - y, axis).astype(jnp.bfloat16), "hid", 1)
-
-    def chain_step(blocks, flows, far):
-        parts = [along(blocks, jnp.clip(z + way * far, 0, depth - 1), 0) for way in ways]
-        if flows is not None:
-            parts = [part + flow.astype(jnp.float32) for part, flow in zip(parts, flows)]
-        return [shifted(part, way) for part, way in zip(parts, ways)]
-
-    def chain_end(blocks, flows):
-        up, down = (flow.astype(jnp.float32) for flow in flows)
-        return along(blocks, z, 0) + up + down
-
-    first, second = split(first), split(second)
-    done = []
-    first_flows, second_flows = None, None
-    for turn in range(depth):
-        if turn == 0:
-            first_got = [swap_of(first, 1)]
-        else:
-            first_flows = first_got = chain_step(first, first_flows, depth - turn)
-        if turn < depth - 1:
-            second_flows = second_got = chain_step(second, second_flows, depth - 1 - turn)
-        else:
-            second = chain_end(second, second_flows)
-            second_got = [swap_of(second, 0)]
-        if turn < len(works):
-            first_got, second_got, work = lax.optimization_barrier(
-                (first_got, second_got, works[turn]())
-            )
-            done.append(work)
-        if turn == 0:
-            first = along(first, y, 1) + first_got[0].astype(jnp.float32)
-        else:
-            first_flows = first_got
-        if turn < depth - 1:
-            second_flows = second_got
-        else:
-            second = along(second, y, 0) + second_got[0].astype(jnp.float32)
-    first = chain_end(first, first_flows)
-    return (jnp.concatenate([first, second], axis=1), done)
+    rows, columns = unit_rows.shape
+    vmem = pl.BlockSpec(memory_space=pltpu.VMEM)
+
+    def body(partial_in, gain_ref, unit_ref, inverse_ref, grad_out, partial_held, *rest):
+        partial_held[...] = partial_in[...]
+        scatter_kernel(
+            depth, peers, partial_held, gain_ref, unit_ref, inverse_ref, grad_out, *rest
+        )
+
+    block = pltpu.VMEM((depth, rows, columns), jnp.bfloat16)
+    pairs = pltpu.SemaphoreType.DMA((2, depth))
+    return pl.pallas_call(
+        body,
+        out_shape=jax.ShapeDtypeStruct((rows, columns), jnp.bfloat16),
+        in_specs=[vmem] * 4,
+        out_specs=vmem,
+        scratch_shapes=[pltpu.VMEM((size, rows, columns), jnp.float32)]
+        + [block] * 6
+        + [pltpu.VMEM((peers, rows, 128), jnp.float32)]
+        + [pairs] * 3
+        + [pltpu.SemaphoreType.DMA((2, peers))],
+        compiler_params=pltpu.CompilerParams(
+            collective_id=1, has_side_effects=True, vmem_limit_bytes=24 * 1024 * 1024
+        ),
+        cost_estimate=pl.CostEstimate(
+            flops=16 * size * rows * columns,
+            bytes_accessed=4 * size * rows * columns,
+            transcendentals=0,
+        ),
+        name="scatter_back",
+    )(
+        partial.reshape(size, rows, columns),
+        norm_gain.reshape(1, columns),
+        unit_rows,
+        inverse,
+    )
 
 
 def both_halves(own, core):
@@ -585,7 +731,7 @@
 ):
     core = lax.axis_index("wid") % 2
     input_rows = inputs.astype(jnp.float32)
-    centre, inverse, total_count = row_moments(input_rows)
+    centre, inverse = row_moments(input_rows)
     inverse = inverse[:, None]
     unit_rows = (input_rows - centre[:, None]) * inverse
     normed = (unit_rows * norm_gain).astype(jnp.bfloat16)
@@ -605,34 +751,14 @@
     qkv_back = both_halves(qkv_back, core)
     attended = both_halves(attended, core)
 
-    def normed_part(span):
-        return product("tf,df->td", pre_grad, up_weight[span]) + product(
-            "tch,dch->td", qkv_back, qkv_weight[span]
-        )
-
-    middle = up_weight.shape[0] // 2
-    normed_grad, (up_grad, down_grad, qkv_grad, out_grad) = scatter_sums(
-        normed_part(slice(None, middle)),
-        normed_part(slice(middle, None)),
-        (
-            lambda: product("td,tf->df", normed_all, pre_grad).astype(jnp.bfloat16),
-            lambda: product("tf,td->fd", hidden, grad_all).astype(jnp.bfloat16),
-            lambda: product("td,tch->dch", normed_all, qkv_back).astype(jnp.bfloat16),
-            lambda: product("th,td->hd", attended, grad_all).astype(jnp.bfloat16),
-        ),
-    )
-    unit_grad = normed_grad * norm_gain
-    grad_total, grad_project = row_totals(
-        jnp.stack([jnp.sum(unit_grad, axis=-1), jnp.sum(unit_grad * unit_rows, axis=-1)])
-    )
-    input_grad = (
-        inverse
-        * (
-            unit_grad
-            - (grad_total / total_count)[:, None]
-            - unit_rows * (grad_project / total_count)[:, None]
-        )
-    ).astype(jnp.bfloat16)
+    normed_grad = product("tf,df->td", pre_grad, up_weight) + product(
+        "tch,dch->td", qkv_back, qkv_weight
+    )
+    up_grad = product("td,tf->df", normed_all, pre_grad).astype(jnp.bfloat16)
+    down_grad = product("tf,td->fd", hidden, grad_all).astype(jnp.bfloat16)
+    qkv_grad = product("td,tch->dch", normed_all, qkv_back).astype(jnp.bfloat16)
+    out_grad = product("th,td->hd", attended, grad_all).astype(jnp.bfloat16)
+    input_grad = scatter_back(normed_grad, norm_gain, unit_rows, inverse)
     return (input_grad, qkv_grad, out_grad, up_grad, down_grad)
 
 

time: 224 us -> 198 us (0.88)
  starting transfers between devices: 43 us -> 3.74 us
  Pallas kernels: 97.1 us -> 128 us
  waiting for transfers between devices: 20.7 us -> 0.15 us
  local copies, waits for them, and re-layouts: 6.74 us -> 14 us
  matrix products: 45.2 us -> 42.4 us
    ppermute x12 -> x0, starting transfers between devices: 37.1 us -> none  [shifted(): return lax.ppermute(flow.astype(jnp.bfloat16), 'hid', pairs)]
    pallas_call x0 -> x1, Pallas kernels: none -> 30.9 us  [scatter_back(): pl.pallas_call(body, out_shape=jax.ShapeDtypeStruct((rows, columns), jnp....]
    ppermute x12 -> x0, waiting for transfers between devices: 13.7 us -> none  [shifted(): return lax.ppermute(flow.astype(jnp.bfloat16), 'hid', pairs)]
    ppermute x8 -> x4, waiting for transfers between devices: 6.98 us -> 0.15 us  [swapped(): return lax.ppermute(value, axis, [(at, at ^ bit) for at in range(size)])]
    unnamed x36 -> x43, local copies, waits for them, and re-layouts: 1.02 us -> 4.25 us
    convert_element_type x6 -> x0, other arithmetic: 2.88 us -> none  [the longest x1 1.75 us: local(): normed = (unit_rows * norm_gain).astype(jnp.bfloat16)]
    dot_general x14 -> x12, matrix products: 43.8 us -> 41 us  [product(): jnp.einsum(form, left_arr, right_arr, preferred_element_type=jnp.float32)]
    ppermute x8 -> x4, starting transfers between devices: 5.85 us -> 3.74 us  [swapped(): return lax.ppermute(value, axis, [(at, at ^ bit) for at in range(size)])]
  transfers between devices with their start and end apart: 20 -> 4, of which waited for: 10 -> 1; matrix products, arithmetic and copies ran while one was open for 12% -> 14% of each run, Pallas kernels for 0% -> 0%
where the time goes in v4:
time: 198 us
  Pallas kernels  128 us (65%)
  matrix products  42.4 us (21%)
  local copies, waits for them, and re-layouts  14 us (7%)
  other arithmetic  8.41 us (4%)
  starting transfers between devices  3.74 us (2%)
    pallas_call x1, Pallas kernels, forward_products(): pl.pallas_call(functools.partial(forward_kernel, (depth, out_n, down_n, u...  96.9 us
    dot_general x12, matrix products, product(): jnp.einsum(form, left_arr, right_arr, preferred_element_type=jnp.float32)  41 us
    pallas_call x1, Pallas kernels, scatter_back(): pl.pallas_call(body, out_shape=jax.ShapeDtypeStruct((rows, columns), jnp....  30.9 us
    unnamed x43, local copies, waits for them, and re-layouts  4.25 us
  transfers between devices with their start and end apart: 4, of which 1 were waited for; matrix products, arithmetic and copies ran while one was open for 14% of the time, Pallas kernels for 0%

profile of v4, /device:TPU:0, one launch (start us, length us, event | category | flops | bytes accessed | tf_op | source)
XLA Modules:
  0.0 197.6 jit_solution(11865494921659106298)
XLA Ops:
  0.6 1.1 convert_reduce_fusion
  1.7 1.2 fusion.23
  3.4 0.7 broadcast_in_dim.2.gain_ref
  4.1 0.7 copy.134
  4.8 2.6 %collective-permute-start.1 = (f32[2,64]{1,0:T(2,128)S(1)}, f32[2,64]{1,0:T(2,128)S(1)}, u32[]{:S(2)}, u32[]{:S(2)}) collective-permute-start(f32[2,64]{1,0:T(2,128)S(1)} %pad_maximum_fusion.5), channel_id=1, source_target_pairs={{0,2},{1,3},{2,0},{3,1},{4,6},{5,7},{6,4},{7,5},{8,10},{9,11},{10,... | collective-permute-start | bytes 1544 | tf_op jit(solution)/shard_map/ppermute | solution.py:20
  7.4 0.7 copy.135
  8.1 0.7 copy.133
  9.5 1.7 fusion.24
  11.3 96.9 %forward_products.1 = (bf16[8,64,1536]{2,1,0:T(8,128)(2,1)}, bf16[8,64,1536]{2,1,0:T(8,128)(2,1)}, bf16[256,512]{1,0:T(8,128)(2,1)}, f32[3,256,512]{2,1,0:T(8,12...) custom-call(bf16[64,1536]{1,0:T(8,128)(2,1)} %cot_ref.1, bf16[64,1536]{1,0:T(8,128)(2,1)} %get-tuple-element.28.normed_ref, ...), custom_call_target="tpu_custom_call" | custom-call | flops 9663676416 | bytes 33554432 | tf_op jit(solution)/shard_map/forward_products/pallas_call | solution.py:463
  108.2 1.1 slice.17
  109.2 1.3 fusion.50
  112.7 0.6 multiply_convert_fusion.3
  114.2 0.6 copy-done.7
  115.0 0.6 multiply_convert_fusion.2
  115.7 1.4 fusion.19
  117.7 1.1 copy.151
  118.8 1.0 convolution_convert_fusion.4
  119.8 1.1 convolution_convert_fusion.5
  121.3 3.5 %fusion.48 = (f32[256,4]{0,1:T(4,128)}, f32[256,4]{0,1:T(4,128)}, f32[1,256,4,128]{1,3,2,0:T(8,128)}) fusion(f32[256,4]{0,1:T(4,128)} %copy-done.7, f32[1,256,4,128]{1,3,2,0:T(8,128)S(1)} %bitcast.140, f32[256,4]{0,1:T(4,128)S(1)} %broadcast_multiply_fusion.5, f32[128]{0:T(128)} %param.16, bf16[256,4,128]{0,2,1:T(8,128)(2,1)S(1)} %copy.124, ...), kind=kOutput, calls=%fused_computation.101 | convolution fusion | flops 69205248 | bytes 3424768 | tf_op jit(solution)/shard_map/ihpq,iqha->ipha/dot_general | solution.py:29
  124.8 2.7 %fusion.49 = (f32[256,4]{0,1:T(4,128)}, f32[256,4]{0,1:T(4,128)}, f32[1,256,4,128]{1,3,2,0:T(8,128)S(1)}) fusion(f32[256,4]{0,1:T(4,128)S(1)} %copy-done.5, f32[1,256,4,128]{1,3,2,0:T(8,128)S(1)} %bitcast.138, f32[256,4]{0,1:T(4,128)S(1)} %broadcast_multiply_fusion.4, f32[128]{0:T(128)S(1)} %copy-done.14, bf16[256,4,128]{0,2,1:T(8,128)(2,1)S(1)} %copy.126, ...), kind=kOutput, calls=%fused_computation.102 | convolution fusion | flops 69205248 | bytes 3424768 | tf_op jit(solution)/shard_map/ihpq,ipha->iqha/dot_general | solution.py:29
  127.5 1.1 copy.132
  128.8 0.7 broadcast_multiply_fusion.2
  129.5 1.2 multiply_convert_fusion.1
  131.7 8.7 %fusion.55 = f32[512,1536]{1,0:T(8,128)} fusion(bf16[512,2048]{1,0:T(8,128)(2,1)} %get-tuple-element.11, bf16[1536,2048]{1,0:T(8,128)(2,1)} %up_ref.1), kind=kOutput, calls=%fused_computation.104 | convolution fusion | flops 3221225472 | bytes 11534336 | tf_op jit(solution)/shard_map/tf,df->td/dot_general | solution.py:29
  140.4 5.6 %convolution_convert_fusion.1 = bf16[1536,2048]{1,0:T(8,128)(2,1)} fusion(bf16[512,1536]{1,0:T(8,128)(2,1)S(1)} %bitcast.153, bf16[512,2048]{1,0:T(8,128)(2,1)S(1)} %copy-done.19), kind=kOutput, calls=%fused_computation.2 | convolution fusion | flops 3224371200 | bytes 9961472 | tf_op jit(solution)/shard_map/td,tf->df/dot_general | solution.py:29
  146.0 5.4 %convolution_convert_fusion = bf16[2048,1536]{1,0:T(8,128)(2,1)} fusion(bf16[512,2048]{1,0:T(8,128)(2,1)S(1)} %copy-done.20, bf16[512,1536]{1,0:T(8,128)(2,1)S(1)} %bitcast.156), kind=kOutput, calls=%fused_computation.1 | convolution fusion | flops 3224371200 | bytes 9961472 | tf_op jit(solution)/shard_map/tf,td->fd/dot_general | solution.py:29
  151.7 3.5 %convolution_convert_fusion.3 = bf16[512,1536]{1,0:T(8,128)(2,1)} fusion(bf16[512,1536]{1,0:T(8,128)(2,1)} %bitcast.155, bf16[256,512]{0,1:T(8,128)(2,1)S(1)} %get-tuple-element.26, bf16[256,512]{0,1:T(8,128)(2,1)S(1)} %get-tuple-element.25), kind=kOutput, calls=%fused_computation.6 | convolution fusion | flops 807141376 | bytes 3670016 | tf_op jit(solution)/shard_map/th,td->hd/dot_general | solution.py:29
  155.4 1.8 copy-done.18
  157.1 4.5 %fusion.1 = f32[512,1536]{1,0:T(8,128)S(1)} fusion(f32[512,1536]{1,0:T(8,128)S(1)} %copy-done.18, bf16[1536,3,512]{2,0,1:T(8,128)(2,1)} %param.12, bf16[256,3,512]{2,0,1:T(8,128)(2,1)S(1)} %get-tuple-element.22, bf16[256,3,512]{2,0,1:T(8,128)(2,1)S(1)} %get-tuple-element.21), kind=kOutput, calls=%fused_computation.5 | convolution fusion | flops 2419851264 | bytes 12582912 | tf_op jit(solution)/shard_map/tch,dch->td/dot_general | solution.py:29
  161.7 30.9 %scatter_back.1 = bf16[64,1536]{1,0:T(8,128)(2,1)S(1)} custom-call(f32[8,64,1536]{2,1,0:T(8,128)S(1)} %bitcast.136, f32[1,1536]{1,0:T(1,128)S(1)} %broadcast_in_dim.2.gain_ref, f32[64,1536]{1,0:T(8,128)S(1)} %get-tuple-element.27.unit_ref, f32[64,1]{1,0:T(8,128)S(1)} %add_rsqrt_fusion.inverse_ref), custom_call_target="tpu_custom_call" | custom-call | flops 12582912 | bytes 3145728 | tf_op jit(solution)/shard_map/scatter_back/pallas_call | solution.py:687
  192.7 4.3 %convolution_convert_fusion.2 = bf16[1536,3,512]{2,0,1:T(8,128)(2,1)} fusion(bf16[512,1536,1]{1,0,2:T(8,128)(2,1)S(1)} %bitcast.154, bf16[256,3,512]{2,0,1:T(8,128)(2,1)S(1)} %get-tuple-element.22, bf16[256,3,512]{2,0,1:T(8,128)(2,1)S(1)} %get-tuple-element.21), kind=kOutput, calls=%fused_computation.3 | convolution fusion | flops 2421424128 | bytes 7864320 | tf_op jit(solution)/shard_map/td,tch->dch/dot_general | solution.py:29
  197.0 0.7 copy.154
  (87 shorter events, 7.0 us)
Async XLA Ops:
  2.9 1.9 collective-permute-start
  4.8 4.1 %collective-permute-start.1 = (f32[2,64]{1,0:T(2,128)S(1)}, f32[2,64]{1,0:T(2,128)S(1)}, u32[]{:S(2)}, u32[]{:S(2)}) collective-permute-start(f32[2,64]{1,0:T(2,128)S(1)} %pad_maximum_fusion.5), channel_id=1, source_target_pairs={{0,2},{1,3},{2,0},{3,1},{4,6},{5,7},{6,4},{7,5},{8,10},{9,11},{10,... | collective-permute-start | bytes 1544 | tf_op jit(solution)/shard_map/ppermute | solution.py:20
  8.9 0.6 copy-start.8
  110.9 1.8 copy-start.13
  111.7 3.3 %copy-start.12 = (f32[128]{0:T(128)S(1)}, f32[128]{0:T(128)}, u32[]{:S(2)}) copy-start(f32[128]{0:T(128)} %param.16) | copy-start | bytes 1540
  112.0 0.6 copy-start.4
  114.2 0.6 copy-start.7
  121.2 3.5 %copy-start.5 = (f32[256,4]{0,1:T(4,128)S(1)}, f32[256,4]{0,1:T(4,128)}, u32[]{:S(2)}) copy-start(f32[256,4]{0,1:T(4,128)} %copy-done.4) | copy-start | bytes 12292
  121.3 3.5 %copy-start.14 = (f32[128]{0:T(128)S(1)}, f32[128]{0:T(128)}, u32[]{:S(2)}) copy-start(f32[128]{0:T(128)} %param.17) | copy-start | bytes 1540
  127.5 3.4 %copy-start.10 = (f32[256,4]{0,1:T(4,128)S(1)}, f32[256,4]{0,1:T(4,128)}, u32[]{:S(2)}) copy-start(f32[256,4]{0,1:T(4,128)} %get-tuple-element.19) | copy-start | bytes 12292
  127.5 3.4 %copy-start.11 = (f32[256,4]{0,1:T(4,128)S(1)}, f32[256,4]{0,1:T(4,128)}, u32[]{:S(2)}) copy-start(f32[256,4]{0,1:T(4,128)} %get-tuple-element.20) | copy-start | bytes 12292
  127.5 3.4 %copy-start.6 = (f32[256,4]{0,1:T(4,128)S(1)}, f32[256,4]{0,1:T(4,128)}, u32[]{:S(2)}) copy-start(f32[256,4]{0,1:T(4,128)} %copy-done.4) | copy-start | bytes 12292
  128.6 23.0 %collective-permute-start.3 = (bf16[256,512]{0,1:T(8,128)(2,1)}, bf16[256,512]{0,1:T(8,128)(2,1)S(1)}, u32[]{:S(2)}, u32[]{:S(2)}) collective-permute-start(bf16[256,512]{0,1:T(8,128)(2,1)} %bitcast.150), channel_id=1, source_target_pairs={{0,1},{1,0},{2,3},{3,2},{4,5},{5,4},{6,7},{7,6},{8,9},{9,8},{10,11... | collective-permute-start | bytes 786440 | tf_op jit(solution)/shard_map/ppermute | solution.py:20
  131.2 24.0 %collective-permute-start.2 = (bf16[256,3,512]{2,0,1:T(8,128)(2,1)S(1)}, bf16[256,3,512]{2,0,1:T(8,128)(2,1)S(1)}, u32[]{:S(2)}, u32[]{:S(2)}) collective-permute-start(bf16[256,3,512]{2,0,1:T(8,128)(2,1)S(1)} %pad_maximum_fusion.3), channel_id=1, source_target_pairs={{0,1},{1,0},{2,3},{3,2},{4,5},{5,4},{6,7},{7,6},{8,9},{9,8},{10,11... | collective-permute-start | bytes 2359304 | tf_op jit(solution)/shard_map/ppermute | solution.py:20
  131.7 8.7 %copy-start.15 = (bf16[8,64,1536]{2,1,0:T(8,128)(2,1)S(1)}, bf16[8,64,1536]{2,1,0:T(8,128)(2,1)}, u32[]{:S(2)}) copy-start(bf16[8,64,1536]{2,1,0:T(8,128)(2,1)} %get-tuple-element.14) | copy-start | bytes 4718596
  131.7 8.7 %copy-start.19 = (bf16[512,2048]{1,0:T(8,128)(2,1)S(1)}, bf16[512,2048]{1,0:T(8,128)(2,1)}, u32[]{:S(2)}) copy-start(bf16[512,2048]{1,0:T(8,128)(2,1)} %get-tuple-element.11) | copy-start | bytes 6291460
  140.4 5.6 %copy-start.17 = (bf16[8,64,1536]{2,1,0:T(8,128)(2,1)S(1)}, bf16[8,64,1536]{2,1,0:T(8,128)(2,1)}, u32[]{:S(2)}) copy-start(bf16[8,64,1536]{2,1,0:T(8,128)(2,1)} %get-tuple-element.15) | copy-start | bytes 4718596
  140.4 5.6 %copy-start.20 = (bf16[512,2048]{1,0:T(8,128)(2,1)S(1)}, bf16[512,2048]{1,0:T(8,128)(2,1)}, u32[]{:S(2)}) copy-start(bf16[512,2048]{1,0:T(8,128)(2,1)} %get-tuple-element.16) | copy-start | bytes 6291460
  146.0 5.4 %copy-start.9 = (f32[2,64]{1,0:T(2,128)S(1)}, f32[2,64]{1,0:T(2,128)}, u32[]{:S(2)}) copy-start(f32[2,64]{1,0:T(2,128)} %copy-done.8) | copy-start | bytes 1540
  146.0 5.6 %copy-start.1 = (f32[64,1]{1,0:T(8,128)S(1)}, f32[64,1]{1,0:T(8,128)}, u32[]{:S(2)}) copy-start(f32[64,1]{1,0:T(8,128)} %copy.134) | copy-start | bytes 772
  146.0 5.6 %copy-start.2 = (f32[64,1]{1,0:T(8,128)S(1)}, f32[64,1]{1,0:T(8,128)}, u32[]{:S(2)}) copy-start(f32[64,1]{1,0:T(8,128)} %copy.135) | copy-start | bytes 772
  146.0 5.6 %copy-start.3 = (f32[64,1]{1,0:T(8,128)S(1)}, f32[64,1]{1,0:T(8,128)}, u32[]{:S(2)}) copy-start(f32[64,1]{1,0:T(8,128)} %copy.133) | copy-start | bytes 772
  146.0 5.6 %copy-start = (bf16[4,128,256]{2,1,0:T(8,128)(2,1)S(1)}, bf16[4,128,256]{2,1,0:T(8,128)(2,1)}, u32[]{:S(2)}) copy-start(bf16[4,128,256]{2,1,0:T(8,128)(2,1)} %convolution_convert_fusion.4) | copy-start | bytes 786436
  155.3 1.9 copy-start.18
  161.7 31.0 %copy-start.16 = (bf16[8,64,1536]{2,1,0:T(8,128)(2,1)S(1)}, bf16[8,64,1536]{2,1,0:T(8,128)(2,1)}, u32[]{:S(2)}) copy-start(bf16[8,64,1536]{2,1,0:T(8,128)(2,1)} %get-tuple-element.14) | copy-start | bytes 4718596

commit v5 on v4

--- a/solution.py
+++ b/solution.py
@@ -18,11 +18,6 @@
 def swapped(value, axis, bit):
     size = lax.axis_size(axis)
     return lax.ppermute(value, axis, [(at, at ^ bit) for at in range(size)])
-
-
-def axis_bits(axis):
-    size = lax.axis_size(axis)
-    return [1 << at for at in range(size.bit_length() - 1)]
 
 
 def product(form, left_arr, right_arr):
@@ -91,20 +86,6 @@
     return (attended, qkv_back)
 
 
-def row_moments(input_rows):
-    count = float(input_rows.shape[1])
-    mean = jnp.mean(input_rows, axis=-1)
-    deviation = input_rows - mean[:, None]
-    square = jnp.sum(deviation * deviation, axis=-1)
-    for bit in axis_bits("wid"):
-        other_mean, other_square = swapped(jnp.stack([mean, square]), "wid", bit)
-        offset = other_mean - mean
-        mean = 0.5 * (mean + other_mean)
-        square = square + other_square + offset * offset * (0.5 * count)
-        count = 2.0 * count
-    return (mean, lax.rsqrt(square / count + EPSILON))
-
-
 MESH = pl.DeviceIdType.MESH
 GELU_SLOPE = math.sqrt(2.0 / math.pi)
 GELU_CUBE = 0.044715
@@ -125,7 +106,8 @@
 def forward_kernel(
     sizes,
     cot_ref,
-    normed_ref,
+    inputs_ref,
+    gain_ref,
     out_ref,
     down_ref,
     qkv_ref,
@@ -136,6 +118,8 @@
     qkv_out,
     hidden_all,
     pre_all,
+    unit_out,
+    inverse_out,
     total,
     out_w,
     down_w,
@@ -156,6 +140,8 @@
     x_in_sem,
     hand_out_sem,
     hand_in_sem,
+    moments,
+    moment_sems,
 ):
     depth, out_n, down_n, up_n, width, stages = sizes
     hid, wid = lax.axis_index("hid"), lax.axis_index("wid")
@@ -178,13 +164,14 @@
 
     gathered = (cot_all, normed_all)
     cot_all[hid] = cot_ref[...]
-    normed_all[hid] = normed_ref[...]
+    peers = moments.shape[0]
 
     barrier = pltpu.get_barrier_semaphore()
     pl.semaphore_signal(barrier, inc=1, device_id={"hid": pair}, device_id_type=MESH)
-    pl.semaphore_signal(barrier, inc=1, device_id={"wid": core_peer}, device_id_type=MESH)
-    for peer in x_peers:
-        pl.semaphore_signal(barrier, inc=1, device_id={"wid": peer}, device_id_type=MESH)
+    for turn in range(1, peers):
+        pl.semaphore_signal(
+            barrier, inc=1, device_id={"wid": (wid + turn) % peers}, device_id_type=MESH
+        )
 
     @pl.when(z < depth - 1)
     def _():
@@ -194,7 +181,7 @@
     def _():
         pl.semaphore_signal(barrier, inc=1, device_id={"hid": below}, device_id_type=MESH)
 
-    neighbours = 2 + stages + jnp.where(z > 0, 1, 0) + jnp.where(z < depth - 1, 1, 0)
+    neighbours = peers + jnp.where(z > 0, 1, 0) + jnp.where(z < depth - 1, 1, 0)
     pl.semaphore_wait(barrier, neighbours)
 
     def block_copy(kind, level, side, sems, target):
@@ -352,7 +339,39 @@
         half = total.shape[1]
         return pl.ds(pl.multiple_of(image * half, half), half)
 
+    def moment_copy(slot, turn):
+        return pltpu.make_async_remote_copy(
+            src_ref=moments.at[slot],
+            dst_ref=moments.at[slot],
+            send_sem=moment_sems.at[0, turn],
+            recv_sem=moment_sems.at[1, slot],
+            device_id={"wid": (wid + turn) % peers},
+            device_id_type=MESH,
+        )
+
     begin(0)
+    values = inputs_ref[...].astype(jnp.float32)
+    rows, columns = values.shape
+    mean = jnp.mean(values, axis=-1, keepdims=True)
+    deviation = values - mean
+    square = jnp.sum(deviation * deviation, axis=-1, keepdims=True)
+    lane = lax.broadcasted_iota(jnp.int32, (rows, 128), 1)
+    moments[wid] = jnp.where(lane < 64, mean, square)
+    for turn in range(1, peers):
+        moment_copy(wid, turn).start()
+    for turn in range(1, peers):
+        moment_copy((wid + turn) % peers, turn).wait_recv()
+    shares = [moments[at] for at in range(peers)]
+    centre = sum(share[:, 0:1] for share in shares) * (1.0 / peers)
+    spread = sum(
+        share[:, 64:65] + columns * (share[:, 0:1] - centre) * (share[:, 0:1] - centre)
+        for share in shares
+    )
+    inverse = lax.rsqrt(spread * (1.0 / (columns * peers)) + EPSILON)
+    unit_rows = (values - centre) * inverse
+    unit_out[...] = unit_rows
+    inverse_out[...] = jnp.broadcast_to(inverse, (rows, 128))
+    normed_all[hid] = (unit_rows * gain_ref[...]).astype(jnp.bfloat16)
     begin(1)
     near = z // (depth // 2)
     far = 1 - near
@@ -427,6 +446,8 @@
         for stage in range(stages):
             x_copy(at, stage).wait_send()
 
+    for turn in range(1, peers):
+        moment_copy(wid, turn).wait_send()
     for kind in range(2):
         for level in range(depth):
             to_pair(kind, level).wait_send()
@@ -440,7 +461,9 @@
                 downward(kind, level).wait_send()
 
 
-def forward_products(cotangent, normed, out_weight, down_weight, qkv_weight, up_weight):
+def forward_products(
+    cotangent, inputs, norm_gain, out_weight, down_weight, qkv_weight, up_weight
+):
     blocks = lax.axis_size("hid")
     depth = blocks // 2
     rows, columns = cotangent.shape
@@ -469,9 +492,11 @@
             jax.ShapeDtypeStruct((3, half, width), jnp.float32),
             jax.ShapeDtypeStruct((2 * half, up_weight.shape[1]), jnp.bfloat16),
             jax.ShapeDtypeStruct((2 * half, up_weight.shape[1]), jnp.bfloat16),
+            jax.ShapeDtypeStruct((rows, columns), jnp.float32),
+            jax.ShapeDtypeStruct((rows, 128), jnp.float32),
         ),
-        in_specs=[vmem, vmem, hbm, hbm, hbm, hbm],
-        out_specs=(vmem,) * 6,
+        in_specs=[vmem, vmem, vmem, hbm, hbm, hbm, hbm],
+        out_specs=(vmem,) * 8,
         scratch_shapes=[pltpu.VMEM((count, half, width), jnp.float32)]
         + [pltpu.VMEM(weight.shape, weight.dtype) for weight in weights]
         + [slots] * 2
@@ -488,6 +513,8 @@
             pltpu.SemaphoreType.DMA((stages, count)),
             pltpu.SemaphoreType.DMA((2, up_n)),
             pltpu.SemaphoreType.DMA((2, up_n)),
+            pltpu.VMEM((2 << stages, rows, 128), jnp.float32),
+            pltpu.SemaphoreType.DMA((2, 2 << stages)),
         ],
         compiler_params=pltpu.CompilerParams(
             collective_id=0, has_side_effects=True, vmem_limit_bytes=56 * 1024 * 1024
@@ -496,7 +523,7 @@
             flops=2 * macs, bytes_accessed=32 * 1024 * 1024, transcendentals=0
         ),
         name="forward_products",
-    )(cotangent, normed, *weights)
+    )(cotangent, inputs, norm_gain.reshape(1, columns), *weights)
 
 
 def scatter_kernel(
@@ -653,7 +680,7 @@
         joint = joint + sums[at]
     joint = joint * (1.0 / (columns * peers))
     grad_out[...] = (
-        inverse_ref[...] * (unit_grad - joint[:, 0:1] - unit_rows * joint[:, 64:65])
+        inverse_ref[:, 0:1] * (unit_grad - joint[:, 0:1] - unit_rows * joint[:, 64:65])
     ).astype(jnp.bfloat16)
 
     for turn in range(1, peers):
@@ -730,14 +757,19 @@
     key_gain,
 ):
     core = lax.axis_index("wid") % 2
-    input_rows = inputs.astype(jnp.float32)
-    centre, inverse = row_moments(input_rows)
-    inverse = inverse[:, None]
-    unit_rows = (input_rows - centre[:, None]) * inverse
-    normed = (unit_rows * norm_gain).astype(jnp.bfloat16)
-    grad_all, normed_all, att_grad, qkv_rows, hidden, pre_grad = forward_products(
+    (
+        grad_all,
+        normed_all,
+        att_grad,
+        qkv_rows,
+        hidden,
+        pre_grad,
+        unit_rows,
+        inverse,
+    ) = forward_products(
         cotangent,
-        normed,
+        inputs,
+        norm_gain,
         out_weight,
         down_weight,
         jnp.transpose(qkv_weight, (1, 0, 2)),

time: 198 us -> 184 us (0.929)
  other arithmetic: 8.41 us -> 3.61 us
  local copies, waits for them, and re-layouts: 14 us -> 9.58 us
  starting transfers between devices: 3.74 us -> 0.56 us
  matrix products: 42.4 us -> 40 us
    ppermute x4 -> x2, starting transfers between devices: 3.74 us -> 0.56 us  [swapped(): return lax.ppermute(value, axis, [(at, at ^ bit) for at in range(size)])]
    dot_general x12, matrix products: 41 us -> 38.6 us  [product(): jnp.einsum(form, left_arr, right_arr, preferred_element_type=jnp.float32)]
    reduce_sum x2 -> x0, other arithmetic: 2.21 us -> none  [the longest x1 1.15 us: row_moments(): square = jnp.sum(deviation * deviation, axis=-1)]
    unnamed x43 -> x25, local copies, waits for them, and re-layouts: 4.25 us -> 2.48 us
  transfers between devices with their start and end apart: 4 -> 2, of which waited for: 1 -> 0; matrix products, arithmetic and copies ran while one was open for 14% -> 18% of each run, Pallas kernels for 0% -> 0%
where the time goes in v5:
time: 184 us; the launch traced here: 183 us
  Pallas kernels  129 us (70%)
  matrix products  40 us (22%)
  local copies, waits for them, and re-layouts  9.58 us (5%)
  other arithmetic  3.61 us (2%)
    pallas_call x1, Pallas kernels, forward_products(): pl.pallas_call(functools.partial(forward_kernel, (depth, out_n, down_n, u...  97.1 us
    dot_general x12, matrix products, product(): jnp.einsum(form, left_arr, right_arr, preferred_element_type=jnp.float32)  38.6 us
    pallas_call x1, Pallas kernels, scatter_back(): pl.pallas_call(body, out_shape=jax.ShapeDtypeStruct((rows, columns), jnp....  31.4 us
  transfers between devices with their start and end apart: 2, of which 0 were waited for; matrix products, arithmetic and copies ran while one was open for 18% of the time, Pallas kernels for 0%

profile of v5, /device:TPU:0, one launch (start us, length us, event | category | flops | bytes accessed | tf_op | source)
XLA Modules:
  0.0 183.3 jit_solution(4096512843111539551)
XLA Ops:
  0.6 1.3 reshape.248.gain_ref
  1.9 97.1 %forward_products.1 = (bf16[8,64,1536]{2,1,0:T(8,128)(2,1)}, bf16[8,64,1536]{2,1,0:T(8,128)(2,1)}, bf16[256,512]{1,0:T(8,128)(2,1)}, f32[3,256,512]{2,1,0:T(8,12...) custom-call(bf16[64,1536]{1,0:T(8,128)(2,1)} %cot_ref.1, ...), custom_call_target="tpu_custom_call" | custom-call | flops 9663676416 | bytes 33554432 | tf_op jit(solution)/shard_map/forward_products/pallas_call | solution.py:486
  99.1 1.1 slice.17
  100.2 1.3 fusion.36
  101.4 0.2 copy.118
  101.6 0.2 reshape_squeeze.13
  101.8 0.2 reshape_squeeze.12
  102.0 0.2 copy.117
  102.4 0.3 reduce_sum.92
  103.2 0.6 multiply_convert_fusion.3
  103.8 0.2 copy.100
  104.0 0.3 reduce_sum.90
  104.8 0.6 multiply_convert_fusion.2
  105.6 0.3 fusion.5
  106.0 1.0 convolution_convert_fusion.4
  107.2 1.4 fusion.19
  108.7 1.1 convolution_convert_fusion.5
  109.8 0.3 fusion.42
  110.1 2.0 %fusion.34 = (f32[256,4]{0,1:T(4,128)S(1)}, f32[256,4]{0,1:T(4,128)S(1)}, f32[1,256,4,128]{1,3,2,0:T(8,128)S(1)}) fusion(f32[256,4]{0,1:T(4,128)S(1)} %add_rsqrt_fusion.1, f32[1,256,4,128]{1,3,2,0:T(8,128)S(1)} %bitcast.76, f32[256,4]{0,1:T(4,128)S(1)} %broadcast_multiply_fusion.5, f32[128]{0:T(128)S(1)} %copy-done.4, bf16[256,4,128]{0,2,1:T(8,128)(2,1)S(1)} %copy.100, ...), kind=kOutput, calls=%fused_computation.66 | convolution fusion | flops 69205248 | bytes 3424768 | tf_op jit(solution)/shard_map/ihpq,iqha->ipha/dot_general | solution.py:24
  112.1 2.0 %fusion.35 = (f32[256,4]{0,1:T(4,128)S(1)}, f32[256,4]{0,1:T(4,128)S(1)}, f32[1,256,4,128]{1,3,2,0:T(8,128)S(1)}) fusion(f32[256,4]{0,1:T(4,128)S(1)} %add_rsqrt_fusion, f32[1,256,4,128]{1,3,2,0:T(8,128)S(1)} %bitcast.74, f32[256,4]{0,1:T(4,128)S(1)} %broadcast_multiply_fusion.4, f32[128]{0:T(128)S(1)} %copy-done.5, bf16[256,4,128]{0,2,1:T(8,128)(2,1)S(1)} %copy.102, ...), kind=kOutput, calls=%fused_computation.67 | convolution fusion | flops 69205248 | bytes 3424768 | tf_op jit(solution)/shard_map/ihpq,ipha->iqha/dot_general | solution.py:24
  114.2 1.1 copy.108
  115.9 0.4 collective-permute-start
  116.4 8.7 %fusion.41 = f32[512,1536]{1,0:T(8,128)} fusion(bf16[512,2048]{1,0:T(8,128)(2,1)} %get-tuple-element.13, bf16[1536,2048]{1,0:T(8,128)(2,1)} %up_ref.1), kind=kOutput, calls=%fused_computation.69 | convolution fusion | flops 3221225472 | bytes 11534336 | tf_op jit(solution)/shard_map/tf,df->td/dot_general | solution.py:24
  125.1 5.4 %convolution_convert_fusion.1 = bf16[1536,2048]{1,0:T(8,128)(2,1)} fusion(bf16[512,1536]{1,0:T(8,128)(2,1)S(1)} %bitcast.87, bf16[512,2048]{1,0:T(8,128)(2,1)S(1)} %copy-done.10), kind=kOutput, calls=%fused_computation.2 | convolution fusion | flops 3224371200 | bytes 9961472 | tf_op jit(solution)/shard_map/td,tf->df/dot_general | solution.py:24
  130.4 5.4 %convolution_convert_fusion = bf16[2048,1536]{1,0:T(8,128)(2,1)} fusion(bf16[512,2048]{1,0:T(8,128)(2,1)S(1)} %copy-done.11, bf16[512,1536]{1,0:T(8,128)(2,1)S(1)} %bitcast.90), kind=kOutput, calls=%fused_computation.1 | convolution fusion | flops 3224371200 | bytes 9961472 | tf_op jit(solution)/shard_map/tf,td->fd/dot_general | solution.py:24
  135.8 1.1 broadcast_select_fusion.3
  136.9 3.5 %convolution_convert_fusion.3 = bf16[512,1536]{1,0:T(8,128)(2,1)} fusion(bf16[512,1536]{1,0:T(8,128)(2,1)} %bitcast.89, bf16[256,512]{0,1:T(8,128)(2,1)S(1)} %get-tuple-element.30, bf16[256,512]{0,1:T(8,128)(2,1)S(1)} %get-tuple-element.29), kind=kOutput, calls=%fused_computation.6 | convolution fusion | flops 807141376 | bytes 3670016 | tf_op jit(solution)/shard_map/th,td->hd/dot_general | solution.py:24
  140.5 1.8 copy-done.9
  142.3 4.6 %fusion.1 = f32[512,1536]{1,0:T(8,128)S(1)} fusion(f32[512,1536]{1,0:T(8,128)S(1)} %copy-done.9, bf16[1536,3,512]{2,0,1:T(8,128)(2,1)} %param.12, bf16[256,3,512]{2,0,1:T(8,128)(2,1)S(1)} %get-tuple-element.26, bf16[256,3,512]{2,0,1:T(8,128)(2,1)S(1)} %get-tuple-element.25), kind=kOutput, calls=%fused_computation.5 | convolution fusion | flops 2419851264 | bytes 12582912 | tf_op jit(solution)/shard_map/tch,dch->td/dot_general | solution.py:24
  146.9 31.4 %scatter_back.1 = bf16[64,1536]{1,0:T(8,128)(2,1)S(1)} custom-call(f32[8,64,1536]{2,1,0:T(8,128)S(1)} %bitcast.72, f32[1,1536]{1,0:T(1,128)S(1)} %copy-done.2, f32[64,1536]{1,0:T(8,128)S(1)} %copy-done, f32[64,128]{1,0:T(8,128)S(1)} %copy-done.1), custom_call_target="tpu_custom_call" | custom-call | flops 12582912 | bytes 3145728 | tf_op jit(solution)/shard_map/scatter_back/pallas_call | solution.py:714
  178.4 4.3 %convolution_convert_fusion.2 = bf16[1536,3,512]{2,0,1:T(8,128)(2,1)} fusion(bf16[512,1536,1]{1,0,2:T(8,128)(2,1)S(1)} %bitcast.88, bf16[256,3,512]{2,0,1:T(8,128)(2,1)S(1)} %get-tuple-element.26, bf16[256,3,512]{2,0,1:T(8,128)(2,1)S(1)} %get-tuple-element.25), kind=kOutput, calls=%fused_computation.3 | convolution fusion | flops 2421424128 | bytes 7864320 | tf_op jit(solution)/shard_map/td,tch->dch/dot_general | solution.py:24
  182.7 0.7 copy.123
  (49 shorter events, 2.3 us)
Async XLA Ops:
  101.8 1.4 copy-start.5
  102.7 2.1 %copy-start.4 = (f32[128]{0:T(128)S(1)}, f32[128]{0:T(128)}, u32[]{:S(2)}) copy-start(f32[128]{0:T(128)} %param.16) | copy-start | bytes 1540
  107.0 1.6 copy-start.3
  107.0 28.8 %collective-permute-start.1 = (bf16[256,512]{0,1:T(8,128)(2,1)}, bf16[256,512]{0,1:T(8,128)(2,1)}, u32[]{:S(2)}, u32[]{:S(2)}) collective-permute-start(bf16[256,512]{0,1:T(8,128)(2,1)} %bitcast.19), channel_id=1, source_target_pairs={{0,1},{1,0},{2,3},{3,2},{4,5},{5,4},{6,7},{7,6},{8,9},{9,8},{10,11... | collective-permute-start | bytes 786440 | tf_op jit(solution)/shard_map/ppermute | solution.py:20
  115.9 24.5 %collective-permute-start = (bf16[256,3,512]{2,0,1:T(8,128)(2,1)S(1)}, bf16[256,3,512]{2,0,1:T(8,128)(2,1)S(1)}, u32[]{:S(2)}, u32[]{:S(2)}) collective-permute-start(bf16[256,3,512]{2,0,1:T(8,128)(2,1)S(1)} %pad_maximum_fusion.3), channel_id=1, source_target_pairs={{0,1},{1,0},{2,3},{3,2},{4,5},{5,4},{6,7},{7,6},{8,9},{9,8},{10,11... | collective-permute-start | bytes 2359304 | tf_op jit(solution)/shard_map/ppermute | solution.py:20
  116.4 8.7 %copy-start.6 = (bf16[8,64,1536]{2,1,0:T(8,128)(2,1)S(1)}, bf16[8,64,1536]{2,1,0:T(8,128)(2,1)}, u32[]{:S(2)}) copy-start(bf16[8,64,1536]{2,1,0:T(8,128)(2,1)} %get-tuple-element.18) | copy-start | bytes 4718596
  116.4 8.7 %copy-start.10 = (bf16[512,2048]{1,0:T(8,128)(2,1)S(1)}, bf16[512,2048]{1,0:T(8,128)(2,1)}, u32[]{:S(2)}) copy-start(bf16[512,2048]{1,0:T(8,128)(2,1)} %get-tuple-element.13) | copy-start | bytes 6291460
  125.1 5.4 %copy-start.8 = (bf16[8,64,1536]{2,1,0:T(8,128)(2,1)S(1)}, bf16[8,64,1536]{2,1,0:T(8,128)(2,1)}, u32[]{:S(2)}) copy-start(bf16[8,64,1536]{2,1,0:T(8,128)(2,1)} %get-tuple-element.19) | copy-start | bytes 4718596
  125.1 5.4 %copy-start.11 = (bf16[512,2048]{1,0:T(8,128)(2,1)S(1)}, bf16[512,2048]{1,0:T(8,128)(2,1)}, u32[]{:S(2)}) copy-start(bf16[512,2048]{1,0:T(8,128)(2,1)} %get-tuple-element.20) | copy-start | bytes 6291460
  140.4 1.9 %copy-start.9 = (f32[512,1536]{1,0:T(8,128)S(1)}, f32[512,1536]{1,0:T(8,128)}, u32[]{:S(2)}) copy-start(f32[512,1536]{1,0:T(8,128)} %fusion.41) | copy-start | bytes 9437188
  142.3 4.6 %copy-start = (f32[64,1536]{1,0:T(8,128)S(1)}, f32[64,1536]{1,0:T(8,128)}, u32[]{:S(2)}) copy-start(f32[64,1536]{1,0:T(8,128)} %get-tuple-element.16.unit_ref) | copy-start | bytes 1179652
  142.3 4.6 %copy-start.1 = (f32[64,128]{1,0:T(8,128)S(1)}, f32[64,128]{1,0:T(8,128)}, u32[]{:S(2)}) copy-start(f32[64,128]{1,0:T(8,128)} %get-tuple-element.17.inverse_ref) | copy-start | bytes 98308
  142.3 4.6 %copy-start.2 = (f32[1,1536]{1,0:T(1,128)S(1)}, f32[1,1536]{1,0:T(1,128)}, u32[]{:S(2)}) copy-start(f32[1,1536]{1,0:T(1,128)} %reshape.248.gain_ref) | copy-start | bytes 18436
  146.9 31.5 %copy-start.7 = (bf16[8,64,1536]{2,1,0:T(8,128)(2,1)S(1)}, bf16[8,64,1536]{2,1,0:T(8,128)(2,1)}, u32[]{:S(2)}) copy-start(bf16[8,64,1536]{2,1,0:T(8,128)(2,1)} %get-tuple-element.18) | copy-start | bytes 4718596
